TPU v7x, 256 devices: a whole 4x4x8 slice. The times are simulated.
256 devices in a mesh: row: 16 (over y_lo, x, core), col: 16 (over y_hi, z).
Axes of the slice: x: 4, y: 4 (y_hi: 2, y_lo: 2; y = y_hi * 2 + y_lo), z: 8, core: 2. Of those that a mesh axis runs over, the one named last changes fastest.
Arguments:
- tokens: bfloat16 [2048, 12288], P(('row', 'col')), may hold values from -32 to 32
- norm_gain: float32 [12288], replicated, may hold values from 0.1 to 1.9
- gate_weight: bfloat16 [12288, 12288], P('row', 'col'), may hold values from -0.0546875 to 0.0546875
- up_weight: bfloat16 [12288, 12288], P('row', 'col'), may hold values from -0.0546875 to 0.0546875
- down_weight: bfloat16 [12288, 12288], P('col', 'row'), may hold values from -0.109375 to 0.109375
Outputs:
- block_output: bfloat16 [2048, 12288], P(('row', 'col'))
All inputs are finite; a program needn't handle non-finite values.
Results may differ from a plain program's by a relative error of at most 0.005.
Values may be sent and summed in bfloat16 or wider, within the bound.
No kernel may reach another device: no remote copies, remote signals or barrier semaphores. Data moves between devices by JAX's collectives and lax.ppermute only.
A program may use at most 128 MiB of HBM per device.

v0:
```python
import jax
import jax.numpy as jnp
from jax import lax
from jax.sharding import PartitionSpec as P

epsilon = 1e-05


def product(left, right):
    return jnp.dot(left, right, preferred_element_type=jnp.float32)


def on_device(tokens, norm_gain, gate_weight, up_weight, down_weight):
    inputs = tokens.astype(jnp.float32)
    inverse_rms = lax.rsqrt(jnp.mean(inputs * inputs, axis=1, keepdims=True) + epsilon)
    normed = (inputs * inverse_rms * norm_gain).astype(jnp.bfloat16)
    spread = lax.all_to_all(normed, "row", split_axis=1, concat_axis=0, tiled=True)
    token_panel = lax.all_gather(spread, "col", axis=0, tiled=True)
    unit_count = gate_weight.shape[1]
    row_block = token_panel
    summed = lax.psum_scatter(
        jnp.concatenate((product(row_block, gate_weight), product(row_block, up_weight)), axis=1),
        "row",
        scatter_dimension=0,
        tiled=True,
    )
    hidden = (jax.nn.silu(summed[:, :unit_count]) * summed[:, unit_count:]).astype(jnp.bfloat16)
    full_hidden = lax.all_gather(hidden, "row", axis=0, tiled=True)
    row_block = full_hidden
    branch = lax.psum_scatter(
        product(row_block, down_weight), "col", scatter_dimension=0, tiled=True
    )
    returned = lax.all_to_all(branch, "row", split_axis=0, concat_axis=1, tiled=True)
    return (inputs + returned).astype(jnp.bfloat16)


def solution(mesh):
    return jax.shard_map(
        on_device,
        mesh=mesh,
        in_specs=(P(("row", "col"), None), P(), P("row", "col"), P("row", "col"), P("col", "row")),
        out_specs=P(("row", "col"), None),
        check_vma=False,
    )
```

profile of v0, /device:TPU:48, one launch (start us, length us, event | category | flops | bytes accessed | tf_op | source)
XLA Modules:
  0.0 511.0 jit_solution(15500942702139462095)
XLA Ops:
  6.5 0.0 copy-start
  6.5 0.0 all-gather.3.cloned.1.call-start
  6.5 1.2 fusion
  7.8 1.0 fusion.2
  8.8 12.1 %all_to_all.38 = bf16[8,16,768]{2,0,1:T(8,128)(2,1)} all-to-all(bf16[8,16,768]{2,0,1:T(8,128)(2,1)S(1)} %bitcast.16), channel_id=1, replica_groups=mesh['row'=16,'col'=16] {'row'}, dimensions={1} | all-to-all | bytes 393216 | tf_op jit(solution)/shard_map/all_to_all | solution.py:17
  21.0 0.0 all-gather.3.cloned.1.call-update
  21.0 0.0 copy-start.3
  21.0 0.0 reduce-scatter.3.cloned.1.call-start
  21.1 91.0 %all-gather.3.cloned.1.call-done = bf16[2048,768]{1,0:T(8,128)(2,1)} async-done(((bf16[128,768]{1,0:T(8,128)(2,1)}), bf16[2048,768]{1,0:T(8,128)(2,1)}) %all-gather.3.cloned.1.call-update) | async-done | bytes 3145744 | tf_op jit(solution)/shard_map/all_gather | solution.py:18
  112.0 0.0 copy-done
  112.0 0.0 copy-start.2
  112.0 6.6 %fusion.6 = f32[2048,768]{0,1:T(8,128)} fusion(bf16[2048,768]{1,0:T(8,128)(2,1)} %all-gather.3.cloned.1.call-done, bf16[768,768]{1,0:T(8,128)(2,1)S(1)} %copy-done), kind=kOutput, calls=%fused_computation.12 | convolution fusion | flops 2415919104 | bytes 10616832 | tf_op jit(solution)/shard_map/dot_general | solution.py:10
  118.6 0.0 copy-done.3
  118.6 0.0 copy-done.2
  118.6 4.6 fusion.5
  123.3 11.3 %pad_maximum_fusion = f32[2048,1536]{0,1:T(8,128)} fusion(f32[2048,768]{0,1:T(8,128)} %fusion.6, f32[2048,768]{0,1:T(8,128)} %fusion.5), kind=kLoop, calls=%fused_computation | loop fusion | flops 3145728 | bytes 25165824 | tf_op jit(solution)/shard_map/concatenate | solution.py:22
  134.6 0.0 copy-start.4
  134.6 0.0 reduce-scatter.3.cloned.1.call-update
  134.6 0.0 all-gather.5.cloned.1.call-start
  134.7 84.6 %reduce-scatter.3.cloned.1.call-done = f32[128,1536]{0,1:T(8,128)} async-done(((f32[2048,1536]{0,1:T(8,128)}), f32[128,1536]{0,1:T(8,128)}) %reduce-scatter.3.cloned.1.call-update) | async-done | bytes 786448 | tf_op jit(solution)/shard_map/reduce_scatter | solution.py:21
  219.3 1.9 fusion.4
  221.2 0.0 all-gather.5.cloned.1.call-update
  221.2 0.0 reduce-scatter.5.cloned.1.call-start
  221.3 42.6 %all-gather.5.cloned.1.call-done = bf16[2048,768]{0,1:T(8,128)(2,1)} async-done(((bf16[128,768]{0,1:T(8,128)(2,1)}), bf16[2048,768]{0,1:T(8,128)(2,1)}) %all-gather.5.cloned.1.call-update) | async-done | bytes 3145744 | tf_op jit(solution)/shard_map/all_gather | solution.py:28
  263.9 0.0 copy-done.4
  263.9 7.2 %fusion.7 = f32[2048,768]{1,0:T(8,128)} fusion(bf16[2048,768]{0,1:T(8,128)(2,1)} %all-gather.5.cloned.1.call-done, bf16[768,768]{1,0:T(8,128)(2,1)S(1)} %copy-done.4), kind=kOutput, calls=%fused_computation.13 | convolution fusion | flops 2415919104 | bytes 10616832 | tf_op jit(solution)/shard_map/dot_general | solution.py:10
  271.1 0.0 copy-start.1
  271.1 0.0 reduce-scatter.5.cloned.1.call-update
  271.2 217.5 %reduce-scatter.5.cloned.1.call-done = f32[128,768]{1,0:T(8,128)} async-done(((f32[2048,768]{1,0:T(8,128)}), f32[128,768]{1,0:T(8,128)}) %reduce-scatter.5.cloned.1.call-update) | async-done | bytes 393232 | tf_op jit(solution)/shard_map/reduce_scatter | solution.py:30
  488.6 15.1 %all_to_all.39 = f32[16,8,768]{2,1,0:T(8,128)S(1)} all-to-all(f32[16,8,768]{2,1,0:T(8,128)} %bitcast.17), channel_id=1, replica_groups=mesh['row'=16,'col'=16] {'row'}, dimensions={0} | all-to-all | bytes 786432 | tf_op jit(solution)/shard_map/all_to_all | solution.py:33
  503.7 0.0 copy-done.1
  503.7 0.7 fusion.3
  (1 shorter events, 0.0 us)
Async XLA Ops:
  6.5 105.5 %copy-start = (bf16[768,768]{1,0:T(8,128)(2,1)S(1)}, bf16[768,768]{1,0:T(8,128)(2,1)}, u32[]{:S(2)}) copy-start(bf16[768,768]{1,0:T(8,128)(2,1)} %param.8) | copy-start | bytes 3538948
  6.5 105.5 %all-gather.3.cloned.1.call-start = ((), (), s32[]{:S(2)}) async-start(), calls=%async_computation.4 | async-start | bytes 3342336 | tf_op jit(solution)/shard_map/all_gather | solution.py:18
  21.0 97.6 %copy-start.3 = (bf16[768,768]{1,0:T(8,128)(2,1)S(1)}, bf16[768,768]{1,0:T(8,128)(2,1)}, u32[]{:S(2)}) copy-start(bf16[768,768]{1,0:T(8,128)(2,1)} %param.7) | copy-start | bytes 3538948
  21.0 198.3 %reduce-scatter.3.cloned.1.call-start = ((), (), s32[]{:S(2)}) async-start(), calls=%async_computation.5 | async-start | bytes 13369344 | tf_op jit(solution)/shard_map/reduce_scatter | solution.py:21
  112.0 6.6 %copy-start.2 = (bf16[2048,768]{1,0:T(8,128)(2,1)S(1)}, bf16[2048,768]{1,0:T(8,128)(2,1)}, u32[]{:S(2)}) copy-start(bf16[2048,768]{1,0:T(8,128)(2,1)} %all-gather.3.cloned.1.call-done) | copy-start | bytes 9437188
  134.6 129.3 %copy-start.4 = (bf16[768,768]{1,0:T(8,128)(2,1)S(1)}, bf16[768,768]{1,0:T(8,128)(2,1)}, u32[]{:S(2)}) copy-start(bf16[768,768]{1,0:T(8,128)(2,1)} %param.9) | copy-start | bytes 3538948
  134.6 129.3 %all-gather.5.cloned.1.call-start = ((), (), s32[]{:S(2)}) async-start(), calls=%async_computation.6 | async-start | bytes 3342336 | tf_op jit(solution)/shard_map/all_gather | solution.py:28
  221.2 267.4 %reduce-scatter.5.cloned.1.call-start = ((), (), s32[]{:S(2)}) async-start(), calls=%async_computation.7 | async-start | bytes 6684672 | tf_op jit(solution)/shard_map/reduce_scatter | solution.py:30
  271.1 232.6 %copy-start.1 = (bf16[8,12288]{1,0:T(8,128)(2,1)S(1)}, bf16[8,12288]{1,0:T(8,128)(2,1)}, u32[]{:S(2)}) copy-start(bf16[8,12288]{1,0:T(8,128)(2,1)} %param.5) | copy-start | bytes 589828
Sparse Core Ops, SparseCore 0:
  21.1 90.8 all-gather.2
  134.8 84.5 reduce-scatter.2
  221.4 42.4 all-gather.4
  271.3 217.3 reduce-scatter.4
where the time goes:
time: 514 us; the launch traced here: 511 us
  waiting for transfers between devices  436 us (85%)
  blocking collectives  27.2 us (5%)
  matrix products  18.5 us (4%)
  other arithmetic  16.2 us (3%)
  between operations  13.1 us (3%)
    reduce_scatter x1, waiting for transfers between devices, on_device(): lax.psum_scatter(product(row_block, down_weight), 'col', scatter_dimensio...  217 us
    all_gather x1, waiting for transfers between devices, on_device(): token_panel = lax.all_gather(spread, 'col', axis=0, tiled=True)  91 us
    reduce_scatter x1, waiting for transfers between devices, on_device(): lax.psum_scatter(jnp.concatenate((product(row_block, gate_weight), produc...  84.6 us
    all_gather x1, waiting for transfers between devices, on_device(): full_hidden = lax.all_gather(hidden, 'row', axis=0, tiled=True)  42.6 us
    dot_general x3, matrix products, product(): return jnp.dot(left, right, preferred_element_type=jnp.float32)  18.5 us
    all_to_all x1, blocking collectives, on_device(): lax.all_to_all(branch, 'row', split_axis=0, concat_axis=1, tiled=True)  15.1 us
    all_to_all x1, blocking collectives, on_device(): lax.all_to_all(normed, 'row', split_axis=1, concat_axis=0, tiled=True)  12.1 us
    concatenate x1, other arithmetic, on_device(): jnp.concatenate((product(row_block, gate_weight), product(row_block, up_w...  11.3 us
  transfers between devices with their start and end apart: 4, of which 4 were waited for; matrix products, arithmetic and copies ran while one was open for 0% of the time, Pallas kernels for 0%

commit v1 on v0

v1 whole, which is shorter than its diff:
```python
import jax
import jax.numpy as jnp
from jax import lax
from jax.sharding import Mesh, PartitionSpec as P

epsilon = 1e-05
f32, bf16 = jnp.float32, jnp.bfloat16
axes = ("yl", "x", "c", "yh", "z")


def product(left, right):
    return jnp.dot(left, right, preferred_element_type=f32)


def shift(block, steps):
    return lax.ppermute(block, "z", [(i, (i + steps) % 8) for i in range(8)])


def core_partner(block):
    return lax.ppermute(block, "c", [(0, 1), (1, 0)])


def y_partner(block, flip):
    return lax.ppermute(block, ("yl", "yh"), [(i, i ^ flip) for i in range(4)])


def swap_where(flag, array, axis):
    return jnp.where(flag, jnp.flip(array, axis), array)


def on_device(tokens, norm_gain, gate_weight, up_weight, down_weight):
    yl, core, yh, z = (lax.axis_index(name) for name in ("yl", "c", "yh", "z"))
    unit = gate_weight.shape[1]

    first = jnp.concatenate((gate_weight, up_weight), axis=1)
    first = jnp.concatenate((first, core_partner(first)), axis=0)
    second = jnp.concatenate(
        (
            jnp.concatenate((down_weight, y_partner(down_weight, 2)), axis=1),
            jnp.concatenate((y_partner(down_weight, 1), y_partner(down_weight, 3)), axis=1),
        ),
        axis=0,
    )
    second = jnp.concatenate((second, core_partner(second)), axis=1)

    inputs = tokens.astype(f32)
    inverse_rms = lax.rsqrt(jnp.mean(inputs * inputs, axis=1, keepdims=True) + epsilon)
    normed = (inputs * inverse_rms * norm_gain).astype(bf16)

    pieces = swap_where(core == 1, normed.reshape(8, 8, 2, unit), 2).reshape(8, 8, 2 * unit)
    pieces = jnp.broadcast_to(pieces.transpose(1, 0, 2)[:, None], (8, 2, 8, 2 * unit))
    block = lax.all_to_all(pieces.reshape(16, 8, 2 * unit), ("yl", "x", "yh"), 0, 0)
    block = block.reshape(128, 2 * unit)

    r1, l1 = shift(block, 1), shift(block, -1)
    r2, l2 = shift(r1, 1), shift(l1, -1)
    r3, l3 = shift(r2, 1), shift(l2, -1)
    opposite = jnp.concatenate((shift(r2[:64], 2), shift(l2[64:], -2)), axis=0)
    panel = jnp.stack(
        [piece.reshape(8, 16, 2 * unit) for piece in (block, r1, r2, r3, opposite, l3, l2, l1)],
        axis=1,
    )
    partial = product(panel.reshape(1024, 2 * unit), first).astype(bf16)
    terms = lax.all_to_all(partial.reshape(8, 128, 2 * unit), ("yl", "x"), 0, 0)
    summed = jnp.sum(terms.astype(f32), axis=0)
    hidden = (jax.nn.silu(summed[:, :unit]) * summed[:, unit:]).astype(bf16)

    hidden = jnp.flip(hidden.reshape(8, 2, 8, unit), 0)
    hidden = lax.dynamic_slice_in_dim(jnp.concatenate((hidden, hidden), axis=0), 7 - z, 8, axis=0)
    hidden = hidden.transpose(1, 0, 2, 3)[None]
    hidden = jnp.broadcast_to(hidden, (4, 2, 8, 8, unit)).reshape(8, 8, 8, unit)
    hidden = lax.all_to_all(hidden, ("x", "yh"), 0, 0).reshape(4, 2, 8, 8, unit)
    hidden = swap_where(yh == 1, hidden, 1)
    hidden = hidden.transpose(2, 0, 3, 1, 4).reshape(256, 2 * unit)

    branch = product(hidden, second).astype(bf16)
    terms = lax.all_to_all(branch.reshape(8, 32, 4 * unit), "z", 0, 0)
    branch = jnp.sum(terms.astype(f32), axis=0).astype(bf16)
    branch = lax.all_to_all(branch.reshape(4, 8, 4 * unit), "x", 0, 0)
    branch = branch.reshape(4, 8, 2, 2, unit)
    branch = swap_where(core == 1, swap_where(yl == 1, branch, 3), 2)
    branch = branch.transpose(1, 3, 0, 2, 4).reshape(8, 16 * unit)
    return (inputs + branch.astype(f32)).astype(bf16)


def solution(mesh):
    grid = Mesh(mesh.devices.reshape(2, 4, 2, 2, 8), axes)
    row, col = ("yl", "x", "c"), ("yh", "z")
    return jax.shard_map(
        on_device,
        mesh=grid,
        in_specs=(P(axes, None), P(), P(row, col), P(row, col), P(col, row)),
        out_specs=P(axes, None),
        check_vma=False,
    )
```

time: 514 us -> 241 us (0.47)
  waiting for transfers between devices: 436 us -> 91.7 us
  starting transfers between devices: 0.13 us -> 53.4 us
  blocking collectives: 27.2 us -> 46.4 us
  between operations: 13.1 us -> 0.36 us
  local copies, waits for them, and re-layouts: 0.02 us -> 7.51 us
    reduce_scatter x2 -> x0, waiting for transfers between devices: 302 us -> none  [the longest x1 217 us: on_device(): lax.psum_scatter(product(row_block, down_weight), 'col', scatter_dimensio...]
    all_gather x2 -> x0, waiting for transfers between devices: 134 us -> none  [the longest x1 91 us: on_device(): token_panel = lax.all_gather(spread, 'col', axis=0, tiled=True)]
    all_to_all x0 -> x4, waiting for transfers between devices: none -> 58.7 us  [the longest x1 38.8 us: on_device(): terms = lax.all_to_all(partial.reshape(8, 128, 2 * unit), ('yl', 'x'), 0, 0)]
    ppermute x0 -> x13, waiting for transfers between devices: none -> 33 us  [the longest x3 19 us: y_partner(): return lax.ppermute(block, ('yl', 'yh'), [(i, i ^ flip) for i in range(4)])]
    all_to_all x0 -> x4, starting transfers between devices: none -> 32.1 us  [the longest x1 16.1 us: on_device(): hidden = lax.all_to_all(hidden, ('x', 'yh'), 0, 0).reshape(4, 2, 8, 8, unit)]
    ppermute x0 -> x13, starting transfers between devices: none -> 21.3 us  [the longest x8 16.4 us: shift(): return lax.ppermute(block, 'z', [(i, (i + steps) % 8) for i in range(8)])]
    all_to_all x2 -> x1, blocking collectives: 27.2 us -> 46.4 us  [on_device(): terms = lax.all_to_all(branch.reshape(8, 32, 4 * unit), 'z', 0, 0)]
    dot_general x3 -> x2, matrix products: 18.5 us -> 22.9 us  [product(): return jnp.dot(left, right, preferred_element_type=f32)]
  transfers between devices with their start and end apart: 4 -> 17, of which waited for: 4 -> 8; matrix products, arithmetic and copies ran while one was open for 0% -> 9% of each run, Pallas kernels for 0% -> 0%
where the time goes in v1:
time: 241 us; the launch traced here: 239 us
  waiting for transfers between devices  91.7 us (38%)
  starting transfers between devices  53.4 us (22%)
  blocking collectives  46.4 us (19%)
  matrix products  22.9 us (10%)
  other arithmetic  16.5 us (7%)
  local copies, waits for them, and re-layouts  7.51 us (3%)
    all_to_all x1, blocking collectives, on_device(): terms = lax.all_to_all(branch.reshape(8, 32, 4 * unit), 'z', 0, 0)  46.4 us
    all_to_all x1, waiting for transfers between devices, on_device(): terms = lax.all_to_all(partial.reshape(8, 128, 2 * unit), ('yl', 'x'), 0, 0)  38.8 us
    dot_general x2, matrix products, product(): return jnp.dot(left, right, preferred_element_type=f32)  22.9 us
    ppermute x3, waiting for transfers between devices, y_partner(): return lax.ppermute(block, ('yl', 'yh'), [(i, i ^ flip) for i in range(4)])  19 us
    ppermute x8, starting transfers between devices, shift(): return lax.ppermute(block, 'z', [(i, (i + steps) % 8) for i in range(8)])  16.4 us
    all_to_all x1, starting transfers between devices, on_device(): hidden = lax.all_to_all(hidden, ('x', 'yh'), 0, 0).reshape(4, 2, 8, 8, unit)  16.1 us
    ppermute x8, waiting for transfers between devices, shift(): return lax.ppermute(block, 'z', [(i, (i + steps) % 8) for i in range(8)])  14 us
    concatenate x1, other arithmetic, on_device(): jnp.concatenate((jnp.concatenate((down_weight, y_partner(down_weight, 2))...  11.2 us
  transfers between devices with their start and end apart: 17, of which 8 were waited for; matrix products, arithmetic and copies ran while one was open for 9% of the time, Pallas kernels for 0%

profile of v1, /device:TPU:48, one launch (start us, length us, event | category | flops | bytes accessed | tf_op | source)
XLA Modules:
  0.0 238.7 jit_solution(11321416935745955885)
XLA Ops:
  0.0 1.2 fusion.21
  1.2 1.0 fusion.23
  2.3 0.2 copy.11
  2.5 1.1 rev.20
  3.6 0.2 broadcast_select_fusion
  3.8 0.1 reshape.54
  4.0 0.8 broadcast_in_dim.4
  4.8 7.3 %all-to-all-start = ((bf16[16,8,1536]{2,1,0:T(8,128)(2,1)}), bf16[16,8,1536]{2,1,0:T(8,128)(2,1)S(1)}, u32[]{:S(2)}, u32[]{:S(2)}) async-start(bf16[16,8,1536]{2,1,0:T(8,128)(2,1)} %bitcast.2), calls=%async_computation | async-start | bytes 786432 | tf_op jit(solution)/shard_map/all_to_all | solution.py:52
  12.1 0.2 collective-permute-start.10
  12.3 2.5 %collective-permute-start.11 = (bf16[768,768]{1,0:T(8,128)(2,1)S(1)}, bf16[768,768]{1,0:T(8,128)(2,1)}, u32[]{:S(2)}, u32[]{:S(2)}) collective-permute-start(bf16[768,768]{1,0:T(8,128)(2,1)S(1)} %copy-done.1), channel_id=1, source_target_pairs={{0,136},{8,128},{128,8},{136,0},{1,137},{9,129},{129,9},{137,1},{2... | collective-permute-start | bytes 3538952 | tf_op jit(solution)/shard_map/ppermute | solution.py:24
  14.8 2.1 collective-permute-start.9
  16.9 2.8 %all-to-all-done = bf16[16,8,1536]{2,1,0:T(8,128)(2,1)S(1)} async-done(((bf16[16,8,1536]{2,1,0:T(8,128)(2,1)}), bf16[16,8,1536]{2,1,0:T(8,128)(2,1)S(1)}, u32[]{:S(2)}, u32[]{:S(2)}) %all-to-all-start) | async-done | bytes 393248 | tf_op jit(solution)/shard_map/all_to_all | solution.py:52
  19.6 1.9 collective-permute-start
  21.6 0.1 collective-permute-start.4
  21.7 1.4 constant_dynamic-update-slice_fusion.9
  23.1 6.2 %collective-permute-done = bf16[128,1536]{1,0:T(8,128)(2,1)S(1)} collective-permute-done((bf16[128,1536]{1,0:T(8,128)(2,1)S(1)}, bf16[128,1536]{1,0:T(8,128)(2,1)S(1)}, u32[]{:S(2)}, u32[]{:S(2)}) %collective-permute-start) | collective-permute-done | bytes 393248 | tf_op jit(solution)/shard_map/ppermute | solution.py:16
  29.4 1.9 collective-permute-start.1
  31.3 2.3 collective-permute-start.5
  33.7 7.3 %collective-permute-done.1 = bf16[128,1536]{1,0:T(8,128)(2,1)S(1)} collective-permute-done((bf16[128,1536]{1,0:T(8,128)(2,1)S(1)}, bf16[128,1536]{1,0:T(8,128)(2,1)S(1)}, u32[]{:S(2)}, u32[]{:S(2)}) %collective-permute-start.1) | collective-permute-done | bytes 393248 | tf_op jit(solution)/shard_map/ppermute | solution.py:16
  40.9 0.5 collective-permute-done.5
  41.4 5.2 %collective-permute-start.3 = (bf16[64,1536]{1,0:T(8,128)(2,1)S(1)}, bf16[64,1536]{1,0:T(8,128)(2,1)S(1)}, u32[]{:S(2)}, u32[]{:S(2)}) collective-permute-start(bf16[64,1536]{1,0:T(8,128)(2,1)S(1)} %slice.16), channel_id=1, source_target_pairs={{0,2},{1,3},{2,4},{3,5},{4,6},{5,7},{6,0},{7,1},{8,10},{9,11},{10,... | collective-permute-start | bytes 589832 | tf_op jit(solution)/shard_map/ppermute | solution.py:16
  46.8 2.9 %collective-permute-start.6 = (bf16[64,1536]{1,0:T(8,128)(2,1)S(1)}, bf16[64,1536]{1,0:T(8,128)(2,1)S(1)}, u32[]{:S(2)}, u32[]{:S(2)}) collective-permute-start(bf16[64,1536]{1,0:T(8,128)(2,1)S(1)} %slice.17), channel_id=1, source_target_pairs={{0,6},{1,7},{2,0},{3,1},{4,2},{5,3},{6,4},{7,5},{8,14},{9,15},{10,... | collective-permute-start | bytes 589832 | tf_op jit(solution)/shard_map/ppermute | solution.py:16
  49.6 18.9 %collective-permute-done.11 = bf16[768,768]{1,0:T(8,128)(2,1)} collective-permute-done((bf16[768,768]{1,0:T(8,128)(2,1)S(1)}, bf16[768,768]{1,0:T(8,128)(2,1)}, u32[]{:S(2)}, u32[]{:S(2)}) %collective-permute-start.11) | collective-permute-done | bytes 1179680 | tf_op jit(solution)/shard_map/ppermute | solution.py:24
  68.6 1.9 collective-permute-start.2
  70.5 0.1 collective-permute-start.7
  70.6 11.2 %maximum_maximum_fusion = bf16[1536,1536]{1,0:T(8,128)(2,1)} fusion(bf16[768,768]{1,0:T(8,128)(2,1)} %collective-permute-done.11, bf16[768,768]{1,0:T(8,128)(2,1)S(1)} %collective-permute-done.10, bf16[768,768]{1,0:T(8,128)(2,1)} %collective-permute-done.9, bf16[768,768]{1,0:T(8,128)(2,1)S(1)} %copy-done.1), kind=kLoop, calls=%fused_computation.15 | loop fusion | flops 18874368 | bytes 9437184 | tf_op jit(solution)/shard_map/concatenate | solution.py:37
  82.2 6.4 %fusion.17 = bf16[1024,1536]{1,0:T(8,128)(2,1)} fusion(bf16[1024,1536]{1,0:T(8,128)(2,1)S(1)} %bitcast.49, bf16[768,1536]{1,0:T(8,128)(2,1)S(1)} %collective-permute-done.8, bf16[768,1536]{1,0:T(8,128)(2,1)S(1)} %constant_dynamic-update-slice_fusion.8), kind=kOutput, calls=%fused_computation.17 | convolution fusion | flops 4842848256 | bytes 11010048 | tf_op jit(solution)/shard_map/dot_general | solution.py:12
  88.6 5.1 %all-to-all-start.1 = ((bf16[8,128,1536]{2,1,0:T(8,128)(2,1)}), bf16[8,128,1536]{2,1,0:T(8,128)(2,1)S(1)}, u32[]{:S(2)}, u32[]{:S(2)}) async-start(bf16[8,128,1536]{2,1,0:T(8,128)(2,1)} %bitcast.30), calls=%async_computation.1 | async-start | bytes 6291456 | tf_op jit(solution)/shard_map/all_to_all | solution.py:64
  93.7 38.8 %all-to-all-done.1 = bf16[8,128,1536]{2,1,0:T(8,128)(2,1)S(1)} async-done(((bf16[8,128,1536]{2,1,0:T(8,128)(2,1)}), bf16[8,128,1536]{2,1,0:T(8,128)(2,1)S(1)}, u32[]{:S(2)}, u32[]{:S(2)}) %all-to-all-start.1) | async-done | bytes 3145760 | tf_op jit(solution)/shard_map/all_to_all | solution.py:64
  132.5 0.4 convert_reduce_fusion
  132.9 0.1 fusion.25
  133.2 0.9 broadcast_in_dim.5
  134.1 16.1 %all-to-all-start.2 = ((bf16[8,8,8,768]{3,2,1,0:T(8,128)(2,1)}), bf16[8,8,8,768]{3,2,1,0:T(8,128)(2,1)S(1)}, u32[]{:S(2)}, u32[]{:S(2)}) async-start(bf16[8,8,8,768]{3,2,1,0:T(8,128)(2,1)} %bitcast.16), calls=%async_computation.2 | async-start | bytes 1572864 | tf_op jit(solution)/shard_map/all_to_all | solution.py:72
  150.2 10.8 %all-to-all-done.2 = bf16[8,8,8,768]{3,2,1,0:T(8,128)(2,1)S(1)} async-done(((bf16[8,8,8,768]{3,2,1,0:T(8,128)(2,1)}), bf16[8,8,8,768]{3,2,1,0:T(8,128)(2,1)S(1)}, u32[]{:S(2)}, u32[]{:S(2)}) %all-to-all-start.2) | async-done | bytes 786464 | tf_op jit(solution)/shard_map/all_to_all | solution.py:72
  161.0 0.1 fusion.20
  161.2 0.8 copy.15
  162.1 16.4 %fusion.14 = bf16[256,3072]{1,0:T(8,128)(2,1)S(1)} fusion(bf16[256,1536]{1,0:T(8,128)(2,1)S(1)} %bitcast.42, bf16[1536,1536]{1,0:T(8,128)(2,1)} %collective-permute-done.12, bf16[768,768]{1,0:T(8,128)(2,1)} %collective-permute-done.11, bf16[768,768]{1,0:T(8,128)(2,1)S(1)} %copy-done.4, bf16[768,768]{1,0:T(8,128)(2,1)} %collective-permute-done.9, ...), kind=kOutput, calls=%fused_computation.16 | convolution fusion | flops 2463891456 | bytes 11796480 | tf_op jit(solution)/shard_map/dot_general | solution.py:12
  178.5 46.4 %all_to_all.25 = bf16[8,32,3072]{2,1,0:T(8,128)(2,1)S(1)} all-to-all(bf16[8,32,3072]{2,1,0:T(8,128)(2,1)S(1)} %bitcast.35), channel_id=1, replica_groups=mesh['yl'=2,'x'=4,'c'=2,'yh'=2,'z'=8] {'z'}, dimensions={0} | all-to-all | bytes 3145728 | tf_op jit(solution)/shard_map/all_to_all | solution.py:77
  224.9 0.9 reduce_sum.32
  225.8 3.6 %all-to-all-start.4 = ((bf16[4,8,3072]{2,1,0:T(8,128)(2,1)}), bf16[4,8,3072]{2,1,0:T(8,128)(2,1)S(1)}, u32[]{:S(2)}, u32[]{:S(2)}) async-start(bf16[4,8,3072]{2,1,0:T(8,128)(2,1)} %bitcast.20), calls=%async_computation.4 | async-start | bytes 393216 | tf_op jit(solution)/shard_map/all_to_all | solution.py:79
  229.5 6.3 %all-to-all-done.4 = bf16[4,8,3072]{2,1,0:T(8,128)(2,1)S(1)} async-done(((bf16[4,8,3072]{2,1,0:T(8,128)(2,1)}), bf16[4,8,3072]{2,1,0:T(8,128)(2,1)S(1)}, u32[]{:S(2)}, u32[]{:S(2)}) %all-to-all-start.4) | async-done | bytes 196640 | tf_op jit(solution)/shard_map/all_to_all | solution.py:79
  235.8 0.1 reshape.65
  235.9 1.1 rev.23
  237.0 0.2 broadcast_select_fusion.1
  237.2 0.2 convert_bitcast_fusion
  237.4 0.2 copy.16
  237.6 0.3 reshape.66
  237.9 0.7 fusion.24
  (41 shorter events, 0.8 us)
Async XLA Ops:
  0.0 12.1 %copy-start.1 = (bf16[768,768]{1,0:T(8,128)(2,1)S(1)}, bf16[768,768]{1,0:T(8,128)(2,1)}, u32[]{:S(2)}) copy-start(bf16[768,768]{1,0:T(8,128)(2,1)} %param.9) | copy-start | bytes 3538948
  4.8 14.9 %all-to-all-start = ((bf16[16,8,1536]{2,1,0:T(8,128)(2,1)}), bf16[16,8,1536]{2,1,0:T(8,128)(2,1)S(1)}, u32[]{:S(2)}, u32[]{:S(2)}) async-start(bf16[16,8,1536]{2,1,0:T(8,128)(2,1)} %bitcast.2), calls=%async_computation | async-start | bytes 786432 | tf_op jit(solution)/shard_map/all_to_all | solution.py:52
  12.1 34.7 %collective-permute-start.10 = (bf16[768,768]{1,0:T(8,128)(2,1)S(1)}, bf16[768,768]{1,0:T(8,128)(2,1)S(1)}, u32[]{:S(2)}, u32[]{:S(2)}) collective-permute-start(bf16[768,768]{1,0:T(8,128)(2,1)S(1)} %copy-done.1), channel_id=1, source_target_pairs={{0,8},{8,0},{128,136},{136,128},{1,9},{9,1},{129,137},{137,129},{2... | collective-permute-start | bytes 3538952 | tf_op jit(solution)/shard_map/ppermute | solution.py:24
  12.3 56.3 %collective-permute-start.11 = (bf16[768,768]{1,0:T(8,128)(2,1)S(1)}, bf16[768,768]{1,0:T(8,128)(2,1)}, u32[]{:S(2)}, u32[]{:S(2)}) collective-permute-start(bf16[768,768]{1,0:T(8,128)(2,1)S(1)} %copy-done.1), channel_id=1, source_target_pairs={{0,136},{8,128},{128,8},{136,0},{1,137},{9,129},{129,9},{137,1},{2... | collective-permute-start | bytes 3538952 | tf_op jit(solution)/shard_map/ppermute | solution.py:24
  14.8 55.7 %collective-permute-start.9 = (bf16[768,768]{1,0:T(8,128)(2,1)S(1)}, bf16[768,768]{1,0:T(8,128)(2,1)}, u32[]{:S(2)}, u32[]{:S(2)}) collective-permute-start(bf16[768,768]{1,0:T(8,128)(2,1)S(1)} %copy-done.1), channel_id=1, source_target_pairs={{0,128},{8,136},{128,0},{136,8},{1,129},{9,137},{129,1},{137,9},{2... | collective-permute-start | bytes 3538952 | tf_op jit(solution)/shard_map/ppermute | solution.py:24
  19.6 3.4 %copy-start.5 = (bf16[768,768]{1,0:T(8,128)(2,1)S(1)}, bf16[768,768]{1,0:T(8,128)(2,1)}, u32[]{:S(2)}) copy-start(bf16[768,768]{1,0:T(8,128)(2,1)} %param.8) | copy-start | bytes 3538948
  19.6 9.7 %collective-permute-start = (bf16[128,1536]{1,0:T(8,128)(2,1)S(1)}, bf16[128,1536]{1,0:T(8,128)(2,1)S(1)}, u32[]{:S(2)}, u32[]{:S(2)}) collective-permute-start(bf16[128,1536]{1,0:T(8,128)(2,1)S(1)} %bitcast.36), channel_id=1, source_target_pairs={{0,1},{1,2},{2,3},{3,4},{4,5},{5,6},{6,7},{7,0},{8,9},{9,10},{10,1... | collective-permute-start | bytes 1179656 | tf_op jit(solution)/shard_map/ppermute | solution.py:16
  21.6 9.7 %collective-permute-start.4 = (bf16[128,1536]{1,0:T(8,128)(2,1)S(1)}, bf16[128,1536]{1,0:T(8,128)(2,1)S(1)}, u32[]{:S(2)}, u32[]{:S(2)}) collective-permute-start(bf16[128,1536]{1,0:T(8,128)(2,1)S(1)} %bitcast.37), channel_id=1, source_target_pairs={{0,7},{1,0},{2,1},{3,2},{4,3},{5,4},{6,5},{7,6},{8,15},{9,8},{10,9... | collective-permute-start | bytes 1179656 | tf_op jit(solution)/shard_map/ppermute | solution.py:16
  29.4 11.5 %collective-permute-start.1 = (bf16[128,1536]{1,0:T(8,128)(2,1)S(1)}, bf16[128,1536]{1,0:T(8,128)(2,1)S(1)}, u32[]{:S(2)}, u32[]{:S(2)}) collective-permute-start(bf16[128,1536]{1,0:T(8,128)(2,1)S(1)} %collective-permute-done), channel_id=1, source_target_pairs={{0,1},{1,2},{2,3},{3,4},{4,5},{5,6},{6,7},{7,0},{8,9},{9,10},{10,1... | collective-permute-start | bytes 1179656 | tf_op jit(solution)/shard_map/ppermute | solution.py:16
  31.3 10.2 %collective-permute-start.5 = (bf16[128,1536]{1,0:T(8,128)(2,1)S(1)}, bf16[128,1536]{1,0:T(8,128)(2,1)S(1)}, u32[]{:S(2)}, u32[]{:S(2)}) collective-permute-start(bf16[128,1536]{1,0:T(8,128)(2,1)S(1)} %collective-permute-done.4), channel_id=1, source_target_pairs={{0,7},{1,0},{2,1},{3,2},{4,3},{5,4},{6,5},{7,6},{8,15},{9,8},{10,9... | collective-permute-start | bytes 1179656 | tf_op jit(solution)/shard_map/ppermute | solution.py:16
  40.9 41.3 %collective-permute-start.8 = (bf16[768,1536]{1,0:T(8,128)(2,1)S(1)}, bf16[768,1536]{1,0:T(8,128)(2,1)S(1)}, u32[]{:S(2)}, u32[]{:S(2)}) collective-permute-start(bf16[768,1536]{1,0:T(8,128)(2,1)S(1)} %constant_dynamic-update-slice_fusion.8), channel_id=1, source_target_pairs={{0,16},{16,0},{1,17},{17,1},{2,18},{18,2},{3,19},{19,3},{4,20},{20... | collective-permute-start | bytes 7077896 | tf_op jit(solution)/shard_map/ppermute | solution.py:20
  41.4 40.4 %collective-permute-start.3 = (bf16[64,1536]{1,0:T(8,128)(2,1)S(1)}, bf16[64,1536]{1,0:T(8,128)(2,1)S(1)}, u32[]{:S(2)}, u32[]{:S(2)}) collective-permute-start(bf16[64,1536]{1,0:T(8,128)(2,1)S(1)} %slice.16), channel_id=1, source_target_pairs={{0,2},{1,3},{2,4},{3,5},{4,6},{5,7},{6,0},{7,1},{8,10},{9,11},{10,... | collective-permute-start | bytes 589832 | tf_op jit(solution)/shard_map/ppermute | solution.py:16
  46.8 35.1 %copy-start.3 = (bf16[768,768]{1,0:T(8,128)(2,1)}, bf16[768,768]{1,0:T(8,128)(2,1)S(1)}, u32[]{:S(2)}) copy-start(bf16[768,768]{1,0:T(8,128)(2,1)S(1)} %collective-permute-done.10) | copy-start | bytes 3538948
  46.8 35.2 %collective-permute-start.6 = (bf16[64,1536]{1,0:T(8,128)(2,1)S(1)}, bf16[64,1536]{1,0:T(8,128)(2,1)S(1)}, u32[]{:S(2)}, u32[]{:S(2)}) collective-permute-start(bf16[64,1536]{1,0:T(8,128)(2,1)S(1)} %slice.17), channel_id=1, source_target_pairs={{0,6},{1,7},{2,0},{3,1},{4,2},{5,3},{6,4},{7,5},{8,14},{9,15},{10,... | collective-permute-start | bytes 589832 | tf_op jit(solution)/shard_map/ppermute | solution.py:16
  68.6 13.4 %collective-permute-start.2 = (bf16[128,1536]{1,0:T(8,128)(2,1)S(1)}, bf16[128,1536]{1,0:T(8,128)(2,1)S(1)}, u32[]{:S(2)}, u32[]{:S(2)}) collective-permute-start(bf16[128,1536]{1,0:T(8,128)(2,1)S(1)} %collective-permute-done.1), channel_id=1, source_target_pairs={{0,1},{1,2},{2,3},{3,4},{4,5},{5,6},{6,7},{7,0},{8,9},{9,10},{10,1... | collective-permute-start | bytes 1179656 | tf_op jit(solution)/shard_map/ppermute | solution.py:16
  70.5 11.5 %collective-permute-start.7 = (bf16[128,1536]{1,0:T(8,128)(2,1)S(1)}, bf16[128,1536]{1,0:T(8,128)(2,1)S(1)}, u32[]{:S(2)}, u32[]{:S(2)}) collective-permute-start(bf16[128,1536]{1,0:T(8,128)(2,1)S(1)} %collective-permute-done.5), channel_id=1, source_target_pairs={{0,7},{1,0},{2,1},{3,2},{4,3},{5,4},{6,5},{7,6},{8,15},{9,8},{10,9... | collective-permute-start | bytes 1179656 | tf_op jit(solution)/shard_map/ppermute | solution.py:16
  81.8 80.2 %collective-permute-start.12 = (bf16[1536,1536]{1,0:T(8,128)(2,1)}, bf16[1536,1536]{1,0:T(8,128)(2,1)}, u32[]{:S(2)}, u32[]{:S(2)}) collective-permute-start(bf16[1536,1536]{1,0:T(8,128)(2,1)} %maximum_maximum_fusion), channel_id=1, source_target_pairs={{0,16},{16,0},{1,17},{17,1},{2,18},{18,2},{3,19},{19,3},{4,20},{20... | collective-permute-start | bytes 14155784 | tf_op jit(solution)/shard_map/ppermute | solution.py:20
  88.6 43.9 %all-to-all-start.1 = ((bf16[8,128,1536]{2,1,0:T(8,128)(2,1)}), bf16[8,128,1536]{2,1,0:T(8,128)(2,1)S(1)}, u32[]{:S(2)}, u32[]{:S(2)}) async-start(bf16[8,128,1536]{2,1,0:T(8,128)(2,1)} %bitcast.30), calls=%async_computation.1 | async-start | bytes 6291456 | tf_op jit(solution)/shard_map/all_to_all | solution.py:64
  134.1 27.9 %copy-start.2 = (bf16[768,768]{1,0:T(8,128)(2,1)S(1)}, bf16[768,768]{1,0:T(8,128)(2,1)}, u32[]{:S(2)}) copy-start(bf16[768,768]{1,0:T(8,128)(2,1)} %param.9) | copy-start | bytes 3538948
  134.1 28.0 %copy-start.4 = (bf16[768,768]{1,0:T(8,128)(2,1)S(1)}, bf16[768,768]{1,0:T(8,128)(2,1)}, u32[]{:S(2)}) copy-start(bf16[768,768]{1,0:T(8,128)(2,1)} %copy-done.3) | copy-start | bytes 3538948
  134.1 26.9 %all-to-all-start.2 = ((bf16[8,8,8,768]{3,2,1,0:T(8,128)(2,1)}), bf16[8,8,8,768]{3,2,1,0:T(8,128)(2,1)S(1)}, u32[]{:S(2)}, u32[]{:S(2)}) async-start(bf16[8,8,8,768]{3,2,1,0:T(8,128)(2,1)} %bitcast.16), calls=%async_computation.2 | async-start | bytes 1572864 | tf_op jit(solution)/shard_map/all_to_all | solution.py:72
  224.9 13.0 %copy-start = (bf16[8,12288]{1,0:T(8,128)(2,1)S(1)}, bf16[8,12288]{1,0:T(8,128)(2,1)}, u32[]{:S(2)}) copy-start(bf16[8,12288]{1,0:T(8,128)(2,1)} %param.5) | copy-start | bytes 589828
  225.8 10.0 %all-to-all-start.4 = ((bf16[4,8,3072]{2,1,0:T(8,128)(2,1)}), bf16[4,8,3072]{2,1,0:T(8,128)(2,1)S(1)}, u32[]{:S(2)}, u32[]{:S(2)}) async-start(bf16[4,8,3072]{2,1,0:T(8,128)(2,1)} %bitcast.20), calls=%async_computation.4 | async-start | bytes 393216 | tf_op jit(solution)/shard_map/all_to_all | solution.py:79

commit v2 on v1

v2 whole, which is shorter than its diff:
```python
import jax
import jax.numpy as jnp
from jax import lax
from jax.experimental import pallas as pl
from jax.experimental.pallas import tpu as pltpu
from jax.sharding import Mesh, PartitionSpec as P

epsilon = 1e-05
f32, bf16 = jnp.float32, jnp.bfloat16
axes = ("yl", "x", "c", "yh", "z")
unit = 768
tile = 256
room = 24 * 2**20
anywhere = pl.BlockSpec(memory_space=pl.ANY)


def product(left, right):
    return jnp.dot(left, right, preferred_element_type=f32)


def shift(block, steps):
    return lax.ppermute(block, "z", [(i, (i + steps) % 8) for i in range(8)])


def core_partner(block):
    return lax.ppermute(block, "c", [(0, 1), (1, 0)])


def yh_partner(block):
    return lax.ppermute(block, "yh", [(0, 1), (1, 0)])


def swap_where(flag, array, axis):
    return jnp.where(flag, jnp.flip(array, axis), array)


def nothing(array, dependency, out):
    pass


def after(dependency, array):
    return pl.pallas_call(
        nothing,
        in_specs=[anywhere, anywhere],
        out_specs=anywhere,
        out_shape=jax.ShapeDtypeStruct(array.shape, array.dtype),
        input_output_aliases={0: 0},
    )(array, dependency)


def first_kernel(count, *refs):
    blocks, (own, other, _, out, panel) = refs[:count], refs[count:]

    @pl.when(pl.program_id(0) == 0)
    def _():
        for s, block in enumerate(blocks):
            for j in range(8):
                panel[j, s] = block[16 * j : 16 * (j + 1)]

    rows = panel[...].reshape(128 * count, 2 * unit)
    total = product(rows[:, :unit], own[...]) + product(rows[:, unit:], other[...])
    out[...] = total.astype(bf16).reshape(8, 16 * count, tile)


def first_product(blocks, own, other, dependency):
    count = len(blocks)
    weight_spec = pl.BlockSpec((unit, tile), lambda j: (0, j))
    return pl.pallas_call(
        lambda *refs: first_kernel(count, *refs),
        grid=(2 * unit // tile,),
        in_specs=[pl.BlockSpec((128, 2 * unit), lambda j: (0, 0))] * count
        + [weight_spec, weight_spec, anywhere],
        out_specs=pl.BlockSpec((8, 16 * count, tile), lambda j: (0, 0, j)),
        out_shape=pltpu.HBM((8, 16 * count, 2 * unit), bf16),
        scratch_shapes=[pltpu.VMEM((8, count, 16, 2 * unit), bf16)],
        compiler_params=pltpu.CompilerParams(vmem_limit_bytes=room),
        cost_estimate=pl.CostEstimate(
            flops=count * 128 * 8 * unit * unit,
            bytes_accessed=8 * unit * unit,
            transcendentals=0,
        ),
    )(*blocks, own, other, dependency)


def second_kernel(hidden, own, other, own_y, other_y, near, left, right, left_half, right_half):
    places = {0: near.at[0], 2: near.at[1], 6: near.at[2]}
    places |= {1: left.at[0], 3: left.at[1], 7: right.at[0], 5: right.at[1]}
    for n, (weight, weight_y) in enumerate(((own, own_y), (other, other_y))):
        total = product(hidden[0], weight[...]) + product(hidden[1], weight_y[...])
        total = total.astype(bf16).reshape(8, 64, tile)
        for s, place in places.items():
            place[n] = total[s]
        (left_half, right_half)[n][...] = total[4]


def second_product(hidden, weights):
    counts = (3, 2, 2)
    return pl.pallas_call(
        second_kernel,
        grid=(unit // tile,),
        in_specs=[pl.BlockSpec((2, 512, unit), lambda j: (0, 0, 0))]
        + [pl.BlockSpec((unit, tile), lambda j: (0, j))] * 4,
        out_specs=[pl.BlockSpec((k, 2, 64, tile), lambda j: (0, 0, 0, j)) for k in counts]
        + [pl.BlockSpec((64, tile), lambda j: (0, j))] * 2,
        out_shape=[jax.ShapeDtypeStruct((k, 2, 64, unit), bf16) for k in counts]
        + [jax.ShapeDtypeStruct((64, unit), bf16)] * 2,
        compiler_params=pltpu.CompilerParams(vmem_limit_bytes=room),
        cost_estimate=pl.CostEstimate(
            flops=512 * 8 * unit * unit, bytes_accessed=8 * unit * unit, transcendentals=0
        ),
    )(hidden, *weights)


def relay_kernel(near, left, right, left_half, right_half, to_left, to_right):
    for n in range(2):
        a = near[1, n].astype(f32) + left[1, n].astype(f32)
        b = near[2, n].astype(f32) + right[1, n].astype(f32)
        if n == 0:
            a += left_half[...].astype(f32)
        else:
            b += right_half[...].astype(f32)
        to_left[n] = a.astype(bf16)
        to_right[n] = b.astype(bf16)


def relay(*arrays):
    return pl.pallas_call(
        relay_kernel, out_shape=[jax.ShapeDtypeStruct((2, 64, unit), bf16)] * 2
    )(*arrays)


def on_device(tokens, norm_gain, gate_weight, up_weight, down_weight):
    core, yh = lax.axis_index("c"), lax.axis_index("yh")

    inputs = tokens.astype(f32)
    inverse_rms = lax.rsqrt(jnp.mean(inputs * inputs, axis=1, keepdims=True) + epsilon)
    normed = (inputs * inverse_rms * norm_gain).astype(bf16)
    pieces = swap_where(core == 1, normed.reshape(8, 8, 2, unit), 2).reshape(8, 8, 2 * unit)
    pieces = jnp.broadcast_to(pieces.transpose(1, 0, 2)[:, None], (8, 2, 8, 2 * unit))
    block = lax.all_to_all(pieces.reshape(16, 8, 2 * unit), ("yl", "x", "yh"), 0, 0)
    block = block.reshape(128, 2 * unit)

    first = jnp.concatenate((gate_weight, up_weight), axis=1)
    first_other = core_partner(first)

    r1, l1 = shift(block, 1), shift(block, -1)
    r2, l2 = shift(r1, 1), shift(l1, -1)
    r3, l3 = shift(r2, 1), shift(l2, -1)
    opposite = jnp.concatenate((shift(r2[:64], 2), shift(l2[64:], -2)), axis=0)

    down_y = yh_partner(after(block, down_weight))
    blocks = (block, r1, r2, r3, opposite, l3, l2, l1)
    partial = first_product(blocks, first, first_other, down_y)
    terms = lax.all_to_all(partial, ("yl", "x"), 0, 0)

    down_y = after(partial, down_y)
    weights = (down_weight, core_partner(down_weight), down_y, core_partner(down_y))

    summed = jnp.sum(terms.astype(f32), axis=0)
    hidden = (jax.nn.silu(summed[:, :unit]) * summed[:, unit:]).astype(bf16)
    hidden = hidden.reshape(8, 2, 8, unit)

    hidden = hidden.transpose(1, 0, 2, 3)[None]
    hidden = jnp.broadcast_to(hidden, (8, 2, 8, 8, unit)).reshape(16, 64, unit)
    hidden = lax.all_to_all(hidden, ("yl", "x", "yh"), 0, 0).reshape(8, 2, 8, 8, unit)
    hidden = swap_where(yh == 1, hidden, 1)
    hidden = hidden.transpose(1, 2, 0, 3, 4).reshape(2, 512, unit)

    mine, left, right, left_half, right_half = second_product(hidden, weights)
    left, right = shift(left, -1), shift(right, 1)
    left_half, right_half = shift(left_half, -2), shift(right_half, 2)
    to_left, to_right = relay(mine, left, right, left_half, right_half)
    terms = (mine[0], left[0], right[0], shift(to_left, -2), shift(to_right, 2))
    branch = sum(term.astype(f32) for term in terms).astype(bf16)

    branch = branch.reshape(2, 8, 8, unit).transpose(1, 0, 2, 3)
    branch = lax.all_to_all(branch.reshape(8, 16, unit), ("yl", "x"), 0, 0)
    branch = swap_where(core == 1, branch.reshape(8, 2, 8, unit), 1)
    branch = branch.transpose(2, 0, 1, 3).reshape(8, 16 * unit)
    return (tokens.astype(f32) + branch.astype(f32)).astype(bf16)


def solution(mesh):
    grid = Mesh(mesh.devices.reshape(2, 4, 2, 2, 8), axes)
    row, col = ("yl", "x", "c"), ("yh", "z")
    return jax.shard_map(
        on_device,
        mesh=grid,
        in_specs=(P(axes, None), P(), P(row, col), P(row, col), P(col, row)),
        out_specs=P(axes, None),
        check_vma=False,
    )
```

time: 241 us -> 195 us (0.81)
  waiting for transfers between devices: 91.7 us -> 57.7 us
  blocking collectives: 46.4 us -> 71.8 us
  matrix products: 22.9 us -> 0 us
  starting transfers between devices: 53.4 us -> 34.8 us
  Pallas kernels: 0 us -> 15 us
  other arithmetic: 16.5 us -> 5.38 us
    all_to_all x4 -> x1, waiting for transfers between devices: 58.7 us -> 17.7 us  [on_device(): lax.all_to_all(hidden, ('yl', 'x', 'yh'), 0, 0).reshape(8, 2, 8, 8, unit)]
    all_to_all x4 -> x1, starting transfers between devices: 32.1 us -> 5.94 us  [on_device(): lax.all_to_all(hidden, ('yl', 'x', 'yh'), 0, 0).reshape(8, 2, 8, 8, unit)]
    ppermute x8 -> x14, waiting for transfers between devices: 14 us -> 40 us  [shift(): return lax.ppermute(block, 'z', [(i, (i + steps) % 8) for i in range(8)])]
    all_to_all x1 -> x3, blocking collectives: 46.4 us -> 71.8 us  [the longest x1 39.8 us: on_device(): terms = lax.all_to_all(partial, ('yl', 'x'), 0, 0)]
    dot_general x2 -> x0, matrix products: 22.9 us -> none  [product(): return jnp.dot(left, right, preferred_element_type=f32)]
    ppermute x3 -> x1, waiting for transfers between devices: 19 us -> 0.01 us  [yh_partner(): return lax.ppermute(block, 'yh', [(0, 1), (1, 0)])]
    pallas_call x0 -> x5, Pallas kernels: none -> 15 us  [the longest x1 9.34 us: first_product(): pl.pallas_call(lambda *refs: first_kernel(count, *refs), grid=(2 * unit /...]
    concatenate x1 -> x0, other arithmetic: 11.2 us -> none  [on_device(): jnp.concatenate((jnp.concatenate((down_weight, y_partner(down_weight, 2))...]
  transfers between devices with their start and end apart: 17 -> 19, of which waited for: 8 -> 10; matrix products, arithmetic and copies ran while one was open for 9% -> 2% of each run, Pallas kernels for 0% -> 0%
where the time goes in v2:
time: 195 us; the launch traced here: 194 us
  blocking collectives  71.8 us (37%)
  waiting for transfers between devices  57.7 us (30%)
  starting transfers between devices  34.8 us (18%)
  Pallas kernels  15 us (8%)
  local copies, waits for them, and re-layouts  9.11 us (5%)
  other arithmetic  5.38 us (3%)
    ppermute x14, waiting for transfers between devices, shift(): return lax.ppermute(block, 'z', [(i, (i + steps) % 8) for i in range(8)])  40 us
    all_to_all x1, blocking collectives, on_device(): terms = lax.all_to_all(partial, ('yl', 'x'), 0, 0)  39.8 us
    ppermute x14, starting transfers between devices, shift(): return lax.ppermute(block, 'z', [(i, (i + steps) % 8) for i in range(8)])  25.7 us
    all_to_all x1, waiting for transfers between devices, on_device(): lax.all_to_all(hidden, ('yl', 'x', 'yh'), 0, 0).reshape(8, 2, 8, 8, unit)  17.7 us
    all_to_all x1, blocking collectives, on_device(): branch = lax.all_to_all(branch.reshape(8, 16, unit), ('yl', 'x'), 0, 0)  16.7 us
    all_to_all x1, blocking collectives, on_device(): lax.all_to_all(pieces.reshape(16, 8, 2 * unit), ('yl', 'x', 'yh'), 0, 0)  15.3 us
    pallas_call x1, Pallas kernels, first_product(): pl.pallas_call(lambda *refs: first_kernel(count, *refs), grid=(2 * unit /...  9.34 us
    unnamed x30, local copies, waits for them, and re-layouts  6.38 us
  transfers between devices with their start and end apart: 19, of which 10 were waited for; matrix products, arithmetic and copies ran while one was open for 2% of the time, Pallas kernels for 0%

profile of v2, /device:TPU:48, one launch (start us, length us, event | category | flops | bytes accessed | tf_op | source)
XLA Modules:
  0.0 194.1 jit_solution(13435598359205563716)
XLA Ops:
  0.0 2.5 %constant_dynamic-update-slice_fusion.1 = bf16[768,1536]{1,0:T(8,128)(2,1)} fusion(bf16[768,768]{1,0:T(8,128)(2,1)} %param.7), kind=kLoop, calls=%fused_computation.22 | loop fusion | bytes 2359296
  2.5 1.1 constant_dynamic-update-slice_fusion.refs_8_
  3.7 0.2 fusion.1
  3.9 0.1 fusion.3
  4.1 15.3 %all_to_all.20 = bf16[16,8,1536]{2,1,0:T(8,128)(2,1)S(1)} all-to-all(bf16[16,8,1536]{2,1,0:T(8,128)(2,1)S(1)} %bitcast.39), channel_id=1, replica_groups=mesh['yl'=2,'x'=4,'c'=2,'yh'=2,'z'=8] {'yl','x','yh'}, dimensions={0} | all-to-all | bytes 786432 | tf_op jit(solution)/shard_map/all_to_all | solution.py:140
  19.4 1.9 collective-permute-start
  21.3 0.1 collective-permute-start.4
  21.5 1.0 copy.16.array
  22.5 2.6 %collective-permute-start.9 = (bf16[768,768]{1,0:T(8,128)(2,1)}, bf16[768,768]{1,0:T(8,128)(2,1)S(1)}, u32[]{:S(2)}, u32[]{:S(2)}) collective-permute-start(bf16[768,768]{1,0:T(8,128)(2,1)} %shard_map.55), channel_id=1, source_target_pairs={{0,8},{8,0},{1,9},{9,1},{2,10},{10,2},{3,11},{11,3},{4,12},{12,4},... | collective-permute-start | bytes 3538952 | tf_op jit(solution)/shard_map/ppermute | solution.py:30
  25.1 4.9 %collective-permute-done.refs_1_ = bf16[128,1536]{1,0:T(8,128)(2,1)S(1)} collective-permute-done((bf16[128,1536]{1,0:T(8,128)(2,1)S(1)}, bf16[128,1536]{1,0:T(8,128)(2,1)S(1)}, u32[]{:S(2)}, u32[]{:S(2)}) %collective-permute-start) | collective-permute-done | bytes 393248 | tf_op jit(solution)/shard_map/ppermute | solution.py:22
  30.0 1.9 collective-permute-start.1
  31.9 2.3 %collective-permute-start.5 = (bf16[128,1536]{1,0:T(8,128)(2,1)S(1)}, bf16[128,1536]{1,0:T(8,128)(2,1)S(1)}, u32[]{:S(2)}, u32[]{:S(2)}) collective-permute-start(bf16[128,1536]{1,0:T(8,128)(2,1)S(1)} %collective-permute-done.4.refs_7_), channel_id=1, source_target_pairs={{0,7},{1,0},{2,1},{3,2},{4,3},{5,4},{6,5},{7,6},{8,15},{9,8},{10,9... | collective-permute-start | bytes 1179656 | tf_op jit(solution)/shard_map/ppermute | solution.py:22
  34.2 8.2 %collective-permute-done.1.refs_2_ = bf16[128,1536]{1,0:T(8,128)(2,1)S(1)} collective-permute-done((bf16[128,1536]{1,0:T(8,128)(2,1)S(1)}, bf16[128,1536]{1,0:T(8,128)(2,1)S(1)}, u32[]{:S(2)}, u32[]{:S(2)}) %collective-permute-start.1) | collective-permute-done | bytes 393248 | tf_op jit(solution)/shard_map/ppermute | solution.py:22
  42.4 2.4 %collective-permute-start.3 = (bf16[64,1536]{1,0:T(8,128)(2,1)S(1)}, bf16[64,1536]{1,0:T(8,128)(2,1)S(1)}, u32[]{:S(2)}, u32[]{:S(2)}) collective-permute-start(bf16[64,1536]{1,0:T(8,128)(2,1)S(1)} %slice.28), channel_id=1, source_target_pairs={{0,2},{1,3},{2,4},{3,5},{4,6},{5,7},{6,0},{7,1},{8,10},{9,11},{10,... | collective-permute-start | bytes 589832 | tf_op jit(solution)/shard_map/ppermute | solution.py:22
  44.9 3.0 %collective-permute-start.6 = (bf16[64,1536]{1,0:T(8,128)(2,1)S(1)}, bf16[64,1536]{1,0:T(8,128)(2,1)S(1)}, u32[]{:S(2)}, u32[]{:S(2)}) collective-permute-start(bf16[64,1536]{1,0:T(8,128)(2,1)S(1)} %slice.29), channel_id=1, source_target_pairs={{0,6},{1,7},{2,0},{3,1},{4,2},{5,3},{6,4},{7,5},{8,14},{9,15},{10,... | collective-permute-start | bytes 589832 | tf_op jit(solution)/shard_map/ppermute | solution.py:22
  47.9 0.9 collective-permute-start.2
  48.7 5.1 %collective-permute-done.3 = bf16[64,1536]{1,0:T(8,128)(2,1)S(1)} collective-permute-done((bf16[64,1536]{1,0:T(8,128)(2,1)S(1)}, bf16[64,1536]{1,0:T(8,128)(2,1)S(1)}, u32[]{:S(2)}, u32[]{:S(2)}) %collective-permute-start.3) | collective-permute-done | bytes 196640 | tf_op jit(solution)/shard_map/ppermute | solution.py:22
  53.9 2.6 %collective-permute-start.7 = (bf16[128,1536]{1,0:T(8,128)(2,1)S(1)}, bf16[128,1536]{1,0:T(8,128)(2,1)S(1)}, u32[]{:S(2)}, u32[]{:S(2)}) collective-permute-start(bf16[128,1536]{1,0:T(8,128)(2,1)S(1)} %collective-permute-done.5.refs_6_), channel_id=1, source_target_pairs={{0,7},{1,0},{2,1},{3,2},{4,3},{5,4},{6,5},{7,6},{8,15},{9,8},{10,9... | collective-permute-start | bytes 1179656 | tf_op jit(solution)/shard_map/ppermute | solution.py:22
  56.5 4.7 %collective-permute-done.2.refs_3_ = bf16[128,1536]{1,0:T(8,128)(2,1)S(1)} collective-permute-done((bf16[128,1536]{1,0:T(8,128)(2,1)S(1)}, bf16[128,1536]{1,0:T(8,128)(2,1)S(1)}, u32[]{:S(2)}, u32[]{:S(2)}) %collective-permute-start.2) | collective-permute-done | bytes 393248 | tf_op jit(solution)/shard_map/ppermute | solution.py:22
  61.3 2.2 %collective-permute-done.7.refs_5_ = bf16[128,1536]{1,0:T(8,128)(2,1)S(1)} collective-permute-done((bf16[128,1536]{1,0:T(8,128)(2,1)S(1)}, bf16[128,1536]{1,0:T(8,128)(2,1)S(1)}, u32[]{:S(2)}, u32[]{:S(2)}) %collective-permute-start.7) | collective-permute-done | bytes 393248 | tf_op jit(solution)/shard_map/ppermute | solution.py:22
  63.5 9.3 %shard_map.56.dependency = bf16[8,128,1536]{2,1,0:T(8,128)(2,1)} custom-call(bf16[128,1536]{1,0:T(8,128)(2,1)S(1)} %bitcast.38, bf16[128,1536]{1,0:T(8,128)(2,1)S(1)} %collective-permute-done.refs_1_, bf16[128,1536]{1,0:T(8,128)(2,1)S(1)} %collective-permute-done.1.refs_2_, bf16[128,1536]{1,0:T(8,128)(2,1)S(1)} %collective-permute-done.2.refs_3_, ...), custom_call_target="tpu_custom_call" | custom-call | flops 4831838208 | bytes 4718592 | tf_op jit(solution)/shard_map/pallas_call | solution.py:68
  72.8 39.8 %all_to_all.21 = bf16[8,128,1536]{2,1,0:T(8,128)(2,1)S(1)} all-to-all(bf16[8,128,1536]{2,1,0:T(8,128)(2,1)} %shard_map.56.dependency), channel_id=1, replica_groups=mesh['yl'=2,'x'=4,'c'=2,'yh'=2,'z'=8] {'yl','x'}, dimensions={0} | all-to-all | bytes 6291456 | tf_op jit(solution)/shard_map/all_to_all | solution.py:154
  112.6 0.4 convert_reduce_fusion
  113.0 0.1 fusion.5
  113.2 1.4 broadcast_in_dim.5
  114.6 5.9 %all-to-all-start.2 = ((bf16[16,64,768]{2,1,0:T(8,128)(2,1)}), bf16[16,64,768]{2,1,0:T(8,128)(2,1)}, u32[]{:S(2)}, u32[]{:S(2)}) async-start(bf16[16,64,768]{2,1,0:T(8,128)(2,1)} %bitcast.7), calls=%async_computation.2 | async-start | bytes 3145728 | tf_op jit(solution)/shard_map/all_to_all | solution.py:165
  120.5 0.5 collective-permute-start.11
  121.0 17.7 %all-to-all-done.2 = bf16[16,64,768]{2,1,0:T(8,128)(2,1)} async-done(((bf16[16,64,768]{2,1,0:T(8,128)(2,1)}), bf16[16,64,768]{2,1,0:T(8,128)(2,1)}, u32[]{:S(2)}, u32[]{:S(2)}) %all-to-all-start.2) | async-done | bytes 1572896 | tf_op jit(solution)/shard_map/all_to_all | solution.py:165
  138.7 2.5 %fusion = bf16[2,8,8,8,768]{4,3,1,0,2:T(8,128)(2,1)S(1)} fusion(bf16[8,2,8,8,768]{4,3,2,1,0:T(8,128)(2,1)} %bitcast.8, pred[]{:T(512)S(6)} %eq.8), kind=kLoop, calls=%fused_computation.2 | loop fusion | flops 786432 | bytes 3145729 | tf_op jit(solution)/shard_map/transpose | solution.py:167
  141.2 0.2 copy.12
  141.4 1.1 copy-done.4
  142.5 3.4 %shard_map.58 = (bf16[3,2,64,768]{3,2,1,0:T(8,128)(2,1)S(1)}, bf16[2,2,64,768]{3,2,1,0:T(8,128)(2,1)S(1)}, bf16[2,2,64,768]{3,2,1,0:T(8,128)(2,1)S(1)}, bf16[64,768]{1,0:T(8,128)(2,1)S(1)}, bf16[64,768]{1,0:T(8,128)(2,1)S(1)}) custom-call(bf16[2,512,768]{2,1,0:T(8,128)(2,1)S(1)} %bitcast.34, bf16[768,768]{1,0:T(8,128)(2,1)S(1)} %copy-done.2, ...), custom_call_target="tpu_custom_call" | custom-call | flops 2415919104 | bytes 4718592 | tf_op jit(solution)/shard_map/pallas_call | solution.py:98
  145.9 0.8 copy-done.5
  146.7 0.4 collective-permute-start.12
  147.1 2.3 %collective-permute-start.13 = (bf16[2,2,64,768]{3,2,1,0:T(8,128)(2,1)S(1)}, bf16[2,2,64,768]{3,2,1,0:T(8,128)(2,1)S(1)}, u32[]{:S(2)}, u32[]{:S(2)}) collective-permute-start(bf16[2,2,64,768]{3,2,1,0:T(8,128)(2,1)S(1)} %get-tuple-element.14), channel_id=1, source_target_pairs={{0,1},{1,2},{2,3},{3,4},{4,5},{5,6},{6,7},{7,0},{8,9},{9,10},{10,1... | collective-permute-start | bytes 1179656 | tf_op jit(solution)/shard_map/ppermute | solution.py:22
  149.4 5.0 %collective-permute-start.14 = (bf16[64,768]{1,0:T(8,128)(2,1)S(1)}, bf16[64,768]{1,0:T(8,128)(2,1)S(1)}, u32[]{:S(2)}, u32[]{:S(2)}) collective-permute-start(bf16[64,768]{1,0:T(8,128)(2,1)S(1)} %get-tuple-element.15), channel_id=1, source_target_pairs={{0,6},{1,7},{2,0},{3,1},{4,2},{5,3},{6,4},{7,5},{8,14},{9,15},{10,... | collective-permute-start | bytes 294920 | tf_op jit(solution)/shard_map/ppermute | solution.py:22
  154.4 4.3 %collective-permute-done.14.left_half = bf16[64,768]{1,0:T(8,128)(2,1)S(1)} collective-permute-done((bf16[64,768]{1,0:T(8,128)(2,1)S(1)}, bf16[64,768]{1,0:T(8,128)(2,1)S(1)}, u32[]{:S(2)}, u32[]{:S(2)}) %collective-permute-start.14) | collective-permute-done | bytes 98336 | tf_op jit(solution)/shard_map/ppermute | solution.py:22
  158.7 4.3 %collective-permute-done.15.right_half = bf16[64,768]{1,0:T(8,128)(2,1)S(1)} collective-permute-done((bf16[64,768]{1,0:T(8,128)(2,1)S(1)}, bf16[64,768]{1,0:T(8,128)(2,1)S(1)}, u32[]{:S(2)}, u32[]{:S(2)}) %collective-permute-start.15) | collective-permute-done | bytes 98336 | tf_op jit(solution)/shard_map/ppermute | solution.py:22
  163.0 0.6 copy-done.12
  163.6 0.2 copy-done.9
  163.8 0.1 copy-done.10
  163.9 2.2 %shard_map.59 = (bf16[2,64,768]{2,1,0:T(8,128)(2,1)}, bf16[2,64,768]{2,1,0:T(8,128)(2,1)}) custom-call(bf16[3,2,64,768]{3,2,1,0:T(8,128)(2,1)} %copy-done.5, bf16[2,2,64,768]{3,2,1,0:T(8,128)(2,1)} %copy-done.9, bf16[2,2,64,768]{3,2,1,0:T(8,128)(2,1)} %copy-done.10, bf16[64,768]{1,0:T(8,128)(2,1)} %copy-done.11, bf16[64,768]{1,0:T(8,128)(2,1)} %copy-done.12), custom_call_target="tpu_custom_call" | custom-call | tf_op jit(solution)/shard_map/pallas_call | solution.py:127
  166.2 2.9 %collective-permute-start.17 = (bf16[2,64,768]{2,1,0:T(8,128)(2,1)}, bf16[2,64,768]{2,1,0:T(8,128)(2,1)S(1)}, u32[]{:S(2)}, u32[]{:S(2)}) collective-permute-start(bf16[2,64,768]{2,1,0:T(8,128)(2,1)} %get-tuple-element.18), channel_id=1, source_target_pairs={{0,2},{1,3},{2,4},{3,5},{4,6},{5,7},{6,0},{7,1},{8,10},{9,11},{10,... | collective-permute-start | bytes 589832 | tf_op jit(solution)/shard_map/ppermute | solution.py:22
  169.1 5.8 %collective-permute-done.16 = bf16[2,64,768]{2,1,0:T(8,128)(2,1)S(1)} collective-permute-done((bf16[2,64,768]{2,1,0:T(8,128)(2,1)}, bf16[2,64,768]{2,1,0:T(8,128)(2,1)S(1)}, u32[]{:S(2)}, u32[]{:S(2)}) %collective-permute-start.16) | collective-permute-done | bytes 196640 | tf_op jit(solution)/shard_map/ppermute | solution.py:22
  174.9 0.4 collective-permute-done.17
  175.3 1.2 copy_bitcast_fusion
  176.6 16.7 %all_to_all.22 = bf16[8,16,768]{2,1,0:T(8,128)(2,1)S(1)} all-to-all(bf16[8,16,768]{2,1,0:T(8,128)(2,1)S(1)} %copy_bitcast_fusion), channel_id=1, replica_groups=mesh['yl'=2,'x'=4,'c'=2,'yh'=2,'z'=8] {'yl','x'}, dimensions={0} | all-to-all | bytes 393216 | tf_op jit(solution)/shard_map/all_to_all | solution.py:177
  193.3 0.7 fusion.4
  (46 shorter events, 0.2 us)
Async XLA Ops:
  0.0 2.5 %copy-start.8 = (bf16[768,768]{1,0:T(8,128)(2,1)S(1)}, bf16[768,768]{1,0:T(8,128)(2,1)}, u32[]{:S(2)}) copy-start(bf16[768,768]{1,0:T(8,128)(2,1)} %param.8) | copy-start | bytes 3538948
  2.5 1.2 copy-start.6
  2.5 1.4 copy-start.13
  3.7 17.8 %copy-start.2 = (bf16[768,768]{1,0:T(8,128)(2,1)S(1)}, bf16[768,768]{1,0:T(8,128)(2,1)}, u32[]{:S(2)}) copy-start(bf16[768,768]{1,0:T(8,128)(2,1)} %own.1) | copy-start | bytes 3538948
  3.7 59.8 %collective-permute-start.8 = (bf16[768,1536]{1,0:T(8,128)(2,1)}, bf16[768,1536]{1,0:T(8,128)(2,1)}, u32[]{:S(2)}, u32[]{:S(2)}) collective-permute-start(bf16[768,1536]{1,0:T(8,128)(2,1)} %constant_dynamic-update-slice_fusion.refs_8_), channel_id=1, source_target_pairs={{0,16},{16,0},{1,17},{17,1},{2,18},{18,2},{3,19},{19,3},{4,20},{20... | collective-permute-start | bytes 7077896 | tf_op jit(solution)/shard_map/ppermute | solution.py:26
  19.4 3.1 %copy-start = (bf16[16,8,1536]{2,1,0:T(8,128)(2,1)}, bf16[16,8,1536]{2,1,0:T(8,128)(2,1)S(1)}, u32[]{:S(2)}) copy-start(bf16[16,8,1536]{2,1,0:T(8,128)(2,1)S(1)} %all_to_all.20) | copy-start | bytes 1179652
  19.4 10.6 %collective-permute-start = (bf16[128,1536]{1,0:T(8,128)(2,1)S(1)}, bf16[128,1536]{1,0:T(8,128)(2,1)S(1)}, u32[]{:S(2)}, u32[]{:S(2)}) collective-permute-start(bf16[128,1536]{1,0:T(8,128)(2,1)S(1)} %bitcast.35), channel_id=1, source_target_pairs={{0,1},{1,2},{2,3},{3,4},{4,5},{5,6},{6,7},{7,0},{8,9},{9,10},{10,1... | collective-permute-start | bytes 1179656 | tf_op jit(solution)/shard_map/ppermute | solution.py:22
  21.3 10.6 %collective-permute-start.4 = (bf16[128,1536]{1,0:T(8,128)(2,1)S(1)}, bf16[128,1536]{1,0:T(8,128)(2,1)S(1)}, u32[]{:S(2)}, u32[]{:S(2)}) collective-permute-start(bf16[128,1536]{1,0:T(8,128)(2,1)S(1)} %bitcast.36), channel_id=1, source_target_pairs={{0,7},{1,0},{2,1},{3,2},{4,3},{5,4},{6,5},{7,6},{8,15},{9,8},{10,9... | collective-permute-start | bytes 1179656 | tf_op jit(solution)/shard_map/ppermute | solution.py:22
  22.5 41.0 %copy-start.1 = (bf16[16,8,1536]{2,1,0:T(8,128)(2,1)S(1)}, bf16[16,8,1536]{2,1,0:T(8,128)(2,1)}, u32[]{:S(2)}) copy-start(bf16[16,8,1536]{2,1,0:T(8,128)(2,1)} %copy-done) | copy-start | bytes 1179652
  22.5 41.0 %collective-permute-start.9 = (bf16[768,768]{1,0:T(8,128)(2,1)}, bf16[768,768]{1,0:T(8,128)(2,1)S(1)}, u32[]{:S(2)}, u32[]{:S(2)}) collective-permute-start(bf16[768,768]{1,0:T(8,128)(2,1)} %shard_map.55), channel_id=1, source_target_pairs={{0,8},{8,0},{1,9},{9,1},{2,10},{10,2},{3,11},{11,3},{4,12},{12,4},... | collective-permute-start | bytes 3538952 | tf_op jit(solution)/shard_map/ppermute | solution.py:30
  30.0 12.4 %collective-permute-start.1 = (bf16[128,1536]{1,0:T(8,128)(2,1)S(1)}, bf16[128,1536]{1,0:T(8,128)(2,1)S(1)}, u32[]{:S(2)}, u32[]{:S(2)}) collective-permute-start(bf16[128,1536]{1,0:T(8,128)(2,1)S(1)} %collective-permute-done.refs_1_), channel_id=1, source_target_pairs={{0,1},{1,2},{2,3},{3,4},{4,5},{5,6},{6,7},{7,0},{8,9},{9,10},{10,1... | collective-permute-start | bytes 1179656 | tf_op jit(solution)/shard_map/ppermute | solution.py:22
  31.9 12.9 %collective-permute-start.5 = (bf16[128,1536]{1,0:T(8,128)(2,1)S(1)}, bf16[128,1536]{1,0:T(8,128)(2,1)S(1)}, u32[]{:S(2)}, u32[]{:S(2)}) collective-permute-start(bf16[128,1536]{1,0:T(8,128)(2,1)S(1)} %collective-permute-done.4.refs_7_), channel_id=1, source_target_pairs={{0,7},{1,0},{2,1},{3,2},{4,3},{5,4},{6,5},{7,6},{8,15},{9,8},{10,9... | collective-permute-start | bytes 1179656 | tf_op jit(solution)/shard_map/ppermute | solution.py:22
  42.4 11.4 %collective-permute-start.3 = (bf16[64,1536]{1,0:T(8,128)(2,1)S(1)}, bf16[64,1536]{1,0:T(8,128)(2,1)S(1)}, u32[]{:S(2)}, u32[]{:S(2)}) collective-permute-start(bf16[64,1536]{1,0:T(8,128)(2,1)S(1)} %slice.28), channel_id=1, source_target_pairs={{0,2},{1,3},{2,4},{3,5},{4,6},{5,7},{6,0},{7,1},{8,10},{9,11},{10,... | collective-permute-start | bytes 589832 | tf_op jit(solution)/shard_map/ppermute | solution.py:22
  44.9 11.6 %collective-permute-start.6 = (bf16[64,1536]{1,0:T(8,128)(2,1)S(1)}, bf16[64,1536]{1,0:T(8,128)(2,1)S(1)}, u32[]{:S(2)}, u32[]{:S(2)}) collective-permute-start(bf16[64,1536]{1,0:T(8,128)(2,1)S(1)} %slice.29), channel_id=1, source_target_pairs={{0,6},{1,7},{2,0},{3,1},{4,2},{5,3},{6,4},{7,5},{8,14},{9,15},{10,... | collective-permute-start | bytes 589832 | tf_op jit(solution)/shard_map/ppermute | solution.py:22
  47.9 13.4 %collective-permute-start.2 = (bf16[128,1536]{1,0:T(8,128)(2,1)S(1)}, bf16[128,1536]{1,0:T(8,128)(2,1)S(1)}, u32[]{:S(2)}, u32[]{:S(2)}) collective-permute-start(bf16[128,1536]{1,0:T(8,128)(2,1)S(1)} %collective-permute-done.1.refs_2_), channel_id=1, source_target_pairs={{0,1},{1,2},{2,3},{3,4},{4,5},{5,6},{6,7},{7,0},{8,9},{9,10},{10,1... | collective-permute-start | bytes 1179656 | tf_op jit(solution)/shard_map/ppermute | solution.py:22
  53.9 9.6 %collective-permute-start.7 = (bf16[128,1536]{1,0:T(8,128)(2,1)S(1)}, bf16[128,1536]{1,0:T(8,128)(2,1)S(1)}, u32[]{:S(2)}, u32[]{:S(2)}) collective-permute-start(bf16[128,1536]{1,0:T(8,128)(2,1)S(1)} %collective-permute-done.5.refs_6_), channel_id=1, source_target_pairs={{0,7},{1,0},{2,1},{3,2},{4,3},{5,4},{6,5},{7,6},{8,15},{9,8},{10,9... | collective-permute-start | bytes 1179656 | tf_op jit(solution)/shard_map/ppermute | solution.py:22
  63.4 9.4 %copy-start.3 = (bf16[768,768]{1,0:T(8,128)(2,1)}, bf16[768,768]{1,0:T(8,128)(2,1)S(1)}, u32[]{:S(2)}) copy-start(bf16[768,768]{1,0:T(8,128)(2,1)S(1)} %collective-permute-done.9.refs_10_.array) | copy-start | bytes 3538948
  114.6 24.2 %all-to-all-start.2 = ((bf16[16,64,768]{2,1,0:T(8,128)(2,1)}), bf16[16,64,768]{2,1,0:T(8,128)(2,1)}, u32[]{:S(2)}, u32[]{:S(2)}) async-start(bf16[16,64,768]{2,1,0:T(8,128)(2,1)} %bitcast.7), calls=%async_computation.2 | async-start | bytes 3145728 | tf_op jit(solution)/shard_map/all_to_all | solution.py:165
  120.5 20.9 %collective-permute-start.10 = (bf16[768,768]{1,0:T(8,128)(2,1)S(1)}, bf16[768,768]{1,0:T(8,128)(2,1)S(1)}, u32[]{:S(2)}, u32[]{:S(2)}) collective-permute-start(bf16[768,768]{1,0:T(8,128)(2,1)S(1)} %copy-done.2), channel_id=1, source_target_pairs={{0,16},{16,0},{1,17},{17,1},{2,18},{18,2},{3,19},{19,3},{4,20},{20... | collective-permute-start | bytes 3538952 | tf_op jit(solution)/shard_map/ppermute | solution.py:26
  120.5 20.9 %collective-permute-start.11 = (bf16[768,768]{1,0:T(8,128)(2,1)}, bf16[768,768]{1,0:T(8,128)(2,1)S(1)}, u32[]{:S(2)}, u32[]{:S(2)}) collective-permute-start(bf16[768,768]{1,0:T(8,128)(2,1)} %shard_map.57.own_y), channel_id=1, source_target_pairs={{0,16},{16,0},{1,17},{17,1},{2,18},{18,2},{3,19},{19,3},{4,20},{20... | collective-permute-start | bytes 3538952 | tf_op jit(solution)/shard_map/ppermute | solution.py:26
  141.2 1.3 copy-start.4
  145.9 0.8 copy-start.5
  146.7 16.3 %collective-permute-start.12 = (bf16[2,2,64,768]{3,2,1,0:T(8,128)(2,1)S(1)}, bf16[2,2,64,768]{3,2,1,0:T(8,128)(2,1)S(1)}, u32[]{:S(2)}, u32[]{:S(2)}) collective-permute-start(bf16[2,2,64,768]{3,2,1,0:T(8,128)(2,1)S(1)} %get-tuple-element.13), channel_id=1, source_target_pairs={{0,7},{1,0},{2,1},{3,2},{4,3},{5,4},{6,5},{7,6},{8,15},{9,8},{10,9... | collective-permute-start | bytes 1179656 | tf_op jit(solution)/shard_map/ppermute | solution.py:22
  147.1 15.9 %collective-permute-start.13 = (bf16[2,2,64,768]{3,2,1,0:T(8,128)(2,1)S(1)}, bf16[2,2,64,768]{3,2,1,0:T(8,128)(2,1)S(1)}, u32[]{:S(2)}, u32[]{:S(2)}) collective-permute-start(bf16[2,2,64,768]{3,2,1,0:T(8,128)(2,1)S(1)} %get-tuple-element.14), channel_id=1, source_target_pairs={{0,1},{1,2},{2,3},{3,4},{4,5},{5,6},{6,7},{7,0},{8,9},{9,10},{10,1... | collective-permute-start | bytes 1179656 | tf_op jit(solution)/shard_map/ppermute | solution.py:22
  149.4 9.2 %collective-permute-start.14 = (bf16[64,768]{1,0:T(8,128)(2,1)S(1)}, bf16[64,768]{1,0:T(8,128)(2,1)S(1)}, u32[]{:S(2)}, u32[]{:S(2)}) collective-permute-start(bf16[64,768]{1,0:T(8,128)(2,1)S(1)} %get-tuple-element.15), channel_id=1, source_target_pairs={{0,6},{1,7},{2,0},{3,1},{4,2},{5,3},{6,4},{7,5},{8,14},{9,15},{10,... | collective-permute-start | bytes 294920 | tf_op jit(solution)/shard_map/ppermute | solution.py:22
  154.4 8.6 %collective-permute-start.15 = (bf16[64,768]{1,0:T(8,128)(2,1)S(1)}, bf16[64,768]{1,0:T(8,128)(2,1)S(1)}, u32[]{:S(2)}, u32[]{:S(2)}) collective-permute-start(bf16[64,768]{1,0:T(8,128)(2,1)S(1)} %get-tuple-element.16), channel_id=1, source_target_pairs={{0,2},{1,3},{2,4},{3,5},{4,6},{5,7},{6,0},{7,1},{8,10},{9,11},{10,... | collective-permute-start | bytes 294920 | tf_op jit(solution)/shard_map/ppermute | solution.py:22
  158.7 4.4 %copy-start.11 = (bf16[64,768]{1,0:T(8,128)(2,1)}, bf16[64,768]{1,0:T(8,128)(2,1)S(1)}, u32[]{:S(2)}) copy-start(bf16[64,768]{1,0:T(8,128)(2,1)S(1)} %collective-permute-done.14.left_half) | copy-start | bytes 294916
  163.0 0.6 copy-start.12
  163.0 0.8 copy-start.9
  163.0 0.9 copy-start.10
  163.9 29.4 %copy-start.7 = (bf16[8,12288]{1,0:T(8,128)(2,1)S(1)}, bf16[8,12288]{1,0:T(8,128)(2,1)}, u32[]{:S(2)}) copy-start(bf16[8,12288]{1,0:T(8,128)(2,1)} %param.5) | copy-start | bytes 589828
  166.2 8.8 %collective-permute-start.16 = (bf16[2,64,768]{2,1,0:T(8,128)(2,1)}, bf16[2,64,768]{2,1,0:T(8,128)(2,1)S(1)}, u32[]{:S(2)}, u32[]{:S(2)}) collective-permute-start(bf16[2,64,768]{2,1,0:T(8,128)(2,1)} %get-tuple-element.17), channel_id=1, source_target_pairs={{0,6},{1,7},{2,0},{3,1},{4,2},{5,3},{6,4},{7,5},{8,14},{9,15},{10,... | collective-permute-start | bytes 589832 | tf_op jit(solution)/shard_map/ppermute | solution.py:22
  166.2 9.2 %collective-permute-start.17 = (bf16[2,64,768]{2,1,0:T(8,128)(2,1)}, bf16[2,64,768]{2,1,0:T(8,128)(2,1)S(1)}, u32[]{:S(2)}, u32[]{:S(2)}) collective-permute-start(bf16[2,64,768]{2,1,0:T(8,128)(2,1)} %get-tuple-element.18), channel_id=1, source_target_pairs={{0,2},{1,3},{2,4},{3,5},{4,6},{5,7},{6,0},{7,1},{8,10},{9,11},{10,... | collective-permute-start | bytes 589832 | tf_op jit(solution)/shard_map/ppermute | solution.py:22

commit v3 on v2

v3 whole, which is shorter than its diff:
```python
import jax
import jax.numpy as jnp
from jax import lax
from jax.experimental import pallas as pl
from jax.experimental.pallas import tpu as pltpu
from jax.sharding import Mesh, PartitionSpec as P

epsilon = 1e-05
f32, bf16 = jnp.float32, jnp.bfloat16
axes = ("yl", "x", "c", "yh", "z")
unit = 768
tile = 256
room = 24 * 2**20
anywhere = pl.BlockSpec(memory_space=pl.ANY)


def in_hbm(array):
    return pltpu.with_memory_space_constraint(array, pltpu.HBM)


def product(left, right):
    return jnp.dot(left, right, preferred_element_type=f32)


def shift(block, steps):
    return lax.ppermute(block, "z", [(i, (i + steps) % 8) for i in range(8)])


def core_partner(block):
    return lax.ppermute(block, "c", [(0, 1), (1, 0)])


def yh_partner(block):
    return lax.ppermute(block, "yh", [(0, 1), (1, 0)])


def swap_where(flag, array, axis):
    return jnp.where(flag, jnp.flip(array, axis), array)


def nothing(array, dependency, out):
    pass


def after(dependency, array):
    return pl.pallas_call(
        nothing,
        in_specs=[anywhere, anywhere],
        out_specs=anywhere,
        out_shape=jax.ShapeDtypeStruct(array.shape, array.dtype),
        input_output_aliases={0: 0},
        compiler_params=pltpu.CompilerParams(vmem_limit_bytes=2**20),
    )(array, dependency)


def first_kernel(rows, *refs):
    pieces, weight, (out, panel) = refs[: len(rows)], refs[len(rows)], refs[-2:]

    @pl.when(pl.program_id(0) == 0)
    def _():
        for (s, first_row), piece in zip(rows, pieces):
            for j in range(piece.shape[0] // 16):
                panel[first_row // 16 + j, s] = piece[16 * j : 16 * (j + 1)]

    total = product(panel[...].reshape(512, 2 * unit), weight[0])
    out[...] = total.astype(bf16).reshape(8, 64, unit)


def first_product(rows, pieces, weight, *beside):
    half = len(beside) // 2
    return pl.pallas_call(
        lambda *refs: first_kernel(rows, *refs),
        grid=(2,),
        in_specs=[pl.BlockSpec(piece.shape, lambda i: (0, 0)) for piece in pieces]
        + [pl.BlockSpec((1, 2 * unit, unit), lambda i: (i, 0, 0))]
        + [anywhere] * len(beside),
        out_specs=pl.BlockSpec((8, 64, unit), lambda i: (0, half, i)),
        out_shape=pltpu.HBM((8, 128, 2 * unit), bf16),
        input_output_aliases={len(rows) + 1: 0} if half else {},
        scratch_shapes=[pltpu.VMEM((8, 4, 16, 2 * unit), bf16)],
        compiler_params=pltpu.CompilerParams(vmem_limit_bytes=room),
        cost_estimate=pl.CostEstimate(
            flops=512 * 8 * unit * unit, bytes_accessed=8 * unit * unit, transcendentals=0
        ),
    )(*pieces, weight, *beside)


def stack_kernel(a, b, c, d, out):
    out[0, :unit], out[0, unit:], out[1, :unit], out[1, unit:] = a[...], b[...], c[...], d[...]


def stack(*weights):
    return pl.pallas_call(
        stack_kernel,
        grid=(3,),
        in_specs=[pl.BlockSpec((unit, tile), lambda j: (0, j))] * 4,
        out_specs=pl.BlockSpec((2, 2 * unit, tile), lambda j: (0, 0, j)),
        out_shape=jax.ShapeDtypeStruct((2, 2 * unit, unit), bf16),
        compiler_params=pltpu.CompilerParams(vmem_limit_bytes=8 * 2**20),
    )(*(in_hbm(weight) for weight in weights))


order = (0, 1, 7, 2, 6, 3, 5, 4)


def second_kernel(_, mine, theirs, weight, near, left, right, left_half, right_half):
    places = {0: near.at[0], 2: near.at[1], 6: near.at[2]}
    places |= {1: left.at[0], 3: left.at[1], 7: right.at[0], 5: right.at[1]}
    total = product(mine[...].reshape(512, unit), weight[0, :unit])
    total += product(theirs[...].reshape(512, unit), weight[0, unit:])
    total = total.reshape(8, 8, 8, unit)
    for k, s in enumerate(order):
        piece = total[:, k].reshape(64, unit).astype(bf16)
        if s != 4:
            places[s][0] = piece
            continue
        for n, half in enumerate((left_half, right_half)):

            @pl.when(pl.program_id(0) == n)
            def _(half=half, piece=piece):
                half[...] = piece


def second_product(yh, hidden, weight):
    counts = (3, 2, 2)
    return pl.pallas_call(
        second_kernel,
        grid_spec=pltpu.PrefetchScalarGridSpec(
            num_scalar_prefetch=1,
            grid=(2,),
            in_specs=[
                pl.BlockSpec((8, 1, 64, unit), lambda n, yh: (0, yh[0], 0, 0)),
                pl.BlockSpec((8, 1, 64, unit), lambda n, yh: (0, 1 - yh[0], 0, 0)),
                pl.BlockSpec((1, 2 * unit, unit), lambda n, yh: (n, 0, 0)),
            ],
            out_specs=[pl.BlockSpec((k, 1, 64, unit), lambda n, yh: (0, n, 0, 0)) for k in counts]
            + [pl.BlockSpec((64, unit), lambda n, yh: (0, 0))] * 2,
        ),
        out_shape=[jax.ShapeDtypeStruct((k, 2, 64, unit), bf16) for k in counts]
        + [jax.ShapeDtypeStruct((64, unit), bf16)] * 2,
        compiler_params=pltpu.CompilerParams(vmem_limit_bytes=room),
        cost_estimate=pl.CostEstimate(
            flops=512 * 8 * unit * unit, bytes_accessed=8 * unit * unit, transcendentals=0
        ),
    )(yh.reshape(1), hidden, hidden, weight)


def relay_kernel(near, left, right, left_half, right_half, to_left, to_right):
    for n in range(2):
        a = near[1, n].astype(f32) + left[1, n].astype(f32)
        b = near[2, n].astype(f32) + right[1, n].astype(f32)
        if n == 0:
            a += left_half[...].astype(f32)
        else:
            b += right_half[...].astype(f32)
        to_left[n] = a.astype(bf16)
        to_right[n] = b.astype(bf16)


def relay(*arrays):
    return pl.pallas_call(
        relay_kernel,
        out_shape=[jax.ShapeDtypeStruct((2, 64, unit), bf16)] * 2,
        compiler_params=pltpu.CompilerParams(vmem_limit_bytes=6 * 2**20),
    )(*arrays)


def prepare_kernel(core, tokens, norm_gain, out):
    inputs = tokens[...].astype(f32)
    inverse_rms = lax.rsqrt(jnp.mean(inputs * inputs, axis=1, keepdims=True) + epsilon)
    normed = inputs * inverse_rms * norm_gain[...]
    swap = core[0] == 1
    for j in range(8):
        low = normed[:, 2 * j * unit : (2 * j + 1) * unit]
        high = normed[:, (2 * j + 1) * unit : (2 * j + 2) * unit]
        for y in range(2):
            out[j, y, :, :unit] = jnp.where(swap, high, low).astype(bf16)
            out[j, y, :, unit:] = jnp.where(swap, low, high).astype(bf16)


def prepare(core, tokens, norm_gain):
    vmem = pl.BlockSpec(memory_space=pltpu.VMEM)
    return pl.pallas_call(
        prepare_kernel,
        in_specs=[pl.BlockSpec(memory_space=pltpu.SMEM), vmem, vmem],
        out_specs=vmem,
        out_shape=pltpu.HBM((8, 2, 8, 2 * unit), bf16),
        compiler_params=pltpu.CompilerParams(vmem_limit_bytes=8 * 2**20),
    )(core.reshape(1), in_hbm(tokens), in_hbm(norm_gain.reshape(1, -1)))


def on_device(tokens, norm_gain, gate_weight, up_weight, down_weight):
    core, yh = lax.axis_index("c"), lax.axis_index("yh")

    pieces = prepare(core, tokens, norm_gain)
    block = lax.all_to_all(pieces.reshape(16, 8, 2 * unit), ("yl", "x", "yh"), 0, 0)
    block = block.reshape(128, 2 * unit)

    r1, l1 = shift(block, 1), shift(block, -1)
    r2, l2 = shift(r1, 1), shift(l1, -1)
    r3, l3 = shift(r2, 1), shift(l2, -1)
    r4, l4 = shift(r2[:64], 2), shift(l2[64:], -2)

    first = stack(
        gate_weight, core_partner(gate_weight), up_weight, core_partner(up_weight)
    )
    down_y = yh_partner(after(block, down_weight))
    whole = [(s, 0) for s in range(4)]
    partial = first_product(whole, (block, r1, l1, r2), first)
    far = [(0, 0), (1, 0), (2, 0), (3, 0), (3, 64)]
    partial = first_product(far, (l2, r3, l3, r4, l4), first, partial, down_y)
    terms = lax.all_to_all(partial, ("yl", "x"), 0, 0)

    down_y = after(partial, down_y)
    second = stack(down_weight, down_y, core_partner(down_weight), core_partner(down_y))

    summed = jnp.sum(terms.astype(f32), axis=0)
    hidden = (jax.nn.silu(summed[:, :unit]) * summed[:, unit:]).astype(bf16)

    hidden = hidden.reshape(8, 2, 8, unit).transpose(1, 0, 2, 3)[None]
    hidden = jnp.broadcast_to(hidden, (8, 2, 8, 8, unit)).reshape(16, 64, unit)
    hidden = lax.all_to_all(hidden, ("yl", "x", "yh"), 0, 0).reshape(8, 2, 64, unit)

    mine, left, right, left_half, right_half = second_product(yh, hidden, second)
    left, right = shift(left, -1), shift(right, 1)
    left_half, right_half = shift(left_half, -2), shift(right_half, 2)
    to_left, to_right = relay(mine, left, right, left_half, right_half)
    terms = (mine[0], left[0], right[0], shift(to_left, -2), shift(to_right, 2))
    branch = sum(term.astype(f32) for term in terms).astype(bf16)

    branch = branch.reshape(2, 8, 8, unit).transpose(1, 0, 2, 3)
    branch = lax.all_to_all(branch.reshape(8, 16, unit), ("yl", "x"), 0, 0)
    branch = swap_where(core == 1, branch.reshape(8, 2, 8, unit), 1)
    branch = branch.transpose(2, 0, 1, 3).reshape(8, 16 * unit)
    return (tokens.astype(f32) + branch.astype(f32)).astype(bf16)


def solution(mesh):
    grid = Mesh(mesh.devices.reshape(2, 4, 2, 2, 8), axes)
    row, col = ("yl", "x", "c"), ("yh", "z")
    return jax.shard_map(
        on_device,
        mesh=grid,
        in_specs=(P(axes, None), P(), P(row, col), P(row, col), P(col, row)),
        out_specs=P(axes, None),
        check_vma=False,
    )
```

time: 195 us -> 172 us (0.88)
  blocking collectives: 71.8 us -> 37.1 us
  starting transfers between devices: 34.8 us -> 45.9 us
  Pallas kernels: 15 us -> 20.7 us
  other arithmetic: 5.38 us -> 2.11 us
  waiting for transfers between devices: 57.7 us -> 54.7 us
    all_to_all x2 -> x0, blocking collectives: 32 us -> none  [the longest x1 16.7 us: on_device(): branch = lax.all_to_all(branch.reshape(8, 16, unit), ('yl', 'x'), 0, 0)]
    all_to_all x1 -> x3, starting transfers between devices: 5.94 us -> 21.2 us  [the longest x1 7.28 us: on_device(): lax.all_to_all(pieces.reshape(16, 8, 2 * unit), ('yl', 'x', 'yh'), 0, 0)]
    pallas_call x2 -> x6, Pallas kernels: 12.8 us -> 20.5 us  [the longest x2 7.7 us: first_product(): pl.pallas_call(lambda *refs: first_kernel(rows, *refs), grid=(2,), in_spe...]
    ppermute x14, waiting for transfers between devices: 40 us -> 33.9 us  [shift(): return lax.ppermute(block, 'z', [(i, (i + steps) % 8) for i in range(8)])]
    ppermute x14, starting transfers between devices: 25.7 us -> 21 us  [shift(): return lax.ppermute(block, 'z', [(i, (i + steps) % 8) for i in range(8)])]
    all_to_all x1, blocking collectives: 39.8 us -> 37.1 us  [on_device(): terms = lax.all_to_all(partial, ('yl', 'x'), 0, 0)]
    ppermute x3 -> x4, waiting for transfers between devices: 0.01 us -> 2.69 us  [core_partner(): return lax.ppermute(block, 'c', [(0, 1), (1, 0)])]
    transpose x1 -> x0, other arithmetic: 2.46 us -> none  [on_device(): hidden = hidden.transpose(1, 2, 0, 3, 4).reshape(2, 512, unit)]
  transfers between devices with their start and end apart: 19 -> 22, of which waited for: 10 -> 12; matrix products, arithmetic and copies ran while one was open for 2% -> 0% of each run, Pallas kernels for 0% -> 6%
where the time goes in v3:
time: 172 us; the launch traced here: 170 us
  waiting for transfers between devices  54.7 us (32%)
  starting transfers between devices  45.9 us (27%)
  blocking collectives  37.1 us (22%)
  Pallas kernels  20.7 us (12%)
  local copies, waits for them, and re-layouts  9.27 us (5%)
  other arithmetic  2.11 us (1%)
    all_to_all x1, blocking collectives, on_device(): terms = lax.all_to_all(partial, ('yl', 'x'), 0, 0)  37.1 us
    ppermute x14, waiting for transfers between devices, shift(): return lax.ppermute(block, 'z', [(i, (i + steps) % 8) for i in range(8)])  33.9 us
    ppermute x14, starting transfers between devices, shift(): return lax.ppermute(block, 'z', [(i, (i + steps) % 8) for i in range(8)])  21 us
    unnamed x21, local copies, waits for them, and re-layouts  7.92 us
    pallas_call x2, Pallas kernels, first_product(): pl.pallas_call(lambda *refs: first_kernel(rows, *refs), grid=(2,), in_spe...  7.7 us
    all_to_all x1, starting transfers between devices, on_device(): lax.all_to_all(pieces.reshape(16, 8, 2 * unit), ('yl', 'x', 'yh'), 0, 0)  7.28 us
    all_to_all x1, starting transfers between devices, on_device(): lax.all_to_all(hidden, ('yl', 'x', 'yh'), 0, 0).reshape(8, 2, 64, unit)  7.11 us
    all_to_all x1, waiting for transfers between devices, on_device(): lax.all_to_all(pieces.reshape(16, 8, 2 * unit), ('yl', 'x', 'yh'), 0, 0)  7.05 us
  transfers between devices with their start and end apart: 22, of which 12 were waited for; matrix products, arithmetic and copies ran while one was open for 0% of the time, Pallas kernels for 6%

profile of v3, /device:TPU:48, one launch (start us, length us, event | category | flops | bytes accessed | tf_op | source)
XLA Modules:
  0.0 170.0 jit_solution(9449239606395839069)
XLA Ops:
  0.0 2.0 %shard_map.55 = bf16[8,2,8,1536]{3,2,1,0:T(8,128)(2,1)} custom-call(s32[1]{0:T(128)} %bitcast.1.core, bf16[8,12288]{1,0:T(8,128)(2,1)} %tokens.1, f32[1,12288]{1,0:T(1,128)} %bitcast.39), custom_call_target="tpu_custom_call" | custom-call | tf_op jit(solution)/shard_map/pallas_call | solution.py:183
  2.0 7.3 %all-to-all-start = ((bf16[16,8,1536]{2,1,0:T(8,128)(2,1)}), bf16[16,8,1536]{2,1,0:T(8,128)(2,1)S(1)}, u32[]{:S(2)}, u32[]{:S(2)}) async-start(bf16[16,8,1536]{2,1,0:T(8,128)(2,1)} %bitcast.35), calls=%async_computation | async-start | bytes 786432 | tf_op jit(solution)/shard_map/all_to_all | solution.py:196
  9.3 0.5 collective-permute-start.9
  9.8 7.1 %all-to-all-done = bf16[16,8,1536]{2,1,0:T(8,128)(2,1)S(1)} async-done(((bf16[16,8,1536]{2,1,0:T(8,128)(2,1)}), bf16[16,8,1536]{2,1,0:T(8,128)(2,1)S(1)}, u32[]{:S(2)}, u32[]{:S(2)}) %all-to-all-start) | async-done | bytes 393248 | tf_op jit(solution)/shard_map/all_to_all | solution.py:196
  16.9 1.9 %collective-permute-start.2 = (bf16[128,1536]{1,0:T(8,128)(2,1)S(1)}, bf16[128,1536]{1,0:T(8,128)(2,1)S(1)}, u32[]{:S(2)}, u32[]{:S(2)}) collective-permute-start(bf16[128,1536]{1,0:T(8,128)(2,1)S(1)} %bitcast.30), channel_id=1, source_target_pairs={{0,1},{1,2},{2,3},{3,4},{4,5},{5,6},{6,7},{7,0},{8,9},{9,10},{10,1... | collective-permute-start | bytes 1179656 | tf_op jit(solution)/shard_map/ppermute | solution.py:26
  18.8 0.1 collective-permute-start
  19.0 2.7 %collective-permute-start.10 = (bf16[768,768]{1,0:T(8,128)(2,1)S(1)}, bf16[768,768]{1,0:T(8,128)(2,1)S(1)}, u32[]{:S(2)}, u32[]{:S(2)}) collective-permute-start(bf16[768,768]{1,0:T(8,128)(2,1)S(1)} %shard_map.58), channel_id=1, source_target_pairs={{0,8},{8,0},{1,9},{9,1},{2,10},{10,2},{3,11},{11,3},{4,12},{12,4},... | collective-permute-start | bytes 3538952 | tf_op jit(solution)/shard_map/ppermute | solution.py:34
  21.7 4.9 %collective-permute-done.2.refs_1_ = bf16[128,1536]{1,0:T(8,128)(2,1)S(1)} collective-permute-done((bf16[128,1536]{1,0:T(8,128)(2,1)S(1)}, bf16[128,1536]{1,0:T(8,128)(2,1)S(1)}, u32[]{:S(2)}, u32[]{:S(2)}) %collective-permute-start.2) | collective-permute-done | bytes 393248 | tf_op jit(solution)/shard_map/ppermute | solution.py:26
  26.6 1.9 %collective-permute-start.3 = (bf16[128,1536]{1,0:T(8,128)(2,1)S(1)}, bf16[128,1536]{1,0:T(8,128)(2,1)S(1)}, u32[]{:S(2)}, u32[]{:S(2)}) collective-permute-start(bf16[128,1536]{1,0:T(8,128)(2,1)S(1)} %collective-permute-done.2.refs_1_), channel_id=1, source_target_pairs={{0,1},{1,2},{2,3},{3,4},{4,5},{5,6},{6,7},{7,0},{8,9},{9,10},{10,1... | collective-permute-start | bytes 1179656 | tf_op jit(solution)/shard_map/ppermute | solution.py:26
  28.5 2.3 %collective-permute-start.1 = (bf16[128,1536]{1,0:T(8,128)(2,1)S(1)}, bf16[128,1536]{1,0:T(8,128)(2,1)S(1)}, u32[]{:S(2)}, u32[]{:S(2)}) collective-permute-start(bf16[128,1536]{1,0:T(8,128)(2,1)S(1)} %collective-permute-done.refs_2_), channel_id=1, source_target_pairs={{0,7},{1,0},{2,1},{3,2},{4,3},{5,4},{6,5},{7,6},{8,15},{9,8},{10,9... | collective-permute-start | bytes 1179656 | tf_op jit(solution)/shard_map/ppermute | solution.py:26
  30.8 7.3 %collective-permute-done.3.refs_3_ = bf16[128,1536]{1,0:T(8,128)(2,1)S(1)} collective-permute-done((bf16[128,1536]{1,0:T(8,128)(2,1)S(1)}, bf16[128,1536]{1,0:T(8,128)(2,1)S(1)}, u32[]{:S(2)}, u32[]{:S(2)}) %collective-permute-start.3) | collective-permute-done | bytes 393248 | tf_op jit(solution)/shard_map/ppermute | solution.py:26
  38.2 0.4 collective-permute-done.1.refs_0_
  38.6 2.5 %collective-permute-start.5 = (bf16[128,1536]{1,0:T(8,128)(2,1)S(1)}, bf16[128,1536]{1,0:T(8,128)(2,1)S(1)}, u32[]{:S(2)}, u32[]{:S(2)}) collective-permute-start(bf16[128,1536]{1,0:T(8,128)(2,1)S(1)} %collective-permute-done.1.refs_0_), channel_id=1, source_target_pairs={{0,7},{1,0},{2,1},{3,2},{4,3},{5,4},{6,5},{7,6},{8,15},{9,8},{10,9... | collective-permute-start | bytes 1179656 | tf_op jit(solution)/shard_map/ppermute | solution.py:26
  41.2 3.2 %collective-permute-start.6 = (bf16[64,1536]{1,0:T(8,128)(2,1)S(1)}, bf16[64,1536]{1,0:T(8,128)(2,1)S(1)}, u32[]{:S(2)}, u32[]{:S(2)}) collective-permute-start(bf16[64,1536]{1,0:T(8,128)(2,1)S(1)} %slice.28), channel_id=1, source_target_pairs={{0,2},{1,3},{2,4},{3,5},{4,6},{5,7},{6,0},{7,1},{8,10},{9,11},{10,... | collective-permute-start | bytes 589832 | tf_op jit(solution)/shard_map/ppermute | solution.py:26
  44.4 1.0 collective-permute-start.7
  45.4 3.3 %shard_map.56.refs_4_.refs_5_ = bf16[2,1536,768]{2,1,0:T(8,128)(2,1)S(1)} custom-call(bf16[768,768]{1,0:T(8,128)(2,1)} %a.2, bf16[768,768]{1,0:T(8,128)(2,1)} %copy-done.7, bf16[768,768]{1,0:T(8,128)(2,1)} %c.1, bf16[768,768]{1,0:T(8,128)(2,1)} %collective-permute-done.9.d), custom_call_target="tpu_custom_call" | custom-call | tf_op jit(solution)/shard_map/pallas_call | solution.py:93
  48.7 3.8 %shard_map.57.refs_6_ = bf16[8,128,1536]{2,1,0:T(8,128)(2,1)} custom-call(bf16[128,1536]{1,0:T(8,128)(2,1)S(1)} %bitcast.33, bf16[128,1536]{1,0:T(8,128)(2,1)S(1)} %collective-permute-done.2.refs_1_, bf16[128,1536]{1,0:T(8,128)(2,1)S(1)} %collective-permute-done.refs_2_, bf16[128,1536]{1,0:T(8,128)(2,1)S(1)} %collective-permute-done.3.refs_3_, ...), custom_call_target="tpu_custom_call" | custom-call | flops 2415919104 | bytes 4718592 | tf_op jit(solution)/shard_map/pallas_call | solution.py:71
  52.5 5.8 %collective-permute-done.6.refs_3_ = bf16[64,1536]{1,0:T(8,128)(2,1)S(1)} collective-permute-done((bf16[64,1536]{1,0:T(8,128)(2,1)S(1)}, bf16[64,1536]{1,0:T(8,128)(2,1)S(1)}, u32[]{:S(2)}, u32[]{:S(2)}) %collective-permute-start.6) | collective-permute-done | bytes 196640 | tf_op jit(solution)/shard_map/ppermute | solution.py:26
  58.4 3.9 %shard_map.59.dependency = bf16[8,128,1536]{2,1,0:T(8,128)(2,1)} custom-call(bf16[128,1536]{1,0:T(8,128)(2,1)S(1)} %collective-permute-done.1.refs_0_, bf16[128,1536]{1,0:T(8,128)(2,1)S(1)} %collective-permute-done.4.refs_1_, bf16[128,1536]{1,0:T(8,128)(2,1)S(1)} %collective-permute-done.5.refs_2_, ...), custom_call_target="tpu_custom_call", output_to_operand_aliasing={{}: (6, {})} | custom-call | flops 2415919104 | bytes 4718592 | tf_op jit(solution)/shard_map/pallas_call | solution.py:71
  62.3 37.1 %all_to_all.20 = bf16[8,128,1536]{2,1,0:T(8,128)(2,1)S(1)} all-to-all(bf16[8,128,1536]{2,1,0:T(8,128)(2,1)} %shard_map.59.dependency), channel_id=1, replica_groups=mesh['yl'=2,'x'=4,'c'=2,'yh'=2,'z'=8] {'yl','x'}, dimensions={0} | all-to-all | bytes 6291456 | tf_op jit(solution)/shard_map/all_to_all | solution.py:212
  99.3 0.4 convert_reduce_fusion
  99.8 0.1 fusion
  99.9 1.3 broadcast_in_dim.2
  101.2 7.1 %all-to-all-start.2 = ((bf16[16,64,768]{2,1,0:T(8,128)(2,1)}), bf16[16,64,768]{2,1,0:T(8,128)(2,1)}, u32[]{:S(2)}, u32[]{:S(2)}) async-start(bf16[16,64,768]{2,1,0:T(8,128)(2,1)} %bitcast.34), calls=%async_computation.2 | async-start | bytes 3145728 | tf_op jit(solution)/shard_map/all_to_all | solution.py:222
  108.4 1.3 copy-done.2
  109.6 1.0 copy-done.3
  110.7 0.5 collective-permute-start.12
  111.1 0.4 collective-permute-done.11.c
  111.5 2.3 %collective-permute-done.12.d = bf16[768,768]{1,0:T(8,128)(2,1)S(1)} collective-permute-done((bf16[768,768]{1,0:T(8,128)(2,1)}, bf16[768,768]{1,0:T(8,128)(2,1)S(1)}, u32[]{:S(2)}, u32[]{:S(2)}) %collective-permute-start.12) | collective-permute-done | bytes 1179680 | tf_op jit(solution)/shard_map/ppermute | solution.py:30
  113.8 1.1 copy-done.8
  114.9 3.2 %shard_map.61.weight = bf16[2,1536,768]{2,1,0:T(8,128)(2,1)S(1)} custom-call(bf16[768,768]{1,0:T(8,128)(2,1)} %a.3, bf16[768,768]{1,0:T(8,128)(2,1)} %copy-done.3, bf16[768,768]{1,0:T(8,128)(2,1)} %collective-permute-done.11.c, bf16[768,768]{1,0:T(8,128)(2,1)} %copy-done.8), custom_call_target="tpu_custom_call" | custom-call | tf_op jit(solution)/shard_map/pallas_call | solution.py:93
  118.2 2.1 %copy-done.4 = bf16[2,1536,768]{2,1,0:T(8,128)(2,1)} copy-done((bf16[2,1536,768]{2,1,0:T(8,128)(2,1)}, bf16[2,1536,768]{2,1,0:T(8,128)(2,1)S(1)}, u32[]{:S(2)}) %copy-start.4) | copy-done | bytes 4718616
  120.3 4.1 %all-to-all-done.2 = bf16[16,64,768]{2,1,0:T(8,128)(2,1)} async-done(((bf16[16,64,768]{2,1,0:T(8,128)(2,1)}), bf16[16,64,768]{2,1,0:T(8,128)(2,1)}, u32[]{:S(2)}, u32[]{:S(2)}) %all-to-all-start.2) | async-done | bytes 1572896 | tf_op jit(solution)/shard_map/all_to_all | solution.py:222
  124.4 2.3 %copy-done.5 = bf16[2,1536,768]{2,1,0:T(8,128)(2,1)S(1)} copy-done((bf16[2,1536,768]{2,1,0:T(8,128)(2,1)S(1)}, bf16[2,1536,768]{2,1,0:T(8,128)(2,1)}, u32[]{:S(2)}) %copy-start.5) | copy-done | bytes 4718616
  126.7 4.3 %shard_map.62 = (bf16[3,2,64,768]{3,2,1,0:T(8,128)(2,1)S(1)}, bf16[2,2,64,768]{3,2,1,0:T(8,128)(2,1)S(1)}, bf16[2,2,64,768]{3,2,1,0:T(8,128)(2,1)S(1)}, bf16[64,768]{1,0:T(8,128)(2,1)S(1)}, bf16[64,768]{1,0:T(8,128)(2,1)S(1)}) custom-call(s32[1]{0:T(128)} %bitcast._, bf16[8,2,64,768]{3,2,1,0:T(8,128)(2,1)} %bitcast.8.mine.theirs, ...), custom_call_target="tpu_custom_call" | custom-call | flops 2415919104 | bytes 4718592 | tf_op jit(solution)/shard_map/pallas_call | solution.py:126
  131.1 2.0 %collective-permute-start.14 = (bf16[2,2,64,768]{3,2,1,0:T(8,128)(2,1)S(1)}, bf16[2,2,64,768]{3,2,1,0:T(8,128)(2,1)S(1)}, u32[]{:S(2)}, u32[]{:S(2)}) collective-permute-start(bf16[2,2,64,768]{3,2,1,0:T(8,128)(2,1)S(1)} %get-tuple-element.14), channel_id=1, source_target_pairs={{0,1},{1,2},{2,3},{3,4},{4,5},{5,6},{6,7},{7,0},{8,9},{9,10},{10,1... | collective-permute-start | bytes 1179656 | tf_op jit(solution)/shard_map/ppermute | solution.py:26
  133.1 1.3 collective-permute-start.15
  134.5 1.6 collective-permute-start.16
  136.1 9.3 %collective-permute-done.15.left_half = bf16[64,768]{1,0:T(8,128)(2,1)S(1)} collective-permute-done((bf16[64,768]{1,0:T(8,128)(2,1)S(1)}, bf16[64,768]{1,0:T(8,128)(2,1)S(1)}, u32[]{:S(2)}, u32[]{:S(2)}) %collective-permute-start.15) | collective-permute-done | bytes 98336 | tf_op jit(solution)/shard_map/ppermute | solution.py:26
  145.4 0.1 shard_map.63
  145.5 0.7 collective-permute-start.17
  146.2 2.3 %collective-permute-start.18 = (bf16[2,64,768]{2,1,0:T(8,128)(2,1)S(1)}, bf16[2,64,768]{2,1,0:T(8,128)(2,1)S(1)}, u32[]{:S(2)}, u32[]{:S(2)}) collective-permute-start(bf16[2,64,768]{2,1,0:T(8,128)(2,1)S(1)} %get-tuple-element.18), channel_id=1, source_target_pairs={{0,2},{1,3},{2,4},{3,5},{4,6},{5,7},{6,0},{7,1},{8,10},{9,11},{10,... | collective-permute-start | bytes 589832 | tf_op jit(solution)/shard_map/ppermute | solution.py:26
  148.5 4.3 %collective-permute-done.17 = bf16[2,64,768]{2,1,0:T(8,128)(2,1)S(1)} collective-permute-done((bf16[2,64,768]{2,1,0:T(8,128)(2,1)S(1)}, bf16[2,64,768]{2,1,0:T(8,128)(2,1)S(1)}, u32[]{:S(2)}, u32[]{:S(2)}) %collective-permute-start.17) | collective-permute-done | bytes 196640 | tf_op jit(solution)/shard_map/ppermute | solution.py:26
  152.8 1.8 %collective-permute-done.18 = bf16[2,64,768]{2,1,0:T(8,128)(2,1)S(1)} collective-permute-done((bf16[2,64,768]{2,1,0:T(8,128)(2,1)S(1)}, bf16[2,64,768]{2,1,0:T(8,128)(2,1)S(1)}, u32[]{:S(2)}, u32[]{:S(2)}) %collective-permute-start.18) | collective-permute-done | bytes 196640 | tf_op jit(solution)/shard_map/ppermute | solution.py:26
  154.6 0.8 copy_bitcast_fusion
  155.4 6.8 %all-to-all-start.3 = ((bf16[8,16,768]{2,1,0:T(8,128)(2,1)}), bf16[8,16,768]{2,1,0:T(8,128)(2,1)S(1)}, u32[]{:S(2)}, u32[]{:S(2)}) async-start(bf16[8,16,768]{2,1,0:T(8,128)(2,1)} %copy_bitcast_fusion), calls=%async_computation.3 | async-start | bytes 393216 | tf_op jit(solution)/shard_map/all_to_all | solution.py:232
  162.2 6.9 %all-to-all-done.3 = bf16[8,16,768]{2,1,0:T(8,128)(2,1)S(1)} async-done(((bf16[8,16,768]{2,1,0:T(8,128)(2,1)}), bf16[8,16,768]{2,1,0:T(8,128)(2,1)S(1)}, u32[]{:S(2)}, u32[]{:S(2)}) %all-to-all-start.3) | async-done | bytes 196640 | tf_op jit(solution)/shard_map/all_to_all | solution.py:232
  169.2 0.7 add_convert_fusion
  (36 shorter events, 0.3 us)
Async XLA Ops:
  0.0 18.9 %copy-start.6 = (bf16[768,768]{1,0:T(8,128)(2,1)S(1)}, bf16[768,768]{1,0:T(8,128)(2,1)}, u32[]{:S(2)}) copy-start(bf16[768,768]{1,0:T(8,128)(2,1)} %a.3) | copy-start | bytes 3538948
  2.0 14.8 %all-to-all-start = ((bf16[16,8,1536]{2,1,0:T(8,128)(2,1)}), bf16[16,8,1536]{2,1,0:T(8,128)(2,1)S(1)}, u32[]{:S(2)}, u32[]{:S(2)}) async-start(bf16[16,8,1536]{2,1,0:T(8,128)(2,1)} %bitcast.35), calls=%async_computation | async-start | bytes 786432 | tf_op jit(solution)/shard_map/all_to_all | solution.py:196
  9.3 31.9 %collective-permute-start.8 = (bf16[768,768]{1,0:T(8,128)(2,1)}, bf16[768,768]{1,0:T(8,128)(2,1)S(1)}, u32[]{:S(2)}, u32[]{:S(2)}) collective-permute-start(bf16[768,768]{1,0:T(8,128)(2,1)} %a.2), channel_id=1, source_target_pairs={{0,16},{16,0},{1,17},{17,1},{2,18},{18,2},{3,19},{19,3},{4,20},{20... | collective-permute-start | bytes 3538952 | tf_op jit(solution)/shard_map/ppermute | solution.py:30
  9.3 35.1 %collective-permute-start.9 = (bf16[768,768]{1,0:T(8,128)(2,1)}, bf16[768,768]{1,0:T(8,128)(2,1)}, u32[]{:S(2)}, u32[]{:S(2)}) collective-permute-start(bf16[768,768]{1,0:T(8,128)(2,1)} %c.1), channel_id=1, source_target_pairs={{0,16},{16,0},{1,17},{17,1},{2,18},{18,2},{3,19},{19,3},{4,20},{20... | collective-permute-start | bytes 3538952 | tf_op jit(solution)/shard_map/ppermute | solution.py:30
  16.9 9.7 %collective-permute-start.2 = (bf16[128,1536]{1,0:T(8,128)(2,1)S(1)}, bf16[128,1536]{1,0:T(8,128)(2,1)S(1)}, u32[]{:S(2)}, u32[]{:S(2)}) collective-permute-start(bf16[128,1536]{1,0:T(8,128)(2,1)S(1)} %bitcast.30), channel_id=1, source_target_pairs={{0,1},{1,2},{2,3},{3,4},{4,5},{5,6},{6,7},{7,0},{8,9},{9,10},{10,1... | collective-permute-start | bytes 1179656 | tf_op jit(solution)/shard_map/ppermute | solution.py:26
  18.8 9.7 %collective-permute-start = (bf16[128,1536]{1,0:T(8,128)(2,1)S(1)}, bf16[128,1536]{1,0:T(8,128)(2,1)S(1)}, u32[]{:S(2)}, u32[]{:S(2)}) collective-permute-start(bf16[128,1536]{1,0:T(8,128)(2,1)S(1)} %bitcast.31), channel_id=1, source_target_pairs={{0,7},{1,0},{2,1},{3,2},{4,3},{5,4},{6,5},{7,6},{8,15},{9,8},{10,9... | collective-permute-start | bytes 1179656 | tf_op jit(solution)/shard_map/ppermute | solution.py:26
  19.0 39.4 %collective-permute-start.10 = (bf16[768,768]{1,0:T(8,128)(2,1)S(1)}, bf16[768,768]{1,0:T(8,128)(2,1)S(1)}, u32[]{:S(2)}, u32[]{:S(2)}) collective-permute-start(bf16[768,768]{1,0:T(8,128)(2,1)S(1)} %shard_map.58), channel_id=1, source_target_pairs={{0,8},{8,0},{1,9},{9,1},{2,10},{10,2},{3,11},{11,3},{4,12},{12,4},... | collective-permute-start | bytes 3538952 | tf_op jit(solution)/shard_map/ppermute | solution.py:34
  26.6 11.6 %collective-permute-start.3 = (bf16[128,1536]{1,0:T(8,128)(2,1)S(1)}, bf16[128,1536]{1,0:T(8,128)(2,1)S(1)}, u32[]{:S(2)}, u32[]{:S(2)}) collective-permute-start(bf16[128,1536]{1,0:T(8,128)(2,1)S(1)} %collective-permute-done.2.refs_1_), channel_id=1, source_target_pairs={{0,1},{1,2},{2,3},{3,4},{4,5},{5,6},{6,7},{7,0},{8,9},{9,10},{10,1... | collective-permute-start | bytes 1179656 | tf_op jit(solution)/shard_map/ppermute | solution.py:26
  28.5 10.1 %collective-permute-start.1 = (bf16[128,1536]{1,0:T(8,128)(2,1)S(1)}, bf16[128,1536]{1,0:T(8,128)(2,1)S(1)}, u32[]{:S(2)}, u32[]{:S(2)}) collective-permute-start(bf16[128,1536]{1,0:T(8,128)(2,1)S(1)} %collective-permute-done.refs_2_), channel_id=1, source_target_pairs={{0,7},{1,0},{2,1},{3,2},{4,3},{5,4},{6,5},{7,6},{8,15},{9,8},{10,9... | collective-permute-start | bytes 1179656 | tf_op jit(solution)/shard_map/ppermute | solution.py:26
  38.2 20.2 %collective-permute-start.4 = (bf16[128,1536]{1,0:T(8,128)(2,1)S(1)}, bf16[128,1536]{1,0:T(8,128)(2,1)S(1)}, u32[]{:S(2)}, u32[]{:S(2)}) collective-permute-start(bf16[128,1536]{1,0:T(8,128)(2,1)S(1)} %collective-permute-done.3.refs_3_), channel_id=1, source_target_pairs={{0,1},{1,2},{2,3},{3,4},{4,5},{5,6},{6,7},{7,0},{8,9},{9,10},{10,1... | collective-permute-start | bytes 1179656 | tf_op jit(solution)/shard_map/ppermute | solution.py:26
  38.6 19.8 %collective-permute-start.5 = (bf16[128,1536]{1,0:T(8,128)(2,1)S(1)}, bf16[128,1536]{1,0:T(8,128)(2,1)S(1)}, u32[]{:S(2)}, u32[]{:S(2)}) collective-permute-start(bf16[128,1536]{1,0:T(8,128)(2,1)S(1)} %collective-permute-done.1.refs_0_), channel_id=1, source_target_pairs={{0,7},{1,0},{2,1},{3,2},{4,3},{5,4},{6,5},{7,6},{8,15},{9,8},{10,9... | collective-permute-start | bytes 1179656 | tf_op jit(solution)/shard_map/ppermute | solution.py:26
  41.2 4.2 %copy-start.7 = (bf16[768,768]{1,0:T(8,128)(2,1)}, bf16[768,768]{1,0:T(8,128)(2,1)S(1)}, u32[]{:S(2)}) copy-start(bf16[768,768]{1,0:T(8,128)(2,1)S(1)} %collective-permute-done.8.b) | copy-start | bytes 3538948
  41.2 17.2 %collective-permute-start.6 = (bf16[64,1536]{1,0:T(8,128)(2,1)S(1)}, bf16[64,1536]{1,0:T(8,128)(2,1)S(1)}, u32[]{:S(2)}, u32[]{:S(2)}) collective-permute-start(bf16[64,1536]{1,0:T(8,128)(2,1)S(1)} %slice.28), channel_id=1, source_target_pairs={{0,2},{1,3},{2,4},{3,5},{4,6},{5,7},{6,0},{7,1},{8,10},{9,11},{10,... | collective-permute-start | bytes 589832 | tf_op jit(solution)/shard_map/ppermute | solution.py:26
  44.4 14.0 %collective-permute-start.7 = (bf16[64,1536]{1,0:T(8,128)(2,1)S(1)}, bf16[64,1536]{1,0:T(8,128)(2,1)S(1)}, u32[]{:S(2)}, u32[]{:S(2)}) collective-permute-start(bf16[64,1536]{1,0:T(8,128)(2,1)S(1)} %slice.29), channel_id=1, source_target_pairs={{0,6},{1,7},{2,0},{3,1},{4,2},{5,3},{6,4},{7,5},{8,14},{9,15},{10,... | collective-permute-start | bytes 589832 | tf_op jit(solution)/shard_map/ppermute | solution.py:26
  58.4 3.9 %copy-start.1 = (bf16[768,768]{1,0:T(8,128)(2,1)}, bf16[768,768]{1,0:T(8,128)(2,1)S(1)}, u32[]{:S(2)}) copy-start(bf16[768,768]{1,0:T(8,128)(2,1)S(1)} %collective-permute-done.10.refs_7_.array) | copy-start | bytes 3538948
  101.2 7.1 %copy-start = (bf16[8,128,1536]{2,1,0:T(8,128)(2,1)S(1)}, bf16[8,128,1536]{2,1,0:T(8,128)(2,1)}, u32[]{:S(2)}) copy-start(bf16[8,128,1536]{2,1,0:T(8,128)(2,1)} %shard_map.59.dependency) | copy-start | bytes 9437188
  101.2 23.2 %all-to-all-start.2 = ((bf16[16,64,768]{2,1,0:T(8,128)(2,1)}), bf16[16,64,768]{2,1,0:T(8,128)(2,1)}, u32[]{:S(2)}, u32[]{:S(2)}) async-start(bf16[16,64,768]{2,1,0:T(8,128)(2,1)} %bitcast.34), calls=%async_computation.2 | async-start | bytes 3145728 | tf_op jit(solution)/shard_map/all_to_all | solution.py:222
  108.3 3.2 %collective-permute-start.11 = (bf16[768,768]{1,0:T(8,128)(2,1)}, bf16[768,768]{1,0:T(8,128)(2,1)}, u32[]{:S(2)}, u32[]{:S(2)}) collective-permute-start(bf16[768,768]{1,0:T(8,128)(2,1)} %a.3), channel_id=1, source_target_pairs={{0,16},{16,0},{1,17},{17,1},{2,18},{18,2},{3,19},{19,3},{4,20},{20... | collective-permute-start | bytes 3538952 | tf_op jit(solution)/shard_map/ppermute | solution.py:30
  108.4 1.3 copy-start.2
  109.6 1.0 copy-start.3
  110.7 3.2 %collective-permute-start.12 = (bf16[768,768]{1,0:T(8,128)(2,1)}, bf16[768,768]{1,0:T(8,128)(2,1)S(1)}, u32[]{:S(2)}, u32[]{:S(2)}) collective-permute-start(bf16[768,768]{1,0:T(8,128)(2,1)} %copy-done.3), channel_id=1, source_target_pairs={{0,16},{16,0},{1,17},{17,1},{2,18},{18,2},{3,19},{19,3},{4,20},{20... | collective-permute-start | bytes 3538952 | tf_op jit(solution)/shard_map/ppermute | solution.py:30
  113.8 1.1 copy-start.8
  118.2 2.1 %copy-start.4 = (bf16[2,1536,768]{2,1,0:T(8,128)(2,1)}, bf16[2,1536,768]{2,1,0:T(8,128)(2,1)S(1)}, u32[]{:S(2)}) copy-start(bf16[2,1536,768]{2,1,0:T(8,128)(2,1)S(1)} %shard_map.61.weight) | copy-start | bytes 14155780
  124.4 2.3 %copy-start.5 = (bf16[2,1536,768]{2,1,0:T(8,128)(2,1)S(1)}, bf16[2,1536,768]{2,1,0:T(8,128)(2,1)}, u32[]{:S(2)}) copy-start(bf16[2,1536,768]{2,1,0:T(8,128)(2,1)} %copy-done.4) | copy-start | bytes 14155780
  131.0 14.3 %collective-permute-start.13 = (bf16[2,2,64,768]{3,2,1,0:T(8,128)(2,1)S(1)}, bf16[2,2,64,768]{3,2,1,0:T(8,128)(2,1)S(1)}, u32[]{:S(2)}, u32[]{:S(2)}) collective-permute-start(bf16[2,2,64,768]{3,2,1,0:T(8,128)(2,1)S(1)} %get-tuple-element.13), channel_id=1, source_target_pairs={{0,7},{1,0},{2,1},{3,2},{4,3},{5,4},{6,5},{7,6},{8,15},{9,8},{10,9... | collective-permute-start | bytes 1179656 | tf_op jit(solution)/shard_map/ppermute | solution.py:26
  131.1 14.2 %collective-permute-start.14 = (bf16[2,2,64,768]{3,2,1,0:T(8,128)(2,1)S(1)}, bf16[2,2,64,768]{3,2,1,0:T(8,128)(2,1)S(1)}, u32[]{:S(2)}, u32[]{:S(2)}) collective-permute-start(bf16[2,2,64,768]{3,2,1,0:T(8,128)(2,1)S(1)} %get-tuple-element.14), channel_id=1, source_target_pairs={{0,1},{1,2},{2,3},{3,4},{4,5},{5,6},{6,7},{7,0},{8,9},{9,10},{10,1... | collective-permute-start | bytes 1179656 | tf_op jit(solution)/shard_map/ppermute | solution.py:26
  133.1 12.2 %collective-permute-start.15 = (bf16[64,768]{1,0:T(8,128)(2,1)S(1)}, bf16[64,768]{1,0:T(8,128)(2,1)S(1)}, u32[]{:S(2)}, u32[]{:S(2)}) collective-permute-start(bf16[64,768]{1,0:T(8,128)(2,1)S(1)} %get-tuple-element.15), channel_id=1, source_target_pairs={{0,6},{1,7},{2,0},{3,1},{4,2},{5,3},{6,4},{7,5},{8,14},{9,15},{10,... | collective-permute-start | bytes 294920 | tf_op jit(solution)/shard_map/ppermute | solution.py:26
  134.5 10.9 %collective-permute-start.16 = (bf16[64,768]{1,0:T(8,128)(2,1)S(1)}, bf16[64,768]{1,0:T(8,128)(2,1)S(1)}, u32[]{:S(2)}, u32[]{:S(2)}) collective-permute-start(bf16[64,768]{1,0:T(8,128)(2,1)S(1)} %get-tuple-element.16), channel_id=1, source_target_pairs={{0,2},{1,3},{2,4},{3,5},{4,6},{5,7},{6,0},{7,1},{8,10},{9,11},{10,... | collective-permute-start | bytes 294920 | tf_op jit(solution)/shard_map/ppermute | solution.py:26
  145.5 23.7 %copy-start.9 = (bf16[8,12288]{1,0:T(8,128)(2,1)S(1)}, bf16[8,12288]{1,0:T(8,128)(2,1)}, u32[]{:S(2)}) copy-start(bf16[8,12288]{1,0:T(8,128)(2,1)} %tokens.1) | copy-start | bytes 589828
  145.5 7.3 %collective-permute-start.17 = (bf16[2,64,768]{2,1,0:T(8,128)(2,1)S(1)}, bf16[2,64,768]{2,1,0:T(8,128)(2,1)S(1)}, u32[]{:S(2)}, u32[]{:S(2)}) collective-permute-start(bf16[2,64,768]{2,1,0:T(8,128)(2,1)S(1)} %get-tuple-element.17), channel_id=1, source_target_pairs={{0,6},{1,7},{2,0},{3,1},{4,2},{5,3},{6,4},{7,5},{8,14},{9,15},{10,... | collective-permute-start | bytes 589832 | tf_op jit(solution)/shard_map/ppermute | solution.py:26
  146.2 8.5 %collective-permute-start.18 = (bf16[2,64,768]{2,1,0:T(8,128)(2,1)S(1)}, bf16[2,64,768]{2,1,0:T(8,128)(2,1)S(1)}, u32[]{:S(2)}, u32[]{:S(2)}) collective-permute-start(bf16[2,64,768]{2,1,0:T(8,128)(2,1)S(1)} %get-tuple-element.18), channel_id=1, source_target_pairs={{0,2},{1,3},{2,4},{3,5},{4,6},{5,7},{6,0},{7,1},{8,10},{9,11},{10,... | collective-permute-start | bytes 589832 | tf_op jit(solution)/shard_map/ppermute | solution.py:26
  155.4 13.7 %all-to-all-start.3 = ((bf16[8,16,768]{2,1,0:T(8,128)(2,1)}), bf16[8,16,768]{2,1,0:T(8,128)(2,1)S(1)}, u32[]{:S(2)}, u32[]{:S(2)}) async-start(bf16[8,16,768]{2,1,0:T(8,128)(2,1)} %copy_bitcast_fusion), calls=%async_computation.3 | async-start | bytes 393216 | tf_op jit(solution)/shard_map/all_to_all | solution.py:232

commit v4 on v3

--- a/solution.py
+++ b/solution.py
@@ -63,7 +63,9 @@
                 panel[first_row // 16 + j, s] = piece[16 * j : 16 * (j + 1)]
 
     total = product(panel[...].reshape(512, 2 * unit), weight[0])
-    out[...] = total.astype(bf16).reshape(8, 64, unit)
+    total = total.reshape(8, 4, 2, 8, unit)
+    for y in range(2):
+        out[:, y] = total[:, :, y].reshape(8, 32, unit).astype(bf16)
 
 
 def first_product(rows, pieces, weight, *beside):
@@ -74,8 +76,8 @@
         in_specs=[pl.BlockSpec(piece.shape, lambda i: (0, 0)) for piece in pieces]
         + [pl.BlockSpec((1, 2 * unit, unit), lambda i: (i, 0, 0))]
         + [anywhere] * len(beside),
-        out_specs=pl.BlockSpec((8, 64, unit), lambda i: (0, half, i)),
-        out_shape=pltpu.HBM((8, 128, 2 * unit), bf16),
+        out_specs=pl.BlockSpec((8, 2, 32, unit), lambda i: (0, 0, half, i)),
+        out_shape=pltpu.HBM((8, 2, 64, 2 * unit), bf16),
         input_output_aliases={len(rows) + 1: 0} if half else {},
         scratch_shapes=[pltpu.VMEM((8, 4, 16, 2 * unit), bf16)],
         compiler_params=pltpu.CompilerParams(vmem_limit_bytes=room),
@@ -89,13 +91,13 @@
     out[0, :unit], out[0, unit:], out[1, :unit], out[1, unit:] = a[...], b[...], c[...], d[...]
 
 
-def stack(*weights):
+def stack(shape, *weights):
     return pl.pallas_call(
         stack_kernel,
         grid=(3,),
         in_specs=[pl.BlockSpec((unit, tile), lambda j: (0, j))] * 4,
         out_specs=pl.BlockSpec((2, 2 * unit, tile), lambda j: (0, 0, j)),
-        out_shape=jax.ShapeDtypeStruct((2, 2 * unit, unit), bf16),
+        out_shape=shape((2, 2 * unit, unit), bf16),
         compiler_params=pltpu.CompilerParams(vmem_limit_bytes=8 * 2**20),
     )(*(in_hbm(weight) for weight in weights))
 
@@ -103,9 +105,9 @@
 order = (0, 1, 7, 2, 6, 3, 5, 4)
 
 
-def second_kernel(_, mine, theirs, weight, near, left, right, left_half, right_half):
+def second_kernel(_, mine, theirs, weight, near, left, right, p1, p7, left_half, right_half):
     places = {0: near.at[0], 2: near.at[1], 6: near.at[2]}
-    places |= {1: left.at[0], 3: left.at[1], 7: right.at[0], 5: right.at[1]}
+    places |= {3: left.at[0], 5: right.at[0], 1: p1.at[0], 7: p7.at[0]}
     total = product(mine[...].reshape(512, unit), weight[0, :unit])
     total += product(theirs[...].reshape(512, unit), weight[0, unit:])
     total = total.reshape(8, 8, 8, unit)
@@ -122,7 +124,7 @@
 
 
 def second_product(yh, hidden, weight):
-    counts = (3, 2, 2)
+    counts = (3, 1, 1, 1, 1)
     return pl.pallas_call(
         second_kernel,
         grid_spec=pltpu.PrefetchScalarGridSpec(
@@ -142,13 +144,13 @@
         cost_estimate=pl.CostEstimate(
             flops=512 * 8 * unit * unit, bytes_accessed=8 * unit * unit, transcendentals=0
         ),
-    )(yh.reshape(1), hidden, hidden, weight)
+    )(yh.reshape(1), hidden, hidden, in_hbm(weight))
 
 
 def relay_kernel(near, left, right, left_half, right_half, to_left, to_right):
     for n in range(2):
-        a = near[1, n].astype(f32) + left[1, n].astype(f32)
-        b = near[2, n].astype(f32) + right[1, n].astype(f32)
+        a = near[1, n].astype(f32) + left[0, n].astype(f32)
+        b = near[2, n].astype(f32) + right[0, n].astype(f32)
         if n == 0:
             a += left_half[...].astype(f32)
         else:
@@ -201,31 +203,31 @@
     r3, l3 = shift(r2, 1), shift(l2, -1)
     r4, l4 = shift(r2[:64], 2), shift(l2[64:], -2)
 
-    first = stack(
-        gate_weight, core_partner(gate_weight), up_weight, core_partner(up_weight)
-    )
+    first = (gate_weight, core_partner(gate_weight), up_weight, core_partner(up_weight))
+    first = stack(jax.ShapeDtypeStruct, *first)
     down_y = yh_partner(after(block, down_weight))
     whole = [(s, 0) for s in range(4)]
     partial = first_product(whole, (block, r1, l1, r2), first)
     far = [(0, 0), (1, 0), (2, 0), (3, 0), (3, 64)]
     partial = first_product(far, (l2, r3, l3, r4, l4), first, partial, down_y)
-    terms = lax.all_to_all(partial, ("yl", "x"), 0, 0)
-
-    down_y = after(partial, down_y)
-    second = stack(down_weight, down_y, core_partner(down_weight), core_partner(down_y))
-
-    summed = jnp.sum(terms.astype(f32), axis=0)
-    hidden = (jax.nn.silu(summed[:, :unit]) * summed[:, unit:]).astype(bf16)
-
-    hidden = hidden.reshape(8, 2, 8, unit).transpose(1, 0, 2, 3)[None]
-    hidden = jnp.broadcast_to(hidden, (8, 2, 8, 8, unit)).reshape(16, 64, unit)
-    hidden = lax.all_to_all(hidden, ("yl", "x", "yh"), 0, 0).reshape(8, 2, 64, unit)
-
-    mine, left, right, left_half, right_half = second_product(yh, hidden, second)
+    terms = lax.all_to_all(partial.reshape(16, 64, 2 * unit), ("yl", "x", "yh"), 0, 0)
+
+    down_y = after(in_hbm(partial), down_y)
+    second = (down_weight, down_y, core_partner(down_weight), core_partner(down_y))
+    second = stack(pltpu.HBM, *second)
+
+    summed = jnp.sum(terms.reshape(8, 2, 64, 2 * unit).astype(f32), axis=0)
+    hidden = (jax.nn.silu(summed[:, :, :unit]) * summed[:, :, unit:]).astype(bf16)
+
+    hidden = jnp.broadcast_to(hidden[None], (8, 2, 64, unit))
+    hidden = lax.all_to_all(hidden, ("yl", "x"), 0, 0)
+
+    mine, left, right, p1, p7, left_half, right_half = second_product(yh, hidden, second)
+    left_half, right_half = shift(left_half, -2), shift(right_half, 2)
     left, right = shift(left, -1), shift(right, 1)
-    left_half, right_half = shift(left_half, -2), shift(right_half, 2)
+    p1, p7 = shift(p1, -1), shift(p7, 1)
     to_left, to_right = relay(mine, left, right, left_half, right_half)
-    terms = (mine[0], left[0], right[0], shift(to_left, -2), shift(to_right, 2))
+    terms = (mine[0], p1[0], p7[0], shift(to_left, -2), shift(to_right, 2))
     branch = sum(term.astype(f32) for term in terms).astype(bf16)
 
     branch = branch.reshape(2, 8, 8, unit).transpose(1, 0, 2, 3)

time: 172 us -> 167 us (0.971)
  local copies, waits for them, and re-layouts: 9.27 us -> 1.48 us
  waiting for transfers between devices: 54.7 us -> 58.4 us
  starting transfers between devices: 45.9 us -> 42.3 us
  Pallas kernels: 20.7 us -> 23.1 us
  blocking collectives: 37.1 us -> 38.9 us
    unnamed x21 -> x9, local copies, waits for them, and re-layouts: 7.92 us -> 0.1 us
    all_to_all x1, starting transfers between devices: 7.11 us -> 3.64 us  [on_device(): hidden = lax.all_to_all(hidden, ('yl', 'x'), 0, 0)]
    all_to_all x1, starting transfers between devices: 6.81 us -> 3.39 us  [on_device(): branch = lax.all_to_all(branch.reshape(8, 16, unit), ('yl', 'x'), 0, 0)]
    ppermute x14 -> x16, starting transfers between devices: 21 us -> 24 us  [shift(): return lax.ppermute(block, 'z', [(i, (i + steps) % 8) for i in range(8)])]
    pallas_call x2, Pallas kernels: 6.5 us -> 8.67 us  [stack(): pl.pallas_call(stack_kernel, grid=(3,), in_specs=[pl.BlockSpec((unit, til...]
    all_to_all x1, blocking collectives: 37.1 us -> 38.9 us  [on_device(): lax.all_to_all(partial.reshape(16, 64, 2 * unit), ('yl', 'x', 'yh'), 0, 0)]
    ppermute x14 -> x16, waiting for transfers between devices: 33.9 us -> 35.3 us  [shift(): return lax.ppermute(block, 'z', [(i, (i + steps) % 8) for i in range(8)])]
  transfers between devices with their start and end apart: 22 -> 24, of which waited for: 12 -> 14; matrix products, arithmetic and copies ran while one was open for 0% -> 0% of each run, Pallas kernels for 6% -> 8%
where the time goes in v4:
time: 167 us
  waiting for transfers between devices  58.4 us (35%)
  starting transfers between devices  42.3 us (25%)
  blocking collectives  38.9 us (23%)
  Pallas kernels  23.1 us (14%)
  other arithmetic  2.13 us (1%)
    all_to_all x1, blocking collectives, on_device(): lax.all_to_all(partial.reshape(16, 64, 2 * unit), ('yl', 'x', 'yh'), 0, 0)  38.9 us
    ppermute x16, waiting for transfers between devices, shift(): return lax.ppermute(block, 'z', [(i, (i + steps) % 8) for i in range(8)])  35.3 us
    ppermute x16, starting transfers between devices, shift(): return lax.ppermute(block, 'z', [(i, (i + steps) % 8) for i in range(8)])  24 us
    pallas_call x2, Pallas kernels, stack(): pl.pallas_call(stack_kernel, grid=(3,), in_specs=[pl.BlockSpec((unit, til...  8.67 us
    pallas_call x2, Pallas kernels, first_product(): pl.pallas_call(lambda *refs: first_kernel(rows, *refs), grid=(2,), in_spe...  7.71 us
    all_to_all x1, starting transfers between devices, on_device(): lax.all_to_all(pieces.reshape(16, 8, 2 * unit), ('yl', 'x', 'yh'), 0, 0)  7.28 us
    all_to_all x1, waiting for transfers between devices, on_device(): lax.all_to_all(pieces.reshape(16, 8, 2 * unit), ('yl', 'x', 'yh'), 0, 0)  7.05 us
    all_to_all x1, waiting for transfers between devices, on_device(): branch = lax.all_to_all(branch.reshape(8, 16, unit), ('yl', 'x'), 0, 0)  6.87 us
  transfers between devices with their start and end apart: 24, of which 14 were waited for; matrix products, arithmetic and copies ran while one was open for 0% of the time, Pallas kernels for 8%

profile of v4, /device:TPU:48, one launch (start us, length us, event | category | flops | bytes accessed | tf_op | source)
XLA Modules:
  0.0 166.6 jit_solution(12299532090799884259)
XLA Ops:
  0.0 2.1 %shard_map.55 = bf16[8,2,8,1536]{3,2,1,0:T(8,128)(2,1)} custom-call(s32[1]{0:T(128)} %bitcast.1.core, bf16[8,12288]{1,0:T(8,128)(2,1)} %tokens.1, f32[1,12288]{1,0:T(1,128)} %bitcast.37), custom_call_target="tpu_custom_call" | custom-call | tf_op jit(solution)/shard_map/pallas_call | solution.py:185
  2.1 7.3 %all-to-all-start = ((bf16[16,8,1536]{2,1,0:T(8,128)(2,1)}), bf16[16,8,1536]{2,1,0:T(8,128)(2,1)S(1)}, u32[]{:S(2)}, u32[]{:S(2)}) async-start(bf16[16,8,1536]{2,1,0:T(8,128)(2,1)} %bitcast.34), calls=%async_computation | async-start | bytes 786432 | tf_op jit(solution)/shard_map/all_to_all | solution.py:198
  9.3 0.5 collective-permute-start.9
  9.8 7.1 %all-to-all-done = bf16[16,8,1536]{2,1,0:T(8,128)(2,1)S(1)} async-done(((bf16[16,8,1536]{2,1,0:T(8,128)(2,1)}), bf16[16,8,1536]{2,1,0:T(8,128)(2,1)S(1)}, u32[]{:S(2)}, u32[]{:S(2)}) %all-to-all-start) | async-done | bytes 393248 | tf_op jit(solution)/shard_map/all_to_all | solution.py:198
  16.9 1.9 %collective-permute-start.2 = (bf16[128,1536]{1,0:T(8,128)(2,1)S(1)}, bf16[128,1536]{1,0:T(8,128)(2,1)S(1)}, u32[]{:S(2)}, u32[]{:S(2)}) collective-permute-start(bf16[128,1536]{1,0:T(8,128)(2,1)S(1)} %bitcast.28), channel_id=1, source_target_pairs={{0,1},{1,2},{2,3},{3,4},{4,5},{5,6},{6,7},{7,0},{8,9},{9,10},{10,1... | collective-permute-start | bytes 1179656 | tf_op jit(solution)/shard_map/ppermute | solution.py:26
  18.8 0.1 collective-permute-start
  18.9 0.1 copy.11.array
  19.0 2.7 %collective-permute-start.10 = (bf16[768,768]{1,0:T(8,128)(2,1)S(1)}, bf16[768,768]{1,0:T(8,128)(2,1)S(1)}, u32[]{:S(2)}, u32[]{:S(2)}) collective-permute-start(bf16[768,768]{1,0:T(8,128)(2,1)S(1)} %shard_map.58), channel_id=1, source_target_pairs={{0,8},{8,0},{1,9},{9,1},{2,10},{10,2},{3,11},{11,3},{4,12},{12,4},... | collective-permute-start | bytes 3538952 | tf_op jit(solution)/shard_map/ppermute | solution.py:34
  21.8 4.9 %collective-permute-done.2.refs_1_ = bf16[128,1536]{1,0:T(8,128)(2,1)S(1)} collective-permute-done((bf16[128,1536]{1,0:T(8,128)(2,1)S(1)}, bf16[128,1536]{1,0:T(8,128)(2,1)S(1)}, u32[]{:S(2)}, u32[]{:S(2)}) %collective-permute-start.2) | collective-permute-done | bytes 393248 | tf_op jit(solution)/shard_map/ppermute | solution.py:26
  26.6 1.9 %collective-permute-start.3 = (bf16[128,1536]{1,0:T(8,128)(2,1)S(1)}, bf16[128,1536]{1,0:T(8,128)(2,1)S(1)}, u32[]{:S(2)}, u32[]{:S(2)}) collective-permute-start(bf16[128,1536]{1,0:T(8,128)(2,1)S(1)} %collective-permute-done.2.refs_1_), channel_id=1, source_target_pairs={{0,1},{1,2},{2,3},{3,4},{4,5},{5,6},{6,7},{7,0},{8,9},{9,10},{10,1... | collective-permute-start | bytes 1179656 | tf_op jit(solution)/shard_map/ppermute | solution.py:26
  28.5 2.3 %collective-permute-start.1 = (bf16[128,1536]{1,0:T(8,128)(2,1)S(1)}, bf16[128,1536]{1,0:T(8,128)(2,1)S(1)}, u32[]{:S(2)}, u32[]{:S(2)}) collective-permute-start(bf16[128,1536]{1,0:T(8,128)(2,1)S(1)} %collective-permute-done.refs_2_), channel_id=1, source_target_pairs={{0,7},{1,0},{2,1},{3,2},{4,3},{5,4},{6,5},{7,6},{8,15},{9,8},{10,9... | collective-permute-start | bytes 1179656 | tf_op jit(solution)/shard_map/ppermute | solution.py:26
  30.9 7.3 %collective-permute-done.3.refs_3_ = bf16[128,1536]{1,0:T(8,128)(2,1)S(1)} collective-permute-done((bf16[128,1536]{1,0:T(8,128)(2,1)S(1)}, bf16[128,1536]{1,0:T(8,128)(2,1)S(1)}, u32[]{:S(2)}, u32[]{:S(2)}) %collective-permute-start.3) | collective-permute-done | bytes 393248 | tf_op jit(solution)/shard_map/ppermute | solution.py:26
  38.2 0.4 collective-permute-done.1.refs_0_
  38.6 2.5 %collective-permute-start.5 = (bf16[128,1536]{1,0:T(8,128)(2,1)S(1)}, bf16[128,1536]{1,0:T(8,128)(2,1)S(1)}, u32[]{:S(2)}, u32[]{:S(2)}) collective-permute-start(bf16[128,1536]{1,0:T(8,128)(2,1)S(1)} %collective-permute-done.1.refs_0_), channel_id=1, source_target_pairs={{0,7},{1,0},{2,1},{3,2},{4,3},{5,4},{6,5},{7,6},{8,15},{9,8},{10,9... | collective-permute-start | bytes 1179656 | tf_op jit(solution)/shard_map/ppermute | solution.py:26
  41.2 3.2 %collective-permute-start.6 = (bf16[64,1536]{1,0:T(8,128)(2,1)S(1)}, bf16[64,1536]{1,0:T(8,128)(2,1)S(1)}, u32[]{:S(2)}, u32[]{:S(2)}) collective-permute-start(bf16[64,1536]{1,0:T(8,128)(2,1)S(1)} %slice.20), channel_id=1, source_target_pairs={{0,2},{1,3},{2,4},{3,5},{4,6},{5,7},{6,0},{7,1},{8,10},{9,11},{10,... | collective-permute-start | bytes 589832 | tf_op jit(solution)/shard_map/ppermute | solution.py:26
  44.4 1.0 collective-permute-start.7
  45.4 3.2 %shard_map.56.refs_4_.refs_5_ = bf16[2,1536,768]{2,1,0:T(8,128)(2,1)S(1)} custom-call(bf16[768,768]{1,0:T(8,128)(2,1)} %a.2, bf16[768,768]{1,0:T(8,128)(2,1)} %copy-done.2, bf16[768,768]{1,0:T(8,128)(2,1)} %c.1, bf16[768,768]{1,0:T(8,128)(2,1)} %collective-permute-done.9.d), custom_call_target="tpu_custom_call" | custom-call | tf_op jit(solution)/shard_map/pallas_call | solution.py:95
  48.7 3.8 %shard_map.57.refs_6_ = bf16[8,2,64,1536]{3,2,1,0:T(8,128)(2,1)} custom-call(bf16[128,1536]{1,0:T(8,128)(2,1)S(1)} %bitcast.31, bf16[128,1536]{1,0:T(8,128)(2,1)S(1)} %collective-permute-done.2.refs_1_, bf16[128,1536]{1,0:T(8,128)(2,1)S(1)} %collective-permute-done.refs_2_, bf16[128,1536]{1,0:T(8,128)(2,1)S(1)} %collective-permute-done.3.refs_3_, ...), custom_call_target="tpu_custom_call" | custom-call | flops 2415919104 | bytes 4718592 | tf_op jit(solution)/shard_map/pallas_call | solution.py:73
  52.5 5.9 %collective-permute-done.6.refs_3_ = bf16[64,1536]{1,0:T(8,128)(2,1)S(1)} collective-permute-done((bf16[64,1536]{1,0:T(8,128)(2,1)S(1)}, bf16[64,1536]{1,0:T(8,128)(2,1)S(1)}, u32[]{:S(2)}, u32[]{:S(2)}) %collective-permute-start.6) | collective-permute-done | bytes 196640 | tf_op jit(solution)/shard_map/ppermute | solution.py:26
  58.4 3.9 %shard_map.59.dependency = bf16[8,2,64,1536]{3,2,1,0:T(8,128)(2,1)} custom-call(bf16[128,1536]{1,0:T(8,128)(2,1)S(1)} %collective-permute-done.1.refs_0_, bf16[128,1536]{1,0:T(8,128)(2,1)S(1)} %collective-permute-done.4.refs_1_, bf16[128,1536]{1,0:T(8,128)(2,1)S(1)} %collective-permute-done.5.refs_2_, ...), custom_call_target="tpu_custom_call", output_to_operand_aliasing={{}: (6, {})} | custom-call | flops 2415919104 | bytes 4718592 | tf_op jit(solution)/shard_map/pallas_call | solution.py:73
  62.3 38.9 %all_to_all.20 = bf16[16,64,1536]{2,1,0:T(8,128)(2,1)S(1)} all-to-all(bf16[16,64,1536]{2,1,0:T(8,128)(2,1)} %bitcast.32), channel_id=1, replica_groups=mesh['yl'=2,'x'=4,'c'=2,'yh'=2,'z'=8] {'yl','x','yh'}, dimensions={0} | all-to-all | bytes 6291456 | tf_op jit(solution)/shard_map/all_to_all | solution.py:213
  101.2 0.5 convert_reduce_fusion
  101.7 0.1 fusion
  101.8 1.4 broadcast_in_dim.2
  103.2 3.6 %all-to-all-start.2 = ((bf16[8,2,64,768]{3,2,1,0:T(8,128)(2,1)}), bf16[8,2,64,768]{3,2,1,0:T(8,128)(2,1)S(1)}, u32[]{:S(2)}, u32[]{:S(2)}) async-start(bf16[8,2,64,768]{3,2,1,0:T(8,128)(2,1)} %broadcast_in_dim.2), calls=%async_computation.2 | async-start | bytes 3145728 | tf_op jit(solution)/shard_map/all_to_all | solution.py:223
  106.8 0.2 collective-permute-start.11
  107.1 0.5 collective-permute-start.12
  107.6 3.1 %collective-permute-done.11.c = bf16[768,768]{1,0:T(8,128)(2,1)} collective-permute-done((bf16[768,768]{1,0:T(8,128)(2,1)}, bf16[768,768]{1,0:T(8,128)(2,1)}, u32[]{:S(2)}, u32[]{:S(2)}) %collective-permute-start.11) | collective-permute-done | bytes 1179680 | tf_op jit(solution)/shard_map/ppermute | solution.py:30
  110.7 1.0 collective-permute-done.12.d
  111.7 5.4 %shard_map.61.weight = bf16[2,1536,768]{2,1,0:T(8,128)(2,1)} custom-call(bf16[768,768]{1,0:T(8,128)(2,1)} %a.3, bf16[768,768]{1,0:T(8,128)(2,1)} %copy-done, bf16[768,768]{1,0:T(8,128)(2,1)} %collective-permute-done.11.c, bf16[768,768]{1,0:T(8,128)(2,1)} %collective-permute-done.12.d), custom_call_target="tpu_custom_call" | custom-call | tf_op jit(solution)/shard_map/pallas_call | solution.py:95
  117.1 5.0 %all-to-all-done.2.mine.theirs = bf16[8,2,64,768]{3,2,1,0:T(8,128)(2,1)S(1)} async-done(((bf16[8,2,64,768]{3,2,1,0:T(8,128)(2,1)}), bf16[8,2,64,768]{3,2,1,0:T(8,128)(2,1)S(1)}, u32[]{:S(2)}, u32[]{:S(2)}) %all-to-all-start.2) | async-done | bytes 1572896 | tf_op jit(solution)/shard_map/all_to_all | solution.py:223
  122.2 4.5 %shard_map.62 = (bf16[3,2,64,768]{3,2,1,0:T(8,128)(2,1)S(1)}, bf16[1,2,64,768]{3,2,1,0:T(8,128)(2,1)S(1)}, bf16[1,2,64,768]{3,2,1,0:T(8,128)(2,1)S(1)}, bf16[1,2...) custom-call(s32[1]{0:T(128)} %bitcast._, ...), custom_call_target="tpu_custom_call" | custom-call | flops 2415919104 | bytes 4718592 | tf_op jit(solution)/shard_map/pallas_call | solution.py:128
  126.7 0.1 collective-permute-start.15
  126.8 4.4 %collective-permute-start.16 = (bf16[1,2,64,768]{3,2,1,0:T(8,128)(2,1)S(1)}, bf16[1,2,64,768]{3,2,1,0:T(8,128)(2,1)S(1)}, u32[]{:S(2)}, u32[]{:S(2)}) collective-permute-start(bf16[1,2,64,768]{3,2,1,0:T(8,128)(2,1)S(1)} %get-tuple-element.18), channel_id=1, source_target_pairs={{0,1},{1,2},{2,3},{3,4},{4,5},{5,6},{6,7},{7,0},{8,9},{9,10},{10,1... | collective-permute-start | bytes 589832 | tf_op jit(solution)/shard_map/ppermute | solution.py:26
  131.2 2.9 %collective-permute-start.18 = (bf16[64,768]{1,0:T(8,128)(2,1)S(1)}, bf16[64,768]{1,0:T(8,128)(2,1)S(1)}, u32[]{:S(2)}, u32[]{:S(2)}) collective-permute-start(bf16[64,768]{1,0:T(8,128)(2,1)S(1)} %get-tuple-element.20), channel_id=1, source_target_pairs={{0,2},{1,3},{2,4},{3,5},{4,6},{5,7},{6,0},{7,1},{8,10},{9,11},{10,... | collective-permute-start | bytes 294920 | tf_op jit(solution)/shard_map/ppermute | solution.py:26
  134.1 0.5 collective-permute-start.13
  134.6 7.2 %collective-permute-done.17.left_half = bf16[64,768]{1,0:T(8,128)(2,1)S(1)} collective-permute-done((bf16[64,768]{1,0:T(8,128)(2,1)S(1)}, bf16[64,768]{1,0:T(8,128)(2,1)S(1)}, u32[]{:S(2)}, u32[]{:S(2)}) %collective-permute-start.17) | collective-permute-done | bytes 98336 | tf_op jit(solution)/shard_map/ppermute | solution.py:26
  141.8 0.1 shard_map.63
  141.9 0.0 copy-start.3
  141.9 3.2 %collective-permute-start.19 = (bf16[2,64,768]{2,1,0:T(8,128)(2,1)S(1)}, bf16[2,64,768]{2,1,0:T(8,128)(2,1)S(1)}, u32[]{:S(2)}, u32[]{:S(2)}) collective-permute-start(bf16[2,64,768]{2,1,0:T(8,128)(2,1)S(1)} %get-tuple-element.21), channel_id=1, source_target_pairs={{0,6},{1,7},{2,0},{3,1},{4,2},{5,3},{6,4},{7,5},{8,14},{9,15},{10,... | collective-permute-start | bytes 589832 | tf_op jit(solution)/shard_map/ppermute | solution.py:26
  145.1 1.6 collective-permute-done.13
  146.7 1.8 %collective-permute-done.14 = bf16[1,2,64,768]{3,2,1,0:T(8,128)(2,1)S(1)} collective-permute-done((bf16[1,2,64,768]{3,2,1,0:T(8,128)(2,1)S(1)}, bf16[1,2,64,768]{3,2,1,0:T(8,128)(2,1)S(1)}, u32[]{:S(2)}, u32[]{:S(2)}) %collective-permute-start.14) | collective-permute-done | bytes 196640 | tf_op jit(solution)/shard_map/ppermute | solution.py:26
  148.5 4.3 %collective-permute-done.19 = bf16[2,64,768]{2,1,0:T(8,128)(2,1)S(1)} collective-permute-done((bf16[2,64,768]{2,1,0:T(8,128)(2,1)S(1)}, bf16[2,64,768]{2,1,0:T(8,128)(2,1)S(1)}, u32[]{:S(2)}, u32[]{:S(2)}) %collective-permute-start.19) | collective-permute-done | bytes 196640 | tf_op jit(solution)/shard_map/ppermute | solution.py:26
  152.8 1.9 %collective-permute-done.20 = bf16[2,64,768]{2,1,0:T(8,128)(2,1)S(1)} collective-permute-done((bf16[2,64,768]{2,1,0:T(8,128)(2,1)S(1)}, bf16[2,64,768]{2,1,0:T(8,128)(2,1)S(1)}, u32[]{:S(2)}, u32[]{:S(2)}) %collective-permute-start.20) | collective-permute-done | bytes 196640 | tf_op jit(solution)/shard_map/ppermute | solution.py:26
  154.7 0.8 copy_bitcast_fusion
  155.5 3.4 %all-to-all-start.3 = ((bf16[8,16,768]{2,1,0:T(8,128)(2,1)}), bf16[8,16,768]{2,1,0:T(8,128)(2,1)S(1)}, u32[]{:S(2)}, u32[]{:S(2)}) async-start(bf16[8,16,768]{2,1,0:T(8,128)(2,1)} %copy_bitcast_fusion), calls=%async_computation.3 | async-start | bytes 393216 | tf_op jit(solution)/shard_map/all_to_all | solution.py:234
  158.9 6.9 %all-to-all-done.3 = bf16[8,16,768]{2,1,0:T(8,128)(2,1)S(1)} async-done(((bf16[8,16,768]{2,1,0:T(8,128)(2,1)}), bf16[8,16,768]{2,1,0:T(8,128)(2,1)S(1)}, u32[]{:S(2)}, u32[]{:S(2)}) %all-to-all-start.3) | async-done | bytes 196640 | tf_op jit(solution)/shard_map/all_to_all | solution.py:234
  165.8 0.7 add_convert_fusion
  (27 shorter events, 0.1 us)
Async XLA Ops:
  0.0 18.9 %copy-start.1 = (bf16[768,768]{1,0:T(8,128)(2,1)S(1)}, bf16[768,768]{1,0:T(8,128)(2,1)}, u32[]{:S(2)}) copy-start(bf16[768,768]{1,0:T(8,128)(2,1)} %a.3) | copy-start | bytes 3538948
  2.1 14.8 %all-to-all-start = ((bf16[16,8,1536]{2,1,0:T(8,128)(2,1)}), bf16[16,8,1536]{2,1,0:T(8,128)(2,1)S(1)}, u32[]{:S(2)}, u32[]{:S(2)}) async-start(bf16[16,8,1536]{2,1,0:T(8,128)(2,1)} %bitcast.34), calls=%async_computation | async-start | bytes 786432 | tf_op jit(solution)/shard_map/all_to_all | solution.py:198
  9.3 31.9 %collective-permute-start.8 = (bf16[768,768]{1,0:T(8,128)(2,1)}, bf16[768,768]{1,0:T(8,128)(2,1)S(1)}, u32[]{:S(2)}, u32[]{:S(2)}) collective-permute-start(bf16[768,768]{1,0:T(8,128)(2,1)} %a.2), channel_id=1, source_target_pairs={{0,16},{16,0},{1,17},{17,1},{2,18},{18,2},{3,19},{19,3},{4,20},{20... | collective-permute-start | bytes 3538952 | tf_op jit(solution)/shard_map/ppermute | solution.py:30
  9.3 35.1 %collective-permute-start.9 = (bf16[768,768]{1,0:T(8,128)(2,1)}, bf16[768,768]{1,0:T(8,128)(2,1)}, u32[]{:S(2)}, u32[]{:S(2)}) collective-permute-start(bf16[768,768]{1,0:T(8,128)(2,1)} %c.1), channel_id=1, source_target_pairs={{0,16},{16,0},{1,17},{17,1},{2,18},{18,2},{3,19},{19,3},{4,20},{20... | collective-permute-start | bytes 3538952 | tf_op jit(solution)/shard_map/ppermute | solution.py:30
  16.9 9.7 %collective-permute-start.2 = (bf16[128,1536]{1,0:T(8,128)(2,1)S(1)}, bf16[128,1536]{1,0:T(8,128)(2,1)S(1)}, u32[]{:S(2)}, u32[]{:S(2)}) collective-permute-start(bf16[128,1536]{1,0:T(8,128)(2,1)S(1)} %bitcast.28), channel_id=1, source_target_pairs={{0,1},{1,2},{2,3},{3,4},{4,5},{5,6},{6,7},{7,0},{8,9},{9,10},{10,1... | collective-permute-start | bytes 1179656 | tf_op jit(solution)/shard_map/ppermute | solution.py:26
  18.8 9.7 %collective-permute-start = (bf16[128,1536]{1,0:T(8,128)(2,1)S(1)}, bf16[128,1536]{1,0:T(8,128)(2,1)S(1)}, u32[]{:S(2)}, u32[]{:S(2)}) collective-permute-start(bf16[128,1536]{1,0:T(8,128)(2,1)S(1)} %bitcast.29), channel_id=1, source_target_pairs={{0,7},{1,0},{2,1},{3,2},{4,3},{5,4},{6,5},{7,6},{8,15},{9,8},{10,9... | collective-permute-start | bytes 1179656 | tf_op jit(solution)/shard_map/ppermute | solution.py:26
  19.0 39.4 %collective-permute-start.10 = (bf16[768,768]{1,0:T(8,128)(2,1)S(1)}, bf16[768,768]{1,0:T(8,128)(2,1)S(1)}, u32[]{:S(2)}, u32[]{:S(2)}) collective-permute-start(bf16[768,768]{1,0:T(8,128)(2,1)S(1)} %shard_map.58), channel_id=1, source_target_pairs={{0,8},{8,0},{1,9},{9,1},{2,10},{10,2},{3,11},{11,3},{4,12},{12,4},... | collective-permute-start | bytes 3538952 | tf_op jit(solution)/shard_map/ppermute | solution.py:34
  26.6 11.6 %collective-permute-start.3 = (bf16[128,1536]{1,0:T(8,128)(2,1)S(1)}, bf16[128,1536]{1,0:T(8,128)(2,1)S(1)}, u32[]{:S(2)}, u32[]{:S(2)}) collective-permute-start(bf16[128,1536]{1,0:T(8,128)(2,1)S(1)} %collective-permute-done.2.refs_1_), channel_id=1, source_target_pairs={{0,1},{1,2},{2,3},{3,4},{4,5},{5,6},{6,7},{7,0},{8,9},{9,10},{10,1... | collective-permute-start | bytes 1179656 | tf_op jit(solution)/shard_map/ppermute | solution.py:26
  28.5 10.1 %collective-permute-start.1 = (bf16[128,1536]{1,0:T(8,128)(2,1)S(1)}, bf16[128,1536]{1,0:T(8,128)(2,1)S(1)}, u32[]{:S(2)}, u32[]{:S(2)}) collective-permute-start(bf16[128,1536]{1,0:T(8,128)(2,1)S(1)} %collective-permute-done.refs_2_), channel_id=1, source_target_pairs={{0,7},{1,0},{2,1},{3,2},{4,3},{5,4},{6,5},{7,6},{8,15},{9,8},{10,9... | collective-permute-start | bytes 1179656 | tf_op jit(solution)/shard_map/ppermute | solution.py:26
  38.2 20.2 %collective-permute-start.4 = (bf16[128,1536]{1,0:T(8,128)(2,1)S(1)}, bf16[128,1536]{1,0:T(8,128)(2,1)S(1)}, u32[]{:S(2)}, u32[]{:S(2)}) collective-permute-start(bf16[128,1536]{1,0:T(8,128)(2,1)S(1)} %collective-permute-done.3.refs_3_), channel_id=1, source_target_pairs={{0,1},{1,2},{2,3},{3,4},{4,5},{5,6},{6,7},{7,0},{8,9},{9,10},{10,1... | collective-permute-start | bytes 1179656 | tf_op jit(solution)/shard_map/ppermute | solution.py:26
  38.6 19.8 %collective-permute-start.5 = (bf16[128,1536]{1,0:T(8,128)(2,1)S(1)}, bf16[128,1536]{1,0:T(8,128)(2,1)S(1)}, u32[]{:S(2)}, u32[]{:S(2)}) collective-permute-start(bf16[128,1536]{1,0:T(8,128)(2,1)S(1)} %collective-permute-done.1.refs_0_), channel_id=1, source_target_pairs={{0,7},{1,0},{2,1},{3,2},{4,3},{5,4},{6,5},{7,6},{8,15},{9,8},{10,9... | collective-permute-start | bytes 1179656 | tf_op jit(solution)/shard_map/ppermute | solution.py:26
  41.2 4.2 %copy-start.2 = (bf16[768,768]{1,0:T(8,128)(2,1)}, bf16[768,768]{1,0:T(8,128)(2,1)S(1)}, u32[]{:S(2)}) copy-start(bf16[768,768]{1,0:T(8,128)(2,1)S(1)} %collective-permute-done.8.b) | copy-start | bytes 3538948
  41.2 17.2 %collective-permute-start.6 = (bf16[64,1536]{1,0:T(8,128)(2,1)S(1)}, bf16[64,1536]{1,0:T(8,128)(2,1)S(1)}, u32[]{:S(2)}, u32[]{:S(2)}) collective-permute-start(bf16[64,1536]{1,0:T(8,128)(2,1)S(1)} %slice.20), channel_id=1, source_target_pairs={{0,2},{1,3},{2,4},{3,5},{4,6},{5,7},{6,0},{7,1},{8,10},{9,11},{10,... | collective-permute-start | bytes 589832 | tf_op jit(solution)/shard_map/ppermute | solution.py:26
  44.4 14.0 %collective-permute-start.7 = (bf16[64,1536]{1,0:T(8,128)(2,1)S(1)}, bf16[64,1536]{1,0:T(8,128)(2,1)S(1)}, u32[]{:S(2)}, u32[]{:S(2)}) collective-permute-start(bf16[64,1536]{1,0:T(8,128)(2,1)S(1)} %slice.21), channel_id=1, source_target_pairs={{0,6},{1,7},{2,0},{3,1},{4,2},{5,3},{6,4},{7,5},{8,14},{9,15},{10,... | collective-permute-start | bytes 589832 | tf_op jit(solution)/shard_map/ppermute | solution.py:26
  103.2 19.0 %all-to-all-start.2 = ((bf16[8,2,64,768]{3,2,1,0:T(8,128)(2,1)}), bf16[8,2,64,768]{3,2,1,0:T(8,128)(2,1)S(1)}, u32[]{:S(2)}, u32[]{:S(2)}) async-start(bf16[8,2,64,768]{3,2,1,0:T(8,128)(2,1)} %broadcast_in_dim.2), calls=%async_computation.2 | async-start | bytes 3145728 | tf_op jit(solution)/shard_map/all_to_all | solution.py:223
  106.8 3.9 %collective-permute-start.11 = (bf16[768,768]{1,0:T(8,128)(2,1)}, bf16[768,768]{1,0:T(8,128)(2,1)}, u32[]{:S(2)}, u32[]{:S(2)}) collective-permute-start(bf16[768,768]{1,0:T(8,128)(2,1)} %a.3), channel_id=1, source_target_pairs={{0,16},{16,0},{1,17},{17,1},{2,18},{18,2},{3,19},{19,3},{4,20},{20... | collective-permute-start | bytes 3538952 | tf_op jit(solution)/shard_map/ppermute | solution.py:30
  107.1 4.6 %copy-start = (bf16[768,768]{1,0:T(8,128)(2,1)}, bf16[768,768]{1,0:T(8,128)(2,1)S(1)}, u32[]{:S(2)}) copy-start(bf16[768,768]{1,0:T(8,128)(2,1)S(1)} %shard_map.60.b) | copy-start | bytes 3538948
  107.1 4.6 %collective-permute-start.12 = (bf16[768,768]{1,0:T(8,128)(2,1)S(1)}, bf16[768,768]{1,0:T(8,128)(2,1)}, u32[]{:S(2)}, u32[]{:S(2)}) collective-permute-start(bf16[768,768]{1,0:T(8,128)(2,1)S(1)} %shard_map.60.b), channel_id=1, source_target_pairs={{0,16},{16,0},{1,17},{17,1},{2,18},{18,2},{3,19},{19,3},{4,20},{20... | collective-permute-start | bytes 3538952 | tf_op jit(solution)/shard_map/ppermute | solution.py:30
  126.7 15.0 %collective-permute-start.15 = (bf16[1,2,64,768]{3,2,1,0:T(8,128)(2,1)S(1)}, bf16[1,2,64,768]{3,2,1,0:T(8,128)(2,1)S(1)}, u32[]{:S(2)}, u32[]{:S(2)}) collective-permute-start(bf16[1,2,64,768]{3,2,1,0:T(8,128)(2,1)S(1)} %get-tuple-element.17), channel_id=1, source_target_pairs={{0,7},{1,0},{2,1},{3,2},{4,3},{5,4},{6,5},{7,6},{8,15},{9,8},{10,9... | collective-permute-start | bytes 589832 | tf_op jit(solution)/shard_map/ppermute | solution.py:26
  126.8 15.0 %collective-permute-start.16 = (bf16[1,2,64,768]{3,2,1,0:T(8,128)(2,1)S(1)}, bf16[1,2,64,768]{3,2,1,0:T(8,128)(2,1)S(1)}, u32[]{:S(2)}, u32[]{:S(2)}) collective-permute-start(bf16[1,2,64,768]{3,2,1,0:T(8,128)(2,1)S(1)} %get-tuple-element.18), channel_id=1, source_target_pairs={{0,1},{1,2},{2,3},{3,4},{4,5},{5,6},{6,7},{7,0},{8,9},{9,10},{10,1... | collective-permute-start | bytes 589832 | tf_op jit(solution)/shard_map/ppermute | solution.py:26
  131.2 10.6 %collective-permute-start.17 = (bf16[64,768]{1,0:T(8,128)(2,1)S(1)}, bf16[64,768]{1,0:T(8,128)(2,1)S(1)}, u32[]{:S(2)}, u32[]{:S(2)}) collective-permute-start(bf16[64,768]{1,0:T(8,128)(2,1)S(1)} %get-tuple-element.19), channel_id=1, source_target_pairs={{0,6},{1,7},{2,0},{3,1},{4,2},{5,3},{6,4},{7,5},{8,14},{9,15},{10,... | collective-permute-start | bytes 294920 | tf_op jit(solution)/shard_map/ppermute | solution.py:26
  131.2 10.6 %collective-permute-start.18 = (bf16[64,768]{1,0:T(8,128)(2,1)S(1)}, bf16[64,768]{1,0:T(8,128)(2,1)S(1)}, u32[]{:S(2)}, u32[]{:S(2)}) collective-permute-start(bf16[64,768]{1,0:T(8,128)(2,1)S(1)} %get-tuple-element.20), channel_id=1, source_target_pairs={{0,2},{1,3},{2,4},{3,5},{4,6},{5,7},{6,0},{7,1},{8,10},{9,11},{10,... | collective-permute-start | bytes 294920 | tf_op jit(solution)/shard_map/ppermute | solution.py:26
  134.1 12.6 %collective-permute-start.13 = (bf16[1,2,64,768]{3,2,1,0:T(8,128)(2,1)S(1)}, bf16[1,2,64,768]{3,2,1,0:T(8,128)(2,1)S(1)}, u32[]{:S(2)}, u32[]{:S(2)}) collective-permute-start(bf16[1,2,64,768]{3,2,1,0:T(8,128)(2,1)S(1)} %get-tuple-element.15), channel_id=1, source_target_pairs={{0,7},{1,0},{2,1},{3,2},{4,3},{5,4},{6,5},{7,6},{8,15},{9,8},{10,9... | collective-permute-start | bytes 589832 | tf_op jit(solution)/shard_map/ppermute | solution.py:26
  141.7 6.8 %collective-permute-start.14 = (bf16[1,2,64,768]{3,2,1,0:T(8,128)(2,1)S(1)}, bf16[1,2,64,768]{3,2,1,0:T(8,128)(2,1)S(1)}, u32[]{:S(2)}, u32[]{:S(2)}) collective-permute-start(bf16[1,2,64,768]{3,2,1,0:T(8,128)(2,1)S(1)} %get-tuple-element.16), channel_id=1, source_target_pairs={{0,1},{1,2},{2,3},{3,4},{4,5},{5,6},{6,7},{7,0},{8,9},{9,10},{10,1... | collective-permute-start | bytes 589832 | tf_op jit(solution)/shard_map/ppermute | solution.py:26
  141.9 23.9 %copy-start.3 = (bf16[8,12288]{1,0:T(8,128)(2,1)S(1)}, bf16[8,12288]{1,0:T(8,128)(2,1)}, u32[]{:S(2)}) copy-start(bf16[8,12288]{1,0:T(8,128)(2,1)} %tokens.1) | copy-start | bytes 589828
  141.9 10.9 %collective-permute-start.19 = (bf16[2,64,768]{2,1,0:T(8,128)(2,1)S(1)}, bf16[2,64,768]{2,1,0:T(8,128)(2,1)S(1)}, u32[]{:S(2)}, u32[]{:S(2)}) collective-permute-start(bf16[2,64,768]{2,1,0:T(8,128)(2,1)S(1)} %get-tuple-element.21), channel_id=1, source_target_pairs={{0,6},{1,7},{2,0},{3,1},{4,2},{5,3},{6,4},{7,5},{8,14},{9,15},{10,... | collective-permute-start | bytes 589832 | tf_op jit(solution)/shard_map/ppermute | solution.py:26
  145.1 9.6 %collective-permute-start.20 = (bf16[2,64,768]{2,1,0:T(8,128)(2,1)S(1)}, bf16[2,64,768]{2,1,0:T(8,128)(2,1)S(1)}, u32[]{:S(2)}, u32[]{:S(2)}) collective-permute-start(bf16[2,64,768]{2,1,0:T(8,128)(2,1)S(1)} %get-tuple-element.22), channel_id=1, source_target_pairs={{0,2},{1,3},{2,4},{3,5},{4,6},{5,7},{6,0},{7,1},{8,10},{9,11},{10,... | collective-permute-start | bytes 589832 | tf_op jit(solution)/shard_map/ppermute | solution.py:26
  155.5 10.3 %all-to-all-start.3 = ((bf16[8,16,768]{2,1,0:T(8,128)(2,1)}), bf16[8,16,768]{2,1,0:T(8,128)(2,1)S(1)}, u32[]{:S(2)}, u32[]{:S(2)}) async-start(bf16[8,16,768]{2,1,0:T(8,128)(2,1)} %copy_bitcast_fusion), calls=%async_computation.3 | async-start | bytes 393216 | tf_op jit(solution)/shard_map/all_to_all | solution.py:234

commit v5 on v4

--- a/solution.py
+++ b/solution.py
@@ -91,13 +91,13 @@
     out[0, :unit], out[0, unit:], out[1, :unit], out[1, unit:] = a[...], b[...], c[...], d[...]
 
 
-def stack(shape, *weights):
+def stack(*weights):
     return pl.pallas_call(
         stack_kernel,
         grid=(3,),
         in_specs=[pl.BlockSpec((unit, tile), lambda j: (0, j))] * 4,
         out_specs=pl.BlockSpec((2, 2 * unit, tile), lambda j: (0, 0, j)),
-        out_shape=shape((2, 2 * unit, unit), bf16),
+        out_shape=jax.ShapeDtypeStruct((2, 2 * unit, unit), bf16),
         compiler_params=pltpu.CompilerParams(vmem_limit_bytes=8 * 2**20),
     )(*(in_hbm(weight) for weight in weights))
 
@@ -105,11 +105,61 @@
 order = (0, 1, 7, 2, 6, 3, 5, 4)
 
 
-def second_kernel(_, mine, theirs, weight, near, left, right, p1, p7, left_half, right_half):
+def activate_kernel(terms, out, hidden, sent):
+    copies = []
+    for y in range(2):
+        total = terms[y].astype(f32)
+        for j in range(1, 8):
+            total += terms[2 * j + y].astype(f32)
+        hidden[y] = (jax.nn.silu(total[:, :unit]) * total[:, unit:]).astype(bf16)
+        for j in range(8):
+            copies.append(pltpu.make_async_copy(hidden.at[y], out.at[j, y], sent.at[y, j]))
+            copies[-1].start()
+    for copy in copies:
+        copy.wait()
+
+
+def activate(terms):
+    return pl.pallas_call(
+        activate_kernel,
+        in_specs=[pl.BlockSpec(memory_space=pltpu.VMEM)],
+        out_specs=anywhere,
+        out_shape=pltpu.HBM((8, 2, 64, unit), bf16),
+        scratch_shapes=[pltpu.VMEM((2, 64, unit), bf16), pltpu.SemaphoreType.DMA((2, 8))],
+        compiler_params=pltpu.CompilerParams(vmem_limit_bytes=12 * 2**20),
+    )(terms)
+
+
+def fetch(weights, held, arrived):
+    return [
+        pltpu.make_async_copy(
+            weight, held.at[k // 2, pl.ds(k % 2 * unit, unit)], arrived.at[k]
+        )
+        for k, weight in enumerate(weights)
+    ]
+
+
+held_weights = [pltpu.VMEM((2, 2 * unit, unit), bf16), pltpu.SemaphoreType.DMA((4,))]
+
+
+def second_kernel(_, mine, theirs, *refs):
+    near, left, right, p1, p7, left_half, right_half, held, arrived = refs[4:]
     places = {0: near.at[0], 2: near.at[1], 6: near.at[2]}
     places |= {3: left.at[0], 5: right.at[0], 1: p1.at[0], 7: p7.at[0]}
-    total = product(mine[...].reshape(512, unit), weight[0, :unit])
-    total += product(theirs[...].reshape(512, unit), weight[0, unit:])
+    step = pl.program_id(0)
+    copies = fetch(refs[:4], held, arrived)
+
+    @pl.when(step == 0)
+    def _():
+        for copy in copies:
+            copy.start()
+        copies[0].wait()
+
+    pl.when(step == 1)(copies[2].wait)
+    total = product(mine[...].reshape(512, unit), held[step, :unit])
+    pl.when(step == 0)(copies[1].wait)
+    pl.when(step == 1)(copies[3].wait)
+    total += product(theirs[...].reshape(512, unit), held[step, unit:])
     total = total.reshape(8, 8, 8, unit)
     for k, s in enumerate(order):
         piece = total[:, k].reshape(64, unit).astype(bf16)
@@ -123,7 +173,7 @@
                 half[...] = piece
 
 
-def second_product(yh, hidden, weight):
+def second_product(yh, hidden, weights):
     counts = (3, 1, 1, 1, 1)
     return pl.pallas_call(
         second_kernel,
@@ -133,10 +183,11 @@
             in_specs=[
                 pl.BlockSpec((8, 1, 64, unit), lambda n, yh: (0, yh[0], 0, 0)),
                 pl.BlockSpec((8, 1, 64, unit), lambda n, yh: (0, 1 - yh[0], 0, 0)),
-                pl.BlockSpec((1, 2 * unit, unit), lambda n, yh: (n, 0, 0)),
-            ],
+            ]
+            + [anywhere] * 4,
             out_specs=[pl.BlockSpec((k, 1, 64, unit), lambda n, yh: (0, n, 0, 0)) for k in counts]
             + [pl.BlockSpec((64, unit), lambda n, yh: (0, 0))] * 2,
+            scratch_shapes=held_weights,
         ),
         out_shape=[jax.ShapeDtypeStruct((k, 2, 64, unit), bf16) for k in counts]
         + [jax.ShapeDtypeStruct((64, unit), bf16)] * 2,
@@ -144,7 +195,7 @@
         cost_estimate=pl.CostEstimate(
             flops=512 * 8 * unit * unit, bytes_accessed=8 * unit * unit, transcendentals=0
         ),
-    )(yh.reshape(1), hidden, hidden, in_hbm(weight))
+    )(yh.reshape(1), hidden, hidden, *(in_hbm(weight) for weight in weights))
 
 
 def relay_kernel(near, left, right, left_half, right_half, to_left, to_right):
@@ -175,9 +226,9 @@
     for j in range(8):
         low = normed[:, 2 * j * unit : (2 * j + 1) * unit]
         high = normed[:, (2 * j + 1) * unit : (2 * j + 2) * unit]
-        for y in range(2):
-            out[j, y, :, :unit] = jnp.where(swap, high, low).astype(bf16)
-            out[j, y, :, unit:] = jnp.where(swap, low, high).astype(bf16)
+        for k, half in enumerate((jnp.where(swap, high, low), jnp.where(swap, low, high))):
+            twice = jnp.concatenate((half, half), axis=0)
+            out[j, :, k * unit : (k + 1) * unit] = twice.astype(bf16)
 
 
 def prepare(core, tokens, norm_gain):
@@ -186,7 +237,7 @@
         prepare_kernel,
         in_specs=[pl.BlockSpec(memory_space=pltpu.SMEM), vmem, vmem],
         out_specs=vmem,
-        out_shape=pltpu.HBM((8, 2, 8, 2 * unit), bf16),
+        out_shape=pltpu.HBM((8, 16, 2 * unit), bf16),
         compiler_params=pltpu.CompilerParams(vmem_limit_bytes=8 * 2**20),
     )(core.reshape(1), in_hbm(tokens), in_hbm(norm_gain.reshape(1, -1)))
 
@@ -204,7 +255,7 @@
     r4, l4 = shift(r2[:64], 2), shift(l2[64:], -2)
 
     first = (gate_weight, core_partner(gate_weight), up_weight, core_partner(up_weight))
-    first = stack(jax.ShapeDtypeStruct, *first)
+    first = stack(*first)
     down_y = yh_partner(after(block, down_weight))
     whole = [(s, 0) for s in range(4)]
     partial = first_product(whole, (block, r1, l1, r2), first)
@@ -214,17 +265,13 @@
 
     down_y = after(in_hbm(partial), down_y)
     second = (down_weight, down_y, core_partner(down_weight), core_partner(down_y))
-    second = stack(pltpu.HBM, *second)
-
-    summed = jnp.sum(terms.reshape(8, 2, 64, 2 * unit).astype(f32), axis=0)
-    hidden = (jax.nn.silu(summed[:, :, :unit]) * summed[:, :, unit:]).astype(bf16)
-
-    hidden = jnp.broadcast_to(hidden[None], (8, 2, 64, unit))
+
+    hidden = activate(terms)
     hidden = lax.all_to_all(hidden, ("yl", "x"), 0, 0)
 
     mine, left, right, p1, p7, left_half, right_half = second_product(yh, hidden, second)
+    left, right = shift(left, -1), shift(right, 1)
     left_half, right_half = shift(left_half, -2), shift(right_half, 2)
-    left, right = shift(left, -1), shift(right, 1)
     p1, p7 = shift(p1, -1), shift(p7, 1)
     to_left, to_right = relay(mine, left, right, left_half, right_half)
     terms = (mine[0], p1[0], p7[0], shift(to_left, -2), shift(to_right, 2))

time: 167 us -> 167 us (level)
  waiting for transfers between devices: 58.4 us -> 62.9 us
  Pallas kernels: 23.1 us -> 19.5 us
    all_to_all x1, waiting for transfers between devices: 5.03 us -> 10.6 us  [on_device(): hidden = lax.all_to_all(hidden, ('yl', 'x'), 0, 0)]
    pallas_call x2 -> x1, Pallas kernels: 8.67 us -> 3.25 us  [stack(): pl.pallas_call(stack_kernel, grid=(3,), in_specs=[pl.BlockSpec((unit, til...]
  transfers between devices with their start and end apart: 24 -> 24, of which waited for: 14 -> 14; matrix products, arithmetic and copies ran while one was open for 0% -> 1% of each run, Pallas kernels for 8% -> 4%
where the time goes in v5:
time: 167 us; the launch traced here: 166 us
  waiting for transfers between devices  62.9 us (38%)
  starting transfers between devices  42.1 us (25%)
  blocking collectives  38.9 us (23%)
  Pallas kernels  19.5 us (12%)
    all_to_all x1, blocking collectives, on_device(): lax.all_to_all(partial.reshape(16, 64, 2 * unit), ('yl', 'x', 'yh'), 0, 0)  38.9 us
    ppermute x16, waiting for transfers between devices, shift(): return lax.ppermute(block, 'z', [(i, (i + steps) % 8) for i in range(8)])  34.2 us
    ppermute x16, starting transfers between devices, shift(): return lax.ppermute(block, 'z', [(i, (i + steps) % 8) for i in range(8)])  24 us
    all_to_all x1, waiting for transfers between devices, on_device(): hidden = lax.all_to_all(hidden, ('yl', 'x'), 0, 0)  10.6 us
    pallas_call x2, Pallas kernels, first_product(): pl.pallas_call(lambda *refs: first_kernel(rows, *refs), grid=(2,), in_spe...  7.73 us
    all_to_all x1, starting transfers between devices, on_device(): lax.all_to_all(pieces.reshape(16, 8, 2 * unit), ('yl', 'x', 'yh'), 0, 0)  7.28 us
    all_to_all x1, waiting for transfers between devices, on_device(): lax.all_to_all(pieces.reshape(16, 8, 2 * unit), ('yl', 'x', 'yh'), 0, 0)  6.96 us
    all_to_all x1, waiting for transfers between devices, on_device(): branch = lax.all_to_all(branch.reshape(8, 16, unit), ('yl', 'x'), 0, 0)  6.87 us
  transfers between devices with their start and end apart: 24, of which 14 were waited for; matrix products, arithmetic and copies ran while one was open for 1% of the time, Pallas kernels for 4%

profile of v5, /device:TPU:48, one launch (start us, length us, event | category | flops | bytes accessed | tf_op | source)
XLA Modules:
  0.0 166.4 jit_solution(3495760574943801084)
XLA Ops:
  0.0 2.0 %shard_map.55 = bf16[8,16,1536]{2,1,0:T(8,128)(2,1)} custom-call(s32[1]{0:T(128)} %bitcast.1.core, bf16[8,12288]{1,0:T(8,128)(2,1)} %tokens.1, f32[1,12288]{1,0:T(1,128)} %bitcast.34), custom_call_target="tpu_custom_call" | custom-call | tf_op jit(solution)/shard_map/pallas_call | solution.py:236
  2.0 7.3 %all-to-all-start = ((bf16[16,8,1536]{2,1,0:T(8,128)(2,1)}), bf16[16,8,1536]{2,1,0:T(8,128)(2,1)S(1)}, u32[]{:S(2)}, u32[]{:S(2)}) async-start(bf16[16,8,1536]{2,1,0:T(8,128)(2,1)} %bitcast.31), calls=%async_computation | async-start | bytes 786432 | tf_op jit(solution)/shard_map/all_to_all | solution.py:249
  9.3 0.1 collective-permute-start.8
  9.4 0.5 collective-permute-start.9
  9.9 7.0 %all-to-all-done = bf16[16,8,1536]{2,1,0:T(8,128)(2,1)S(1)} async-done(((bf16[16,8,1536]{2,1,0:T(8,128)(2,1)}), bf16[16,8,1536]{2,1,0:T(8,128)(2,1)S(1)}, u32[]{:S(2)}, u32[]{:S(2)}) %all-to-all-start) | async-done | bytes 393248 | tf_op jit(solution)/shard_map/all_to_all | solution.py:249
  16.9 1.9 %collective-permute-start.2 = (bf16[128,1536]{1,0:T(8,128)(2,1)S(1)}, bf16[128,1536]{1,0:T(8,128)(2,1)S(1)}, u32[]{:S(2)}, u32[]{:S(2)}) collective-permute-start(bf16[128,1536]{1,0:T(8,128)(2,1)S(1)} %bitcast.26), channel_id=1, source_target_pairs={{0,1},{1,2},{2,3},{3,4},{4,5},{5,6},{6,7},{7,0},{8,9},{9,10},{10,1... | collective-permute-start | bytes 1179656 | tf_op jit(solution)/shard_map/ppermute | solution.py:26
  18.8 0.1 collective-permute-start
  18.9 1.3 copy.11.array
  20.2 2.6 %collective-permute-start.10 = (bf16[768,768]{1,0:T(8,128)(2,1)S(1)}, bf16[768,768]{1,0:T(8,128)(2,1)S(1)}, u32[]{:S(2)}, u32[]{:S(2)}) collective-permute-start(bf16[768,768]{1,0:T(8,128)(2,1)S(1)} %shard_map.58), channel_id=1, source_target_pairs={{0,8},{8,0},{1,9},{9,1},{2,10},{10,2},{3,11},{11,3},{4,12},{12,4},... | collective-permute-start | bytes 3538952 | tf_op jit(solution)/shard_map/ppermute | solution.py:34
  22.8 3.8 %collective-permute-done.2.refs_1_ = bf16[128,1536]{1,0:T(8,128)(2,1)S(1)} collective-permute-done((bf16[128,1536]{1,0:T(8,128)(2,1)S(1)}, bf16[128,1536]{1,0:T(8,128)(2,1)S(1)}, u32[]{:S(2)}, u32[]{:S(2)}) %collective-permute-start.2) | collective-permute-done | bytes 393248 | tf_op jit(solution)/shard_map/ppermute | solution.py:26
  26.6 1.9 %collective-permute-start.3 = (bf16[128,1536]{1,0:T(8,128)(2,1)S(1)}, bf16[128,1536]{1,0:T(8,128)(2,1)S(1)}, u32[]{:S(2)}, u32[]{:S(2)}) collective-permute-start(bf16[128,1536]{1,0:T(8,128)(2,1)S(1)} %collective-permute-done.2.refs_1_), channel_id=1, source_target_pairs={{0,1},{1,2},{2,3},{3,4},{4,5},{5,6},{6,7},{7,0},{8,9},{9,10},{10,1... | collective-permute-start | bytes 1179656 | tf_op jit(solution)/shard_map/ppermute | solution.py:26
  28.5 2.3 %collective-permute-start.1 = (bf16[128,1536]{1,0:T(8,128)(2,1)S(1)}, bf16[128,1536]{1,0:T(8,128)(2,1)S(1)}, u32[]{:S(2)}, u32[]{:S(2)}) collective-permute-start(bf16[128,1536]{1,0:T(8,128)(2,1)S(1)} %collective-permute-done.refs_2_), channel_id=1, source_target_pairs={{0,7},{1,0},{2,1},{3,2},{4,3},{5,4},{6,5},{7,6},{8,15},{9,8},{10,9... | collective-permute-start | bytes 1179656 | tf_op jit(solution)/shard_map/ppermute | solution.py:26
  30.8 7.3 %collective-permute-done.3.refs_3_ = bf16[128,1536]{1,0:T(8,128)(2,1)S(1)} collective-permute-done((bf16[128,1536]{1,0:T(8,128)(2,1)S(1)}, bf16[128,1536]{1,0:T(8,128)(2,1)S(1)}, u32[]{:S(2)}, u32[]{:S(2)}) %collective-permute-start.3) | collective-permute-done | bytes 393248 | tf_op jit(solution)/shard_map/ppermute | solution.py:26
  38.2 0.0 collective-permute-start.4
  38.2 0.4 collective-permute-done.1.refs_0_
  38.6 2.5 %collective-permute-start.5 = (bf16[128,1536]{1,0:T(8,128)(2,1)S(1)}, bf16[128,1536]{1,0:T(8,128)(2,1)S(1)}, u32[]{:S(2)}, u32[]{:S(2)}) collective-permute-start(bf16[128,1536]{1,0:T(8,128)(2,1)S(1)} %collective-permute-done.1.refs_0_), channel_id=1, source_target_pairs={{0,7},{1,0},{2,1},{3,2},{4,3},{5,4},{6,5},{7,6},{8,15},{9,8},{10,9... | collective-permute-start | bytes 1179656 | tf_op jit(solution)/shard_map/ppermute | solution.py:26
  41.2 3.2 %collective-permute-start.6 = (bf16[64,1536]{1,0:T(8,128)(2,1)S(1)}, bf16[64,1536]{1,0:T(8,128)(2,1)S(1)}, u32[]{:S(2)}, u32[]{:S(2)}) collective-permute-start(bf16[64,1536]{1,0:T(8,128)(2,1)S(1)} %slice.12), channel_id=1, source_target_pairs={{0,2},{1,3},{2,4},{3,5},{4,6},{5,7},{6,0},{7,1},{8,10},{9,11},{10,... | collective-permute-start | bytes 589832 | tf_op jit(solution)/shard_map/ppermute | solution.py:26
  44.4 1.0 collective-permute-start.7
  45.4 3.2 %shard_map.56.refs_4_.refs_5_ = bf16[2,1536,768]{2,1,0:T(8,128)(2,1)S(1)} custom-call(bf16[768,768]{1,0:T(8,128)(2,1)} %a.1, bf16[768,768]{1,0:T(8,128)(2,1)} %collective-permute-done.8.b, bf16[768,768]{1,0:T(8,128)(2,1)} %c.1, bf16[768,768]{1,0:T(8,128)(2,1)} %collective-permute-done.9.d), custom_call_target="tpu_custom_call" | custom-call | tf_op jit(solution)/shard_map/pallas_call | solution.py:95
  48.7 3.9 %shard_map.57.refs_6_ = bf16[8,2,64,1536]{3,2,1,0:T(8,128)(2,1)} custom-call(bf16[128,1536]{1,0:T(8,128)(2,1)S(1)} %bitcast.29, bf16[128,1536]{1,0:T(8,128)(2,1)S(1)} %collective-permute-done.2.refs_1_, bf16[128,1536]{1,0:T(8,128)(2,1)S(1)} %collective-permute-done.refs_2_, bf16[128,1536]{1,0:T(8,128)(2,1)S(1)} %collective-permute-done.3.refs_3_, ...), custom_call_target="tpu_custom_call" | custom-call | flops 2415919104 | bytes 4718592 | tf_op jit(solution)/shard_map/pallas_call | solution.py:73
  52.5 5.8 %collective-permute-done.6.refs_3_ = bf16[64,1536]{1,0:T(8,128)(2,1)S(1)} collective-permute-done((bf16[64,1536]{1,0:T(8,128)(2,1)S(1)}, bf16[64,1536]{1,0:T(8,128)(2,1)S(1)}, u32[]{:S(2)}, u32[]{:S(2)}) %collective-permute-start.6) | collective-permute-done | bytes 196640 | tf_op jit(solution)/shard_map/ppermute | solution.py:26
  58.4 0.0 collective-permute-done.7.refs_4_
  58.4 3.9 %shard_map.59.dependency = bf16[8,2,64,1536]{3,2,1,0:T(8,128)(2,1)} custom-call(bf16[128,1536]{1,0:T(8,128)(2,1)S(1)} %collective-permute-done.1.refs_0_, bf16[128,1536]{1,0:T(8,128)(2,1)S(1)} %collective-permute-done.4.refs_1_, bf16[128,1536]{1,0:T(8,128)(2,1)S(1)} %collective-permute-done.5.refs_2_, ...), custom_call_target="tpu_custom_call", output_to_operand_aliasing={{}: (6, {})} | custom-call | flops 2415919104 | bytes 4718592 | tf_op jit(solution)/shard_map/pallas_call | solution.py:73
  62.3 38.9 %all_to_all.20.terms = bf16[16,64,1536]{2,1,0:T(8,128)(2,1)S(1)} all-to-all(bf16[16,64,1536]{2,1,0:T(8,128)(2,1)} %bitcast.30), channel_id=1, replica_groups=mesh['yl'=2,'x'=4,'c'=2,'yh'=2,'z'=8] {'yl','x','yh'}, dimensions={0} | all-to-all | bytes 6291456 | tf_op jit(solution)/shard_map/all_to_all | solution.py:264
  101.2 1.6 shard_map.60
  102.8 3.6 %all-to-all-start.2 = ((bf16[8,2,64,768]{3,2,1,0:T(8,128)(2,1)}), bf16[8,2,64,768]{3,2,1,0:T(8,128)(2,1)S(1)}, u32[]{:S(2)}, u32[]{:S(2)}) async-start(bf16[8,2,64,768]{3,2,1,0:T(8,128)(2,1)} %shard_map.60), calls=%async_computation.2 | async-start | bytes 3145728 | tf_op jit(solution)/shard_map/all_to_all | solution.py:270
  106.4 0.1 collective-permute-start.11
  106.5 0.5 collective-permute-start.12
  107.0 2.7 %collective-permute-done.11.refs_2_ = bf16[768,768]{1,0:T(8,128)(2,1)} collective-permute-done((bf16[768,768]{1,0:T(8,128)(2,1)}, bf16[768,768]{1,0:T(8,128)(2,1)}, u32[]{:S(2)}, u32[]{:S(2)}) %collective-permute-start.11) | collective-permute-done | bytes 1179680 | tf_op jit(solution)/shard_map/ppermute | solution.py:30
  109.7 1.5 collective-permute-done.12.refs_3_
  111.2 10.6 %all-to-all-done.2.mine.theirs = bf16[8,2,64,768]{3,2,1,0:T(8,128)(2,1)S(1)} async-done(((bf16[8,2,64,768]{3,2,1,0:T(8,128)(2,1)}), bf16[8,2,64,768]{3,2,1,0:T(8,128)(2,1)S(1)}, u32[]{:S(2)}, u32[]{:S(2)}) %all-to-all-start.2) | async-done | bytes 1572896 | tf_op jit(solution)/shard_map/all_to_all | solution.py:270
  121.8 4.8 %shard_map.62 = (bf16[3,2,64,768]{3,2,1,0:T(8,128)(2,1)S(1)}, bf16[1,2,64,768]{3,2,1,0:T(8,128)(2,1)S(1)}, bf16[1,2,64,768]{3,2,1,0:T(8,128)(2,1)S(1)}, bf16[1,2...) custom-call(s32[1]{0:T(128)} %bitcast._, ...), custom_call_target="tpu_custom_call" | custom-call | flops 2415919104 | bytes 4718592 | tf_op jit(solution)/shard_map/pallas_call | solution.py:178
  126.6 0.1 collective-permute-start.15
  126.7 4.4 %collective-permute-start.16 = (bf16[1,2,64,768]{3,2,1,0:T(8,128)(2,1)S(1)}, bf16[1,2,64,768]{3,2,1,0:T(8,128)(2,1)S(1)}, u32[]{:S(2)}, u32[]{:S(2)}) collective-permute-start(bf16[1,2,64,768]{3,2,1,0:T(8,128)(2,1)S(1)} %get-tuple-element.18), channel_id=1, source_target_pairs={{0,1},{1,2},{2,3},{3,4},{4,5},{5,6},{6,7},{7,0},{8,9},{9,10},{10,1... | collective-permute-start | bytes 589832 | tf_op jit(solution)/shard_map/ppermute | solution.py:26
  131.0 2.9 %collective-permute-start.18 = (bf16[64,768]{1,0:T(8,128)(2,1)S(1)}, bf16[64,768]{1,0:T(8,128)(2,1)S(1)}, u32[]{:S(2)}, u32[]{:S(2)}) collective-permute-start(bf16[64,768]{1,0:T(8,128)(2,1)S(1)} %get-tuple-element.20), channel_id=1, source_target_pairs={{0,2},{1,3},{2,4},{3,5},{4,6},{5,7},{6,0},{7,1},{8,10},{9,11},{10,... | collective-permute-start | bytes 294920 | tf_op jit(solution)/shard_map/ppermute | solution.py:26
  134.0 0.5 collective-permute-start.13
  134.4 7.2 %collective-permute-done.17.left_half = bf16[64,768]{1,0:T(8,128)(2,1)S(1)} collective-permute-done((bf16[64,768]{1,0:T(8,128)(2,1)S(1)}, bf16[64,768]{1,0:T(8,128)(2,1)S(1)}, u32[]{:S(2)}, u32[]{:S(2)}) %collective-permute-start.17) | collective-permute-done | bytes 98336 | tf_op jit(solution)/shard_map/ppermute | solution.py:26
  141.6 0.1 shard_map.63
  141.8 0.0 copy-start.2
  141.8 3.2 %collective-permute-start.19 = (bf16[2,64,768]{2,1,0:T(8,128)(2,1)S(1)}, bf16[2,64,768]{2,1,0:T(8,128)(2,1)S(1)}, u32[]{:S(2)}, u32[]{:S(2)}) collective-permute-start(bf16[2,64,768]{2,1,0:T(8,128)(2,1)S(1)} %get-tuple-element.21), channel_id=1, source_target_pairs={{0,6},{1,7},{2,0},{3,1},{4,2},{5,3},{6,4},{7,5},{8,14},{9,15},{10,... | collective-permute-start | bytes 589832 | tf_op jit(solution)/shard_map/ppermute | solution.py:26
  144.9 1.6 collective-permute-done.13
  146.6 1.8 %collective-permute-done.14 = bf16[1,2,64,768]{3,2,1,0:T(8,128)(2,1)S(1)} collective-permute-done((bf16[1,2,64,768]{3,2,1,0:T(8,128)(2,1)S(1)}, bf16[1,2,64,768]{3,2,1,0:T(8,128)(2,1)S(1)}, u32[]{:S(2)}, u32[]{:S(2)}) %collective-permute-start.14) | collective-permute-done | bytes 196640 | tf_op jit(solution)/shard_map/ppermute | solution.py:26
  148.3 4.3 %collective-permute-done.19 = bf16[2,64,768]{2,1,0:T(8,128)(2,1)S(1)} collective-permute-done((bf16[2,64,768]{2,1,0:T(8,128)(2,1)S(1)}, bf16[2,64,768]{2,1,0:T(8,128)(2,1)S(1)}, u32[]{:S(2)}, u32[]{:S(2)}) %collective-permute-start.19) | collective-permute-done | bytes 196640 | tf_op jit(solution)/shard_map/ppermute | solution.py:26
  152.7 1.9 %collective-permute-done.20 = bf16[2,64,768]{2,1,0:T(8,128)(2,1)S(1)} collective-permute-done((bf16[2,64,768]{2,1,0:T(8,128)(2,1)S(1)}, bf16[2,64,768]{2,1,0:T(8,128)(2,1)S(1)}, u32[]{:S(2)}, u32[]{:S(2)}) %collective-permute-start.20) | collective-permute-done | bytes 196640 | tf_op jit(solution)/shard_map/ppermute | solution.py:26
  154.6 0.8 copy_bitcast_fusion
  155.4 3.4 %all-to-all-start.3 = ((bf16[8,16,768]{2,1,0:T(8,128)(2,1)}), bf16[8,16,768]{2,1,0:T(8,128)(2,1)S(1)}, u32[]{:S(2)}, u32[]{:S(2)}) async-start(bf16[8,16,768]{2,1,0:T(8,128)(2,1)} %copy_bitcast_fusion), calls=%async_computation.3 | async-start | bytes 393216 | tf_op jit(solution)/shard_map/all_to_all | solution.py:281
  158.8 6.9 %all-to-all-done.3 = bf16[8,16,768]{2,1,0:T(8,128)(2,1)S(1)} async-done(((bf16[8,16,768]{2,1,0:T(8,128)(2,1)}), bf16[8,16,768]{2,1,0:T(8,128)(2,1)S(1)}, u32[]{:S(2)}, u32[]{:S(2)}) %all-to-all-start.3) | async-done | bytes 196640 | tf_op jit(solution)/shard_map/all_to_all | solution.py:281
  165.7 0.7 add_convert_fusion
  (22 shorter events, 0.1 us)
Async XLA Ops:
  0.0 9.3 %copy-start.1 = (bf16[768,768]{1,0:T(8,128)(2,1)S(1)}, bf16[768,768]{1,0:T(8,128)(2,1)}, u32[]{:S(2)}) copy-start(bf16[768,768]{1,0:T(8,128)(2,1)} %a.1) | copy-start | bytes 3538948
  2.0 14.8 %all-to-all-start = ((bf16[16,8,1536]{2,1,0:T(8,128)(2,1)}), bf16[16,8,1536]{2,1,0:T(8,128)(2,1)S(1)}, u32[]{:S(2)}, u32[]{:S(2)}) async-start(bf16[16,8,1536]{2,1,0:T(8,128)(2,1)} %bitcast.31), calls=%async_computation | async-start | bytes 786432 | tf_op jit(solution)/shard_map/all_to_all | solution.py:249
  9.3 31.9 %collective-permute-start.8 = (bf16[768,768]{1,0:T(8,128)(2,1)S(1)}, bf16[768,768]{1,0:T(8,128)(2,1)}, u32[]{:S(2)}, u32[]{:S(2)}) collective-permute-start(bf16[768,768]{1,0:T(8,128)(2,1)S(1)} %copy-done.1), channel_id=1, source_target_pairs={{0,16},{16,0},{1,17},{17,1},{2,18},{18,2},{3,19},{19,3},{4,20},{20... | collective-permute-start | bytes 3538952 | tf_op jit(solution)/shard_map/ppermute | solution.py:30
  9.4 35.0 %collective-permute-start.9 = (bf16[768,768]{1,0:T(8,128)(2,1)}, bf16[768,768]{1,0:T(8,128)(2,1)}, u32[]{:S(2)}, u32[]{:S(2)}) collective-permute-start(bf16[768,768]{1,0:T(8,128)(2,1)} %c.1), channel_id=1, source_target_pairs={{0,16},{16,0},{1,17},{17,1},{2,18},{18,2},{3,19},{19,3},{4,20},{20... | collective-permute-start | bytes 3538952 | tf_op jit(solution)/shard_map/ppermute | solution.py:30
  16.9 9.7 %collective-permute-start.2 = (bf16[128,1536]{1,0:T(8,128)(2,1)S(1)}, bf16[128,1536]{1,0:T(8,128)(2,1)S(1)}, u32[]{:S(2)}, u32[]{:S(2)}) collective-permute-start(bf16[128,1536]{1,0:T(8,128)(2,1)S(1)} %bitcast.26), channel_id=1, source_target_pairs={{0,1},{1,2},{2,3},{3,4},{4,5},{5,6},{6,7},{7,0},{8,9},{9,10},{10,1... | collective-permute-start | bytes 1179656 | tf_op jit(solution)/shard_map/ppermute | solution.py:26
  18.8 9.7 %collective-permute-start = (bf16[128,1536]{1,0:T(8,128)(2,1)S(1)}, bf16[128,1536]{1,0:T(8,128)(2,1)S(1)}, u32[]{:S(2)}, u32[]{:S(2)}) collective-permute-start(bf16[128,1536]{1,0:T(8,128)(2,1)S(1)} %bitcast.27), channel_id=1, source_target_pairs={{0,7},{1,0},{2,1},{3,2},{4,3},{5,4},{6,5},{7,6},{8,15},{9,8},{10,9... | collective-permute-start | bytes 1179656 | tf_op jit(solution)/shard_map/ppermute | solution.py:26
  20.2 38.2 %collective-permute-start.10 = (bf16[768,768]{1,0:T(8,128)(2,1)S(1)}, bf16[768,768]{1,0:T(8,128)(2,1)S(1)}, u32[]{:S(2)}, u32[]{:S(2)}) collective-permute-start(bf16[768,768]{1,0:T(8,128)(2,1)S(1)} %shard_map.58), channel_id=1, source_target_pairs={{0,8},{8,0},{1,9},{9,1},{2,10},{10,2},{3,11},{11,3},{4,12},{12,4},... | collective-permute-start | bytes 3538952 | tf_op jit(solution)/shard_map/ppermute | solution.py:34
  26.6 11.6 %collective-permute-start.3 = (bf16[128,1536]{1,0:T(8,128)(2,1)S(1)}, bf16[128,1536]{1,0:T(8,128)(2,1)S(1)}, u32[]{:S(2)}, u32[]{:S(2)}) collective-permute-start(bf16[128,1536]{1,0:T(8,128)(2,1)S(1)} %collective-permute-done.2.refs_1_), channel_id=1, source_target_pairs={{0,1},{1,2},{2,3},{3,4},{4,5},{5,6},{6,7},{7,0},{8,9},{9,10},{10,1... | collective-permute-start | bytes 1179656 | tf_op jit(solution)/shard_map/ppermute | solution.py:26
  28.5 10.1 %collective-permute-start.1 = (bf16[128,1536]{1,0:T(8,128)(2,1)S(1)}, bf16[128,1536]{1,0:T(8,128)(2,1)S(1)}, u32[]{:S(2)}, u32[]{:S(2)}) collective-permute-start(bf16[128,1536]{1,0:T(8,128)(2,1)S(1)} %collective-permute-done.refs_2_), channel_id=1, source_target_pairs={{0,7},{1,0},{2,1},{3,2},{4,3},{5,4},{6,5},{7,6},{8,15},{9,8},{10,9... | collective-permute-start | bytes 1179656 | tf_op jit(solution)/shard_map/ppermute | solution.py:26
  38.2 20.2 %collective-permute-start.4 = (bf16[128,1536]{1,0:T(8,128)(2,1)S(1)}, bf16[128,1536]{1,0:T(8,128)(2,1)S(1)}, u32[]{:S(2)}, u32[]{:S(2)}) collective-permute-start(bf16[128,1536]{1,0:T(8,128)(2,1)S(1)} %collective-permute-done.3.refs_3_), channel_id=1, source_target_pairs={{0,1},{1,2},{2,3},{3,4},{4,5},{5,6},{6,7},{7,0},{8,9},{9,10},{10,1... | collective-permute-start | bytes 1179656 | tf_op jit(solution)/shard_map/ppermute | solution.py:26
  38.6 19.8 %collective-permute-start.5 = (bf16[128,1536]{1,0:T(8,128)(2,1)S(1)}, bf16[128,1536]{1,0:T(8,128)(2,1)S(1)}, u32[]{:S(2)}, u32[]{:S(2)}) collective-permute-start(bf16[128,1536]{1,0:T(8,128)(2,1)S(1)} %collective-permute-done.1.refs_0_), channel_id=1, source_target_pairs={{0,7},{1,0},{2,1},{3,2},{4,3},{5,4},{6,5},{7,6},{8,15},{9,8},{10,9... | collective-permute-start | bytes 1179656 | tf_op jit(solution)/shard_map/ppermute | solution.py:26
  41.2 17.2 %collective-permute-start.6 = (bf16[64,1536]{1,0:T(8,128)(2,1)S(1)}, bf16[64,1536]{1,0:T(8,128)(2,1)S(1)}, u32[]{:S(2)}, u32[]{:S(2)}) collective-permute-start(bf16[64,1536]{1,0:T(8,128)(2,1)S(1)} %slice.12), channel_id=1, source_target_pairs={{0,2},{1,3},{2,4},{3,5},{4,6},{5,7},{6,0},{7,1},{8,10},{9,11},{10,... | collective-permute-start | bytes 589832 | tf_op jit(solution)/shard_map/ppermute | solution.py:26
  44.4 14.0 %collective-permute-start.7 = (bf16[64,1536]{1,0:T(8,128)(2,1)S(1)}, bf16[64,1536]{1,0:T(8,128)(2,1)S(1)}, u32[]{:S(2)}, u32[]{:S(2)}) collective-permute-start(bf16[64,1536]{1,0:T(8,128)(2,1)S(1)} %slice.13), channel_id=1, source_target_pairs={{0,6},{1,7},{2,0},{3,1},{4,2},{5,3},{6,4},{7,5},{8,14},{9,15},{10,... | collective-permute-start | bytes 589832 | tf_op jit(solution)/shard_map/ppermute | solution.py:26
  102.8 19.0 %all-to-all-start.2 = ((bf16[8,2,64,768]{3,2,1,0:T(8,128)(2,1)}), bf16[8,2,64,768]{3,2,1,0:T(8,128)(2,1)S(1)}, u32[]{:S(2)}, u32[]{:S(2)}) async-start(bf16[8,2,64,768]{3,2,1,0:T(8,128)(2,1)} %shard_map.60), calls=%async_computation.2 | async-start | bytes 3145728 | tf_op jit(solution)/shard_map/all_to_all | solution.py:270
  106.4 3.2 %collective-permute-start.11 = (bf16[768,768]{1,0:T(8,128)(2,1)}, bf16[768,768]{1,0:T(8,128)(2,1)}, u32[]{:S(2)}, u32[]{:S(2)}) collective-permute-start(bf16[768,768]{1,0:T(8,128)(2,1)} %refs_0_.1), channel_id=1, source_target_pairs={{0,16},{16,0},{1,17},{17,1},{2,18},{18,2},{3,19},{19,3},{4,20},{20... | collective-permute-start | bytes 3538952 | tf_op jit(solution)/shard_map/ppermute | solution.py:30
  106.5 15.3 %copy-start = (bf16[768,768]{1,0:T(8,128)(2,1)}, bf16[768,768]{1,0:T(8,128)(2,1)S(1)}, u32[]{:S(2)}) copy-start(bf16[768,768]{1,0:T(8,128)(2,1)S(1)} %shard_map.61.refs_1_) | copy-start | bytes 3538948
  106.5 4.6 %collective-permute-start.12 = (bf16[768,768]{1,0:T(8,128)(2,1)S(1)}, bf16[768,768]{1,0:T(8,128)(2,1)}, u32[]{:S(2)}, u32[]{:S(2)}) collective-permute-start(bf16[768,768]{1,0:T(8,128)(2,1)S(1)} %shard_map.61.refs_1_), channel_id=1, source_target_pairs={{0,16},{16,0},{1,17},{17,1},{2,18},{18,2},{3,19},{19,3},{4,20},{20... | collective-permute-start | bytes 3538952 | tf_op jit(solution)/shard_map/ppermute | solution.py:30
  126.6 15.0 %collective-permute-start.15 = (bf16[1,2,64,768]{3,2,1,0:T(8,128)(2,1)S(1)}, bf16[1,2,64,768]{3,2,1,0:T(8,128)(2,1)S(1)}, u32[]{:S(2)}, u32[]{:S(2)}) collective-permute-start(bf16[1,2,64,768]{3,2,1,0:T(8,128)(2,1)S(1)} %get-tuple-element.17), channel_id=1, source_target_pairs={{0,7},{1,0},{2,1},{3,2},{4,3},{5,4},{6,5},{7,6},{8,15},{9,8},{10,9... | collective-permute-start | bytes 589832 | tf_op jit(solution)/shard_map/ppermute | solution.py:26
  126.7 15.0 %collective-permute-start.16 = (bf16[1,2,64,768]{3,2,1,0:T(8,128)(2,1)S(1)}, bf16[1,2,64,768]{3,2,1,0:T(8,128)(2,1)S(1)}, u32[]{:S(2)}, u32[]{:S(2)}) collective-permute-start(bf16[1,2,64,768]{3,2,1,0:T(8,128)(2,1)S(1)} %get-tuple-element.18), channel_id=1, source_target_pairs={{0,1},{1,2},{2,3},{3,4},{4,5},{5,6},{6,7},{7,0},{8,9},{9,10},{10,1... | collective-permute-start | bytes 589832 | tf_op jit(solution)/shard_map/ppermute | solution.py:26
  131.0 10.6 %collective-permute-start.17 = (bf16[64,768]{1,0:T(8,128)(2,1)S(1)}, bf16[64,768]{1,0:T(8,128)(2,1)S(1)}, u32[]{:S(2)}, u32[]{:S(2)}) collective-permute-start(bf16[64,768]{1,0:T(8,128)(2,1)S(1)} %get-tuple-element.19), channel_id=1, source_target_pairs={{0,6},{1,7},{2,0},{3,1},{4,2},{5,3},{6,4},{7,5},{8,14},{9,15},{10,... | collective-permute-start | bytes 294920 | tf_op jit(solution)/shard_map/ppermute | solution.py:26
  131.0 10.6 %collective-permute-start.18 = (bf16[64,768]{1,0:T(8,128)(2,1)S(1)}, bf16[64,768]{1,0:T(8,128)(2,1)S(1)}, u32[]{:S(2)}, u32[]{:S(2)}) collective-permute-start(bf16[64,768]{1,0:T(8,128)(2,1)S(1)} %get-tuple-element.20), channel_id=1, source_target_pairs={{0,2},{1,3},{2,4},{3,5},{4,6},{5,7},{6,0},{7,1},{8,10},{9,11},{10,... | collective-permute-start | bytes 294920 | tf_op jit(solution)/shard_map/ppermute | solution.py:26
  134.0 12.6 %collective-permute-start.13 = (bf16[1,2,64,768]{3,2,1,0:T(8,128)(2,1)S(1)}, bf16[1,2,64,768]{3,2,1,0:T(8,128)(2,1)S(1)}, u32[]{:S(2)}, u32[]{:S(2)}) collective-permute-start(bf16[1,2,64,768]{3,2,1,0:T(8,128)(2,1)S(1)} %get-tuple-element.15), channel_id=1, source_target_pairs={{0,7},{1,0},{2,1},{3,2},{4,3},{5,4},{6,5},{7,6},{8,15},{9,8},{10,9... | collective-permute-start | bytes 589832 | tf_op jit(solution)/shard_map/ppermute | solution.py:26
  141.6 6.8 %collective-permute-start.14 = (bf16[1,2,64,768]{3,2,1,0:T(8,128)(2,1)S(1)}, bf16[1,2,64,768]{3,2,1,0:T(8,128)(2,1)S(1)}, u32[]{:S(2)}, u32[]{:S(2)}) collective-permute-start(bf16[1,2,64,768]{3,2,1,0:T(8,128)(2,1)S(1)} %get-tuple-element.16), channel_id=1, source_target_pairs={{0,1},{1,2},{2,3},{3,4},{4,5},{5,6},{6,7},{7,0},{8,9},{9,10},{10,1... | collective-permute-start | bytes 589832 | tf_op jit(solution)/shard_map/ppermute | solution.py:26
  141.8 23.9 %copy-start.2 = (bf16[8,12288]{1,0:T(8,128)(2,1)S(1)}, bf16[8,12288]{1,0:T(8,128)(2,1)}, u32[]{:S(2)}) copy-start(bf16[8,12288]{1,0:T(8,128)(2,1)} %tokens.1) | copy-start | bytes 589828
  141.8 10.9 %collective-permute-start.19 = (bf16[2,64,768]{2,1,0:T(8,128)(2,1)S(1)}, bf16[2,64,768]{2,1,0:T(8,128)(2,1)S(1)}, u32[]{:S(2)}, u32[]{:S(2)}) collective-permute-start(bf16[2,64,768]{2,1,0:T(8,128)(2,1)S(1)} %get-tuple-element.21), channel_id=1, source_target_pairs={{0,6},{1,7},{2,0},{3,1},{4,2},{5,3},{6,4},{7,5},{8,14},{9,15},{10,... | collective-permute-start | bytes 589832 | tf_op jit(solution)/shard_map/ppermute | solution.py:26
  144.9 9.6 %collective-permute-start.20 = (bf16[2,64,768]{2,1,0:T(8,128)(2,1)S(1)}, bf16[2,64,768]{2,1,0:T(8,128)(2,1)S(1)}, u32[]{:S(2)}, u32[]{:S(2)}) collective-permute-start(bf16[2,64,768]{2,1,0:T(8,128)(2,1)S(1)} %get-tuple-element.22), channel_id=1, source_target_pairs={{0,2},{1,3},{2,4},{3,5},{4,6},{5,7},{6,0},{7,1},{8,10},{9,11},{10,... | collective-permute-start | bytes 589832 | tf_op jit(solution)/shard_map/ppermute | solution.py:26
  155.4 10.3 %all-to-all-start.3 = ((bf16[8,16,768]{2,1,0:T(8,128)(2,1)}), bf16[8,16,768]{2,1,0:T(8,128)(2,1)S(1)}, u32[]{:S(2)}, u32[]{:S(2)}) async-start(bf16[8,16,768]{2,1,0:T(8,128)(2,1)} %copy_bitcast_fusion), calls=%async_computation.3 | async-start | bytes 393216 | tf_op jit(solution)/shard_map/all_to_all | solution.py:281

commit v6 on v5

--- a/solution.py
+++ b/solution.py
@@ -77,7 +77,7 @@
         + [pl.BlockSpec((1, 2 * unit, unit), lambda i: (i, 0, 0))]
         + [anywhere] * len(beside),
         out_specs=pl.BlockSpec((8, 2, 32, unit), lambda i: (0, 0, half, i)),
-        out_shape=pltpu.HBM((8, 2, 64, 2 * unit), bf16),
+        out_shape=jax.ShapeDtypeStruct((8, 2, 64, 2 * unit), bf16),
         input_output_aliases={len(rows) + 1: 0} if half else {},
         scratch_shapes=[pltpu.VMEM((8, 4, 16, 2 * unit), bf16)],
         compiler_params=pltpu.CompilerParams(vmem_limit_bytes=room),
@@ -263,10 +263,10 @@
     partial = first_product(far, (l2, r3, l3, r4, l4), first, partial, down_y)
     terms = lax.all_to_all(partial.reshape(16, 64, 2 * unit), ("yl", "x", "yh"), 0, 0)
 
-    down_y = after(in_hbm(partial), down_y)
+    hidden = activate(terms)
+
+    down_y = after(in_hbm(hidden), down_y)
     second = (down_weight, down_y, core_partner(down_weight), core_partner(down_y))
-
-    hidden = activate(terms)
     hidden = lax.all_to_all(hidden, ("yl", "x"), 0, 0)
 
     mine, left, right, p1, p7, left_half, right_half = second_product(yh, hidden, second)

time: 167 us -> 166 us (level)
  Pallas kernels: 19.5 us -> 17.7 us
    pallas_call x2, Pallas kernels: 7.73 us -> 5.99 us  [first_product(): pl.pallas_call(lambda *refs: first_kernel(rows, *refs), grid=(2,), in_spe...]
where the time goes in v6:
time: 166 us; the launch traced here: 165 us
  waiting for transfers between devices  63.7 us (38%)
  starting transfers between devices  42.1 us (25%)
  blocking collectives  38.7 us (23%)
  Pallas kernels  17.7 us (11%)
    all_to_all x1, blocking collectives, on_device(): lax.all_to_all(partial.reshape(16, 64, 2 * unit), ('yl', 'x', 'yh'), 0, 0)  38.7 us
    ppermute x16, waiting for transfers between devices, shift(): return lax.ppermute(block, 'z', [(i, (i + steps) % 8) for i in range(8)])  35.1 us
    ppermute x16, starting transfers between devices, shift(): return lax.ppermute(block, 'z', [(i, (i + steps) % 8) for i in range(8)])  24 us
    all_to_all x1, waiting for transfers between devices, on_device(): hidden = lax.all_to_all(hidden, ('yl', 'x'), 0, 0)  10.6 us
    all_to_all x1, starting transfers between devices, on_device(): lax.all_to_all(pieces.reshape(16, 8, 2 * unit), ('yl', 'x', 'yh'), 0, 0)  7.28 us
    all_to_all x1, waiting for transfers between devices, on_device(): lax.all_to_all(pieces.reshape(16, 8, 2 * unit), ('yl', 'x', 'yh'), 0, 0)  6.96 us
    all_to_all x1, waiting for transfers between devices, on_device(): branch = lax.all_to_all(branch.reshape(8, 16, unit), ('yl', 'x'), 0, 0)  6.87 us
    pallas_call x2, Pallas kernels, first_product(): pl.pallas_call(lambda *refs: first_kernel(rows, *refs), grid=(2,), in_spe...  5.99 us
  transfers between devices with their start and end apart: 24, of which 14 were waited for; matrix products, arithmetic and copies ran while one was open for 1% of the time, Pallas kernels for 4%

profile of v6, /device:TPU:48, one launch (start us, length us, event | category | flops | bytes accessed | tf_op | source)
XLA Modules:
  0.0 165.3 jit_solution(18194167064184072691)
XLA Ops:
  0.0 2.0 %shard_map.55 = bf16[8,16,1536]{2,1,0:T(8,128)(2,1)} custom-call(s32[1]{0:T(128)} %bitcast.1.core, bf16[8,12288]{1,0:T(8,128)(2,1)} %tokens.1, f32[1,12288]{1,0:T(1,128)} %bitcast.34), custom_call_target="tpu_custom_call" | custom-call | tf_op jit(solution)/shard_map/pallas_call | solution.py:236
  2.0 7.3 %all-to-all-start = ((bf16[16,8,1536]{2,1,0:T(8,128)(2,1)}), bf16[16,8,1536]{2,1,0:T(8,128)(2,1)S(1)}, u32[]{:S(2)}, u32[]{:S(2)}) async-start(bf16[16,8,1536]{2,1,0:T(8,128)(2,1)} %bitcast.31), calls=%async_computation | async-start | bytes 786432 | tf_op jit(solution)/shard_map/all_to_all | solution.py:249
  9.3 0.1 collective-permute-start.8
  9.4 0.5 collective-permute-start.9
  9.9 7.0 %all-to-all-done = bf16[16,8,1536]{2,1,0:T(8,128)(2,1)S(1)} async-done(((bf16[16,8,1536]{2,1,0:T(8,128)(2,1)}), bf16[16,8,1536]{2,1,0:T(8,128)(2,1)S(1)}, u32[]{:S(2)}, u32[]{:S(2)}) %all-to-all-start) | async-done | bytes 393248 | tf_op jit(solution)/shard_map/all_to_all | solution.py:249
  16.9 1.9 %collective-permute-start.2 = (bf16[128,1536]{1,0:T(8,128)(2,1)S(1)}, bf16[128,1536]{1,0:T(8,128)(2,1)S(1)}, u32[]{:S(2)}, u32[]{:S(2)}) collective-permute-start(bf16[128,1536]{1,0:T(8,128)(2,1)S(1)} %bitcast.27), channel_id=1, source_target_pairs={{0,1},{1,2},{2,3},{3,4},{4,5},{5,6},{6,7},{7,0},{8,9},{9,10},{10,1... | collective-permute-start | bytes 1179656 | tf_op jit(solution)/shard_map/ppermute | solution.py:26
  18.8 0.1 collective-permute-start
  18.9 1.3 copy.11.array
  20.2 2.6 %collective-permute-start.10 = (bf16[768,768]{1,0:T(8,128)(2,1)S(1)}, bf16[768,768]{1,0:T(8,128)(2,1)S(1)}, u32[]{:S(2)}, u32[]{:S(2)}) collective-permute-start(bf16[768,768]{1,0:T(8,128)(2,1)S(1)} %shard_map.58), channel_id=1, source_target_pairs={{0,8},{8,0},{1,9},{9,1},{2,10},{10,2},{3,11},{11,3},{4,12},{12,4},... | collective-permute-start | bytes 3538952 | tf_op jit(solution)/shard_map/ppermute | solution.py:34
  22.8 3.8 %collective-permute-done.2.refs_1_ = bf16[128,1536]{1,0:T(8,128)(2,1)S(1)} collective-permute-done((bf16[128,1536]{1,0:T(8,128)(2,1)S(1)}, bf16[128,1536]{1,0:T(8,128)(2,1)S(1)}, u32[]{:S(2)}, u32[]{:S(2)}) %collective-permute-start.2) | collective-permute-done | bytes 393248 | tf_op jit(solution)/shard_map/ppermute | solution.py:26
  26.6 1.9 %collective-permute-start.3 = (bf16[128,1536]{1,0:T(8,128)(2,1)S(1)}, bf16[128,1536]{1,0:T(8,128)(2,1)S(1)}, u32[]{:S(2)}, u32[]{:S(2)}) collective-permute-start(bf16[128,1536]{1,0:T(8,128)(2,1)S(1)} %collective-permute-done.2.refs_1_), channel_id=1, source_target_pairs={{0,1},{1,2},{2,3},{3,4},{4,5},{5,6},{6,7},{7,0},{8,9},{9,10},{10,1... | collective-permute-start | bytes 1179656 | tf_op jit(solution)/shard_map/ppermute | solution.py:26
  28.5 2.3 %collective-permute-start.1 = (bf16[128,1536]{1,0:T(8,128)(2,1)S(1)}, bf16[128,1536]{1,0:T(8,128)(2,1)S(1)}, u32[]{:S(2)}, u32[]{:S(2)}) collective-permute-start(bf16[128,1536]{1,0:T(8,128)(2,1)S(1)} %collective-permute-done.refs_2_), channel_id=1, source_target_pairs={{0,7},{1,0},{2,1},{3,2},{4,3},{5,4},{6,5},{7,6},{8,15},{9,8},{10,9... | collective-permute-start | bytes 1179656 | tf_op jit(solution)/shard_map/ppermute | solution.py:26
  30.8 7.3 %collective-permute-done.3.refs_3_ = bf16[128,1536]{1,0:T(8,128)(2,1)S(1)} collective-permute-done((bf16[128,1536]{1,0:T(8,128)(2,1)S(1)}, bf16[128,1536]{1,0:T(8,128)(2,1)S(1)}, u32[]{:S(2)}, u32[]{:S(2)}) %collective-permute-start.3) | collective-permute-done | bytes 393248 | tf_op jit(solution)/shard_map/ppermute | solution.py:26
  38.2 0.0 collective-permute-start.4
  38.2 0.4 collective-permute-done.1.refs_0_
  38.6 2.5 %collective-permute-start.5 = (bf16[128,1536]{1,0:T(8,128)(2,1)S(1)}, bf16[128,1536]{1,0:T(8,128)(2,1)S(1)}, u32[]{:S(2)}, u32[]{:S(2)}) collective-permute-start(bf16[128,1536]{1,0:T(8,128)(2,1)S(1)} %collective-permute-done.1.refs_0_), channel_id=1, source_target_pairs={{0,7},{1,0},{2,1},{3,2},{4,3},{5,4},{6,5},{7,6},{8,15},{9,8},{10,9... | collective-permute-start | bytes 1179656 | tf_op jit(solution)/shard_map/ppermute | solution.py:26
  41.2 3.2 %collective-permute-start.6 = (bf16[64,1536]{1,0:T(8,128)(2,1)S(1)}, bf16[64,1536]{1,0:T(8,128)(2,1)S(1)}, u32[]{:S(2)}, u32[]{:S(2)}) collective-permute-start(bf16[64,1536]{1,0:T(8,128)(2,1)S(1)} %slice.12), channel_id=1, source_target_pairs={{0,2},{1,3},{2,4},{3,5},{4,6},{5,7},{6,0},{7,1},{8,10},{9,11},{10,... | collective-permute-start | bytes 589832 | tf_op jit(solution)/shard_map/ppermute | solution.py:26
  44.4 1.0 collective-permute-start.7
  45.4 3.3 %shard_map.56.refs_4_.refs_5_ = bf16[2,1536,768]{2,1,0:T(8,128)(2,1)S(1)} custom-call(bf16[768,768]{1,0:T(8,128)(2,1)} %a.1, bf16[768,768]{1,0:T(8,128)(2,1)} %collective-permute-done.8.b, bf16[768,768]{1,0:T(8,128)(2,1)} %c.1, bf16[768,768]{1,0:T(8,128)(2,1)} %collective-permute-done.9.d), custom_call_target="tpu_custom_call" | custom-call | tf_op jit(solution)/shard_map/pallas_call | solution.py:95
  48.7 3.0 %shard_map.57.refs_6_ = bf16[8,2,64,1536]{3,2,1,0:T(8,128)(2,1)S(1)} custom-call(bf16[128,1536]{1,0:T(8,128)(2,1)S(1)} %bitcast.30, bf16[128,1536]{1,0:T(8,128)(2,1)S(1)} %collective-permute-done.2.refs_1_, bf16[128,1536]{1,0:T(8,128)(2,1)S(1)} %collective-permute-done.refs_2_, bf16[128,1536]{1,0:T(8,128)(2,1)S(1)} %collective-permute-done.3.refs_3_, ...), custom_call_target="tpu_custom_call" | custom-call | flops 2415919104 | bytes 4718592 | tf_op jit(solution)/shard_map/pallas_call | solution.py:73
  51.7 6.7 %collective-permute-done.6.refs_3_ = bf16[64,1536]{1,0:T(8,128)(2,1)S(1)} collective-permute-done((bf16[64,1536]{1,0:T(8,128)(2,1)S(1)}, bf16[64,1536]{1,0:T(8,128)(2,1)S(1)}, u32[]{:S(2)}, u32[]{:S(2)}) %collective-permute-start.6) | collective-permute-done | bytes 196640 | tf_op jit(solution)/shard_map/ppermute | solution.py:26
  58.4 0.0 collective-permute-done.7.refs_4_
  58.4 3.0 %shard_map.59 = bf16[8,2,64,1536]{3,2,1,0:T(8,128)(2,1)S(1)} custom-call(bf16[128,1536]{1,0:T(8,128)(2,1)S(1)} %collective-permute-done.1.refs_0_, bf16[128,1536]{1,0:T(8,128)(2,1)S(1)} %collective-permute-done.4.refs_1_, bf16[128,1536]{1,0:T(8,128)(2,1)S(1)} %collective-permute-done.5.refs_2_, ...), custom_call_target="tpu_custom_call", output_to_operand_aliasing={{}: (6, {})} | custom-call | flops 2415919104 | bytes 4718592 | tf_op jit(solution)/shard_map/pallas_call | solution.py:73
  61.4 38.7 %all_to_all.20.terms = bf16[16,64,1536]{2,1,0:T(8,128)(2,1)S(1)} all-to-all(bf16[16,64,1536]{2,1,0:T(8,128)(2,1)S(1)} %bitcast.26), channel_id=1, replica_groups=mesh['yl'=2,'x'=4,'c'=2,'yh'=2,'z'=8] {'yl','x','yh'}, dimensions={0} | all-to-all | bytes 6291456 | tf_op jit(solution)/shard_map/all_to_all | solution.py:264
  100.1 1.5 shard_map.60.dependency
  101.7 3.6 %all-to-all-start.2 = ((bf16[8,2,64,768]{3,2,1,0:T(8,128)(2,1)}), bf16[8,2,64,768]{3,2,1,0:T(8,128)(2,1)S(1)}, u32[]{:S(2)}, u32[]{:S(2)}) async-start(bf16[8,2,64,768]{3,2,1,0:T(8,128)(2,1)} %shard_map.60.dependency), calls=%async_computation.2 | async-start | bytes 3145728 | tf_op jit(solution)/shard_map/all_to_all | solution.py:270
  105.3 0.1 collective-permute-start.11
  105.4 0.5 collective-permute-start.12
  105.9 2.7 %collective-permute-done.11.refs_2_ = bf16[768,768]{1,0:T(8,128)(2,1)} collective-permute-done((bf16[768,768]{1,0:T(8,128)(2,1)}, bf16[768,768]{1,0:T(8,128)(2,1)}, u32[]{:S(2)}, u32[]{:S(2)}) %collective-permute-start.11) | collective-permute-done | bytes 1179680 | tf_op jit(solution)/shard_map/ppermute | solution.py:30
  108.6 1.5 collective-permute-done.12.refs_3_
  110.0 10.6 %all-to-all-done.2.mine.theirs = bf16[8,2,64,768]{3,2,1,0:T(8,128)(2,1)S(1)} async-done(((bf16[8,2,64,768]{3,2,1,0:T(8,128)(2,1)}), bf16[8,2,64,768]{3,2,1,0:T(8,128)(2,1)S(1)}, u32[]{:S(2)}, u32[]{:S(2)}) %all-to-all-start.2) | async-done | bytes 1572896 | tf_op jit(solution)/shard_map/all_to_all | solution.py:270
  120.7 4.8 %shard_map.62 = (bf16[3,2,64,768]{3,2,1,0:T(8,128)(2,1)S(1)}, bf16[1,2,64,768]{3,2,1,0:T(8,128)(2,1)S(1)}, bf16[1,2,64,768]{3,2,1,0:T(8,128)(2,1)S(1)}, bf16[1,2...) custom-call(s32[1]{0:T(128)} %bitcast._, ...), custom_call_target="tpu_custom_call" | custom-call | flops 2415919104 | bytes 4718592 | tf_op jit(solution)/shard_map/pallas_call | solution.py:178
  125.5 0.1 collective-permute-start.15
  125.6 4.4 %collective-permute-start.16 = (bf16[1,2,64,768]{3,2,1,0:T(8,128)(2,1)S(1)}, bf16[1,2,64,768]{3,2,1,0:T(8,128)(2,1)S(1)}, u32[]{:S(2)}, u32[]{:S(2)}) collective-permute-start(bf16[1,2,64,768]{3,2,1,0:T(8,128)(2,1)S(1)} %get-tuple-element.18), channel_id=1, source_target_pairs={{0,1},{1,2},{2,3},{3,4},{4,5},{5,6},{6,7},{7,0},{8,9},{9,10},{10,1... | collective-permute-start | bytes 589832 | tf_op jit(solution)/shard_map/ppermute | solution.py:26
  129.9 2.9 %collective-permute-start.18 = (bf16[64,768]{1,0:T(8,128)(2,1)S(1)}, bf16[64,768]{1,0:T(8,128)(2,1)S(1)}, u32[]{:S(2)}, u32[]{:S(2)}) collective-permute-start(bf16[64,768]{1,0:T(8,128)(2,1)S(1)} %get-tuple-element.20), channel_id=1, source_target_pairs={{0,2},{1,3},{2,4},{3,5},{4,6},{5,7},{6,0},{7,1},{8,10},{9,11},{10,... | collective-permute-start | bytes 294920 | tf_op jit(solution)/shard_map/ppermute | solution.py:26
  132.9 0.5 collective-permute-start.13
  133.3 7.2 %collective-permute-done.17.left_half = bf16[64,768]{1,0:T(8,128)(2,1)S(1)} collective-permute-done((bf16[64,768]{1,0:T(8,128)(2,1)S(1)}, bf16[64,768]{1,0:T(8,128)(2,1)S(1)}, u32[]{:S(2)}, u32[]{:S(2)}) %collective-permute-start.17) | collective-permute-done | bytes 98336 | tf_op jit(solution)/shard_map/ppermute | solution.py:26
  140.5 0.1 shard_map.63
  140.6 0.0 copy-start.2
  140.7 3.2 %collective-permute-start.19 = (bf16[2,64,768]{2,1,0:T(8,128)(2,1)S(1)}, bf16[2,64,768]{2,1,0:T(8,128)(2,1)S(1)}, u32[]{:S(2)}, u32[]{:S(2)}) collective-permute-start(bf16[2,64,768]{2,1,0:T(8,128)(2,1)S(1)} %get-tuple-element.21), channel_id=1, source_target_pairs={{0,6},{1,7},{2,0},{3,1},{4,2},{5,3},{6,4},{7,5},{8,14},{9,15},{10,... | collective-permute-start | bytes 589832 | tf_op jit(solution)/shard_map/ppermute | solution.py:26
  143.8 1.6 collective-permute-done.13
  145.5 1.8 %collective-permute-done.14 = bf16[1,2,64,768]{3,2,1,0:T(8,128)(2,1)S(1)} collective-permute-done((bf16[1,2,64,768]{3,2,1,0:T(8,128)(2,1)S(1)}, bf16[1,2,64,768]{3,2,1,0:T(8,128)(2,1)S(1)}, u32[]{:S(2)}, u32[]{:S(2)}) %collective-permute-start.14) | collective-permute-done | bytes 196640 | tf_op jit(solution)/shard_map/ppermute | solution.py:26
  147.2 4.3 %collective-permute-done.19 = bf16[2,64,768]{2,1,0:T(8,128)(2,1)S(1)} collective-permute-done((bf16[2,64,768]{2,1,0:T(8,128)(2,1)S(1)}, bf16[2,64,768]{2,1,0:T(8,128)(2,1)S(1)}, u32[]{:S(2)}, u32[]{:S(2)}) %collective-permute-start.19) | collective-permute-done | bytes 196640 | tf_op jit(solution)/shard_map/ppermute | solution.py:26
  151.6 1.9 %collective-permute-done.20 = bf16[2,64,768]{2,1,0:T(8,128)(2,1)S(1)} collective-permute-done((bf16[2,64,768]{2,1,0:T(8,128)(2,1)S(1)}, bf16[2,64,768]{2,1,0:T(8,128)(2,1)S(1)}, u32[]{:S(2)}, u32[]{:S(2)}) %collective-permute-start.20) | collective-permute-done | bytes 196640 | tf_op jit(solution)/shard_map/ppermute | solution.py:26
  153.5 0.8 copy_bitcast_fusion
  154.3 3.4 %all-to-all-start.3 = ((bf16[8,16,768]{2,1,0:T(8,128)(2,1)}), bf16[8,16,768]{2,1,0:T(8,128)(2,1)S(1)}, u32[]{:S(2)}, u32[]{:S(2)}) async-start(bf16[8,16,768]{2,1,0:T(8,128)(2,1)} %copy_bitcast_fusion), calls=%async_computation.3 | async-start | bytes 393216 | tf_op jit(solution)/shard_map/all_to_all | solution.py:281
  157.7 6.9 %all-to-all-done.3 = bf16[8,16,768]{2,1,0:T(8,128)(2,1)S(1)} async-done(((bf16[8,16,768]{2,1,0:T(8,128)(2,1)}), bf16[8,16,768]{2,1,0:T(8,128)(2,1)S(1)}, u32[]{:S(2)}, u32[]{:S(2)}) %all-to-all-start.3) | async-done | bytes 196640 | tf_op jit(solution)/shard_map/all_to_all | solution.py:281
  164.6 0.7 add_convert_fusion
  (22 shorter events, 0.1 us)
Async XLA Ops:
  0.0 9.3 %copy-start.1 = (bf16[768,768]{1,0:T(8,128)(2,1)S(1)}, bf16[768,768]{1,0:T(8,128)(2,1)}, u32[]{:S(2)}) copy-start(bf16[768,768]{1,0:T(8,128)(2,1)} %a.1) | copy-start | bytes 3538948
  2.0 14.8 %all-to-all-start = ((bf16[16,8,1536]{2,1,0:T(8,128)(2,1)}), bf16[16,8,1536]{2,1,0:T(8,128)(2,1)S(1)}, u32[]{:S(2)}, u32[]{:S(2)}) async-start(bf16[16,8,1536]{2,1,0:T(8,128)(2,1)} %bitcast.31), calls=%async_computation | async-start | bytes 786432 | tf_op jit(solution)/shard_map/all_to_all | solution.py:249
  9.3 31.9 %collective-permute-start.8 = (bf16[768,768]{1,0:T(8,128)(2,1)S(1)}, bf16[768,768]{1,0:T(8,128)(2,1)}, u32[]{:S(2)}, u32[]{:S(2)}) collective-permute-start(bf16[768,768]{1,0:T(8,128)(2,1)S(1)} %copy-done.1), channel_id=1, source_target_pairs={{0,16},{16,0},{1,17},{17,1},{2,18},{18,2},{3,19},{19,3},{4,20},{20... | collective-permute-start | bytes 3538952 | tf_op jit(solution)/shard_map/ppermute | solution.py:30
  9.4 35.0 %collective-permute-start.9 = (bf16[768,768]{1,0:T(8,128)(2,1)}, bf16[768,768]{1,0:T(8,128)(2,1)}, u32[]{:S(2)}, u32[]{:S(2)}) collective-permute-start(bf16[768,768]{1,0:T(8,128)(2,1)} %c.1), channel_id=1, source_target_pairs={{0,16},{16,0},{1,17},{17,1},{2,18},{18,2},{3,19},{19,3},{4,20},{20... | collective-permute-start | bytes 3538952 | tf_op jit(solution)/shard_map/ppermute | solution.py:30
  16.9 9.7 %collective-permute-start.2 = (bf16[128,1536]{1,0:T(8,128)(2,1)S(1)}, bf16[128,1536]{1,0:T(8,128)(2,1)S(1)}, u32[]{:S(2)}, u32[]{:S(2)}) collective-permute-start(bf16[128,1536]{1,0:T(8,128)(2,1)S(1)} %bitcast.27), channel_id=1, source_target_pairs={{0,1},{1,2},{2,3},{3,4},{4,5},{5,6},{6,7},{7,0},{8,9},{9,10},{10,1... | collective-permute-start | bytes 1179656 | tf_op jit(solution)/shard_map/ppermute | solution.py:26
  18.8 9.7 %collective-permute-start = (bf16[128,1536]{1,0:T(8,128)(2,1)S(1)}, bf16[128,1536]{1,0:T(8,128)(2,1)S(1)}, u32[]{:S(2)}, u32[]{:S(2)}) collective-permute-start(bf16[128,1536]{1,0:T(8,128)(2,1)S(1)} %bitcast.28), channel_id=1, source_target_pairs={{0,7},{1,0},{2,1},{3,2},{4,3},{5,4},{6,5},{7,6},{8,15},{9,8},{10,9... | collective-permute-start | bytes 1179656 | tf_op jit(solution)/shard_map/ppermute | solution.py:26
  20.2 38.2 %collective-permute-start.10 = (bf16[768,768]{1,0:T(8,128)(2,1)S(1)}, bf16[768,768]{1,0:T(8,128)(2,1)S(1)}, u32[]{:S(2)}, u32[]{:S(2)}) collective-permute-start(bf16[768,768]{1,0:T(8,128)(2,1)S(1)} %shard_map.58), channel_id=1, source_target_pairs={{0,8},{8,0},{1,9},{9,1},{2,10},{10,2},{3,11},{11,3},{4,12},{12,4},... | collective-permute-start | bytes 3538952 | tf_op jit(solution)/shard_map/ppermute | solution.py:34
  26.6 11.6 %collective-permute-start.3 = (bf16[128,1536]{1,0:T(8,128)(2,1)S(1)}, bf16[128,1536]{1,0:T(8,128)(2,1)S(1)}, u32[]{:S(2)}, u32[]{:S(2)}) collective-permute-start(bf16[128,1536]{1,0:T(8,128)(2,1)S(1)} %collective-permute-done.2.refs_1_), channel_id=1, source_target_pairs={{0,1},{1,2},{2,3},{3,4},{4,5},{5,6},{6,7},{7,0},{8,9},{9,10},{10,1... | collective-permute-start | bytes 1179656 | tf_op jit(solution)/shard_map/ppermute | solution.py:26
  28.5 10.1 %collective-permute-start.1 = (bf16[128,1536]{1,0:T(8,128)(2,1)S(1)}, bf16[128,1536]{1,0:T(8,128)(2,1)S(1)}, u32[]{:S(2)}, u32[]{:S(2)}) collective-permute-start(bf16[128,1536]{1,0:T(8,128)(2,1)S(1)} %collective-permute-done.refs_2_), channel_id=1, source_target_pairs={{0,7},{1,0},{2,1},{3,2},{4,3},{5,4},{6,5},{7,6},{8,15},{9,8},{10,9... | collective-permute-start | bytes 1179656 | tf_op jit(solution)/shard_map/ppermute | solution.py:26
  38.2 20.2 %collective-permute-start.4 = (bf16[128,1536]{1,0:T(8,128)(2,1)S(1)}, bf16[128,1536]{1,0:T(8,128)(2,1)S(1)}, u32[]{:S(2)}, u32[]{:S(2)}) collective-permute-start(bf16[128,1536]{1,0:T(8,128)(2,1)S(1)} %collective-permute-done.3.refs_3_), channel_id=1, source_target_pairs={{0,1},{1,2},{2,3},{3,4},{4,5},{5,6},{6,7},{7,0},{8,9},{9,10},{10,1... | collective-permute-start | bytes 1179656 | tf_op jit(solution)/shard_map/ppermute | solution.py:26
  38.6 19.8 %collective-permute-start.5 = (bf16[128,1536]{1,0:T(8,128)(2,1)S(1)}, bf16[128,1536]{1,0:T(8,128)(2,1)S(1)}, u32[]{:S(2)}, u32[]{:S(2)}) collective-permute-start(bf16[128,1536]{1,0:T(8,128)(2,1)S(1)} %collective-permute-done.1.refs_0_), channel_id=1, source_target_pairs={{0,7},{1,0},{2,1},{3,2},{4,3},{5,4},{6,5},{7,6},{8,15},{9,8},{10,9... | collective-permute-start | bytes 1179656 | tf_op jit(solution)/shard_map/ppermute | solution.py:26
  41.2 17.2 %collective-permute-start.6 = (bf16[64,1536]{1,0:T(8,128)(2,1)S(1)}, bf16[64,1536]{1,0:T(8,128)(2,1)S(1)}, u32[]{:S(2)}, u32[]{:S(2)}) collective-permute-start(bf16[64,1536]{1,0:T(8,128)(2,1)S(1)} %slice.12), channel_id=1, source_target_pairs={{0,2},{1,3},{2,4},{3,5},{4,6},{5,7},{6,0},{7,1},{8,10},{9,11},{10,... | collective-permute-start | bytes 589832 | tf_op jit(solution)/shard_map/ppermute | solution.py:26
  44.4 14.0 %collective-permute-start.7 = (bf16[64,1536]{1,0:T(8,128)(2,1)S(1)}, bf16[64,1536]{1,0:T(8,128)(2,1)S(1)}, u32[]{:S(2)}, u32[]{:S(2)}) collective-permute-start(bf16[64,1536]{1,0:T(8,128)(2,1)S(1)} %slice.13), channel_id=1, source_target_pairs={{0,6},{1,7},{2,0},{3,1},{4,2},{5,3},{6,4},{7,5},{8,14},{9,15},{10,... | collective-permute-start | bytes 589832 | tf_op jit(solution)/shard_map/ppermute | solution.py:26
  101.7 19.0 %all-to-all-start.2 = ((bf16[8,2,64,768]{3,2,1,0:T(8,128)(2,1)}), bf16[8,2,64,768]{3,2,1,0:T(8,128)(2,1)S(1)}, u32[]{:S(2)}, u32[]{:S(2)}) async-start(bf16[8,2,64,768]{3,2,1,0:T(8,128)(2,1)} %shard_map.60.dependency), calls=%async_computation.2 | async-start | bytes 3145728 | tf_op jit(solution)/shard_map/all_to_all | solution.py:270
  105.3 3.2 %collective-permute-start.11 = (bf16[768,768]{1,0:T(8,128)(2,1)}, bf16[768,768]{1,0:T(8,128)(2,1)}, u32[]{:S(2)}, u32[]{:S(2)}) collective-permute-start(bf16[768,768]{1,0:T(8,128)(2,1)} %refs_0_.1), channel_id=1, source_target_pairs={{0,16},{16,0},{1,17},{17,1},{2,18},{18,2},{3,19},{19,3},{4,20},{20... | collective-permute-start | bytes 3538952 | tf_op jit(solution)/shard_map/ppermute | solution.py:30
  105.4 15.3 %copy-start = (bf16[768,768]{1,0:T(8,128)(2,1)}, bf16[768,768]{1,0:T(8,128)(2,1)S(1)}, u32[]{:S(2)}) copy-start(bf16[768,768]{1,0:T(8,128)(2,1)S(1)} %shard_map.61.refs_1_) | copy-start | bytes 3538948
  105.4 4.6 %collective-permute-start.12 = (bf16[768,768]{1,0:T(8,128)(2,1)S(1)}, bf16[768,768]{1,0:T(8,128)(2,1)}, u32[]{:S(2)}, u32[]{:S(2)}) collective-permute-start(bf16[768,768]{1,0:T(8,128)(2,1)S(1)} %shard_map.61.refs_1_), channel_id=1, source_target_pairs={{0,16},{16,0},{1,17},{17,1},{2,18},{18,2},{3,19},{19,3},{4,20},{20... | collective-permute-start | bytes 3538952 | tf_op jit(solution)/shard_map/ppermute | solution.py:30
  125.5 15.0 %collective-permute-start.15 = (bf16[1,2,64,768]{3,2,1,0:T(8,128)(2,1)S(1)}, bf16[1,2,64,768]{3,2,1,0:T(8,128)(2,1)S(1)}, u32[]{:S(2)}, u32[]{:S(2)}) collective-permute-start(bf16[1,2,64,768]{3,2,1,0:T(8,128)(2,1)S(1)} %get-tuple-element.17), channel_id=1, source_target_pairs={{0,7},{1,0},{2,1},{3,2},{4,3},{5,4},{6,5},{7,6},{8,15},{9,8},{10,9... | collective-permute-start | bytes 589832 | tf_op jit(solution)/shard_map/ppermute | solution.py:26
  125.6 15.0 %collective-permute-start.16 = (bf16[1,2,64,768]{3,2,1,0:T(8,128)(2,1)S(1)}, bf16[1,2,64,768]{3,2,1,0:T(8,128)(2,1)S(1)}, u32[]{:S(2)}, u32[]{:S(2)}) collective-permute-start(bf16[1,2,64,768]{3,2,1,0:T(8,128)(2,1)S(1)} %get-tuple-element.18), channel_id=1, source_target_pairs={{0,1},{1,2},{2,3},{3,4},{4,5},{5,6},{6,7},{7,0},{8,9},{9,10},{10,1... | collective-permute-start | bytes 589832 | tf_op jit(solution)/shard_map/ppermute | solution.py:26
  129.9 10.6 %collective-permute-start.17 = (bf16[64,768]{1,0:T(8,128)(2,1)S(1)}, bf16[64,768]{1,0:T(8,128)(2,1)S(1)}, u32[]{:S(2)}, u32[]{:S(2)}) collective-permute-start(bf16[64,768]{1,0:T(8,128)(2,1)S(1)} %get-tuple-element.19), channel_id=1, source_target_pairs={{0,6},{1,7},{2,0},{3,1},{4,2},{5,3},{6,4},{7,5},{8,14},{9,15},{10,... | collective-permute-start | bytes 294920 | tf_op jit(solution)/shard_map/ppermute | solution.py:26
  129.9 10.6 %collective-permute-start.18 = (bf16[64,768]{1,0:T(8,128)(2,1)S(1)}, bf16[64,768]{1,0:T(8,128)(2,1)S(1)}, u32[]{:S(2)}, u32[]{:S(2)}) collective-permute-start(bf16[64,768]{1,0:T(8,128)(2,1)S(1)} %get-tuple-element.20), channel_id=1, source_target_pairs={{0,2},{1,3},{2,4},{3,5},{4,6},{5,7},{6,0},{7,1},{8,10},{9,11},{10,... | collective-permute-start | bytes 294920 | tf_op jit(solution)/shard_map/ppermute | solution.py:26
  132.9 12.6 %collective-permute-start.13 = (bf16[1,2,64,768]{3,2,1,0:T(8,128)(2,1)S(1)}, bf16[1,2,64,768]{3,2,1,0:T(8,128)(2,1)S(1)}, u32[]{:S(2)}, u32[]{:S(2)}) collective-permute-start(bf16[1,2,64,768]{3,2,1,0:T(8,128)(2,1)S(1)} %get-tuple-element.15), channel_id=1, source_target_pairs={{0,7},{1,0},{2,1},{3,2},{4,3},{5,4},{6,5},{7,6},{8,15},{9,8},{10,9... | collective-permute-start | bytes 589832 | tf_op jit(solution)/shard_map/ppermute | solution.py:26
  140.5 6.8 %collective-permute-start.14 = (bf16[1,2,64,768]{3,2,1,0:T(8,128)(2,1)S(1)}, bf16[1,2,64,768]{3,2,1,0:T(8,128)(2,1)S(1)}, u32[]{:S(2)}, u32[]{:S(2)}) collective-permute-start(bf16[1,2,64,768]{3,2,1,0:T(8,128)(2,1)S(1)} %get-tuple-element.16), channel_id=1, source_target_pairs={{0,1},{1,2},{2,3},{3,4},{4,5},{5,6},{6,7},{7,0},{8,9},{9,10},{10,1... | collective-permute-start | bytes 589832 | tf_op jit(solution)/shard_map/ppermute | solution.py:26
  140.6 23.9 %copy-start.2 = (bf16[8,12288]{1,0:T(8,128)(2,1)S(1)}, bf16[8,12288]{1,0:T(8,128)(2,1)}, u32[]{:S(2)}) copy-start(bf16[8,12288]{1,0:T(8,128)(2,1)} %tokens.1) | copy-start | bytes 589828
  140.7 10.9 %collective-permute-start.19 = (bf16[2,64,768]{2,1,0:T(8,128)(2,1)S(1)}, bf16[2,64,768]{2,1,0:T(8,128)(2,1)S(1)}, u32[]{:S(2)}, u32[]{:S(2)}) collective-permute-start(bf16[2,64,768]{2,1,0:T(8,128)(2,1)S(1)} %get-tuple-element.21), channel_id=1, source_target_pairs={{0,6},{1,7},{2,0},{3,1},{4,2},{5,3},{6,4},{7,5},{8,14},{9,15},{10,... | collective-permute-start | bytes 589832 | tf_op jit(solution)/shard_map/ppermute | solution.py:26
  143.8 9.6 %collective-permute-start.20 = (bf16[2,64,768]{2,1,0:T(8,128)(2,1)S(1)}, bf16[2,64,768]{2,1,0:T(8,128)(2,1)S(1)}, u32[]{:S(2)}, u32[]{:S(2)}) collective-permute-start(bf16[2,64,768]{2,1,0:T(8,128)(2,1)S(1)} %get-tuple-element.22), channel_id=1, source_target_pairs={{0,2},{1,3},{2,4},{3,5},{4,6},{5,7},{6,0},{7,1},{8,10},{9,11},{10,... | collective-permute-start | bytes 589832 | tf_op jit(solution)/shard_map/ppermute | solution.py:26
  154.3 10.3 %all-to-all-start.3 = ((bf16[8,16,768]{2,1,0:T(8,128)(2,1)}), bf16[8,16,768]{2,1,0:T(8,128)(2,1)S(1)}, u32[]{:S(2)}, u32[]{:S(2)}) async-start(bf16[8,16,768]{2,1,0:T(8,128)(2,1)} %copy_bitcast_fusion), calls=%async_computation.3 | async-start | bytes 393216 | tf_op jit(solution)/shard_map/all_to_all | solution.py:281
